TPU v7x, 32 devices: a whole 2x2x4 slice. The times are simulated.
32 devices in a mesh: grp: 2 (over x), seq: 8 (over z, y), head: 2 (over core).
Axes of the slice: x: 2, y: 2, z: 4, core: 2. Of those that a mesh axis runs over, the one named last changes fastest.
Arguments:
- q_nope: bfloat16 [8, 128, 128], P('grp', ('seq', 'head')), parts along dimension 0, may hold values from -6 to 6
- q_rope: bfloat16 [8, 128, 64], P('grp', ('seq', 'head')), parts along dimension 0, may hold values from -150 to 150
- w_uk: bfloat16 [128, 128, 512], P(('seq', 'head')), may hold values from -0.5 to 0.5
- w_uv: bfloat16 [128, 512, 128], P(('seq', 'head')), may hold values from -1 to 1
- cache: bfloat16 [8, 4096, 576], P('grp', 'seq'), parts along dimension 0, may hold values from -12 to 12
- lengths: int32 [8], P('grp'), parts along dimension 0, may hold values from 2048 to 4096, as said below
- selected: int32 [8, 8, 32], P('grp'), parts along dimension 0, may hold values from 0 to 63, as said below
Outputs:
- attended: bfloat16 [8, 128, 128], P('grp', ('seq', 'head')), parts along dimension 0
- bounds: float32 [8, 8, 64], P('grp', None, 'seq'), parts along dimension 0
There are 2 independent parts, one for each index of `grp`. A program takes and returns all parts, laid end to end along the dimension named above; an argument that names none is the same for every part. Nothing has to cross between parts.
Inputs may be any that keep to these rules, and one draw needn't show every extreme that they name: `lengths`: some request has exactly 4096 cached tokens; every request has 2048 or more. `selected`: for each request and head group the 32 page numbers are distinct and below ceil(lengths[r] / 64); page 0 and the page of the request's last cached token are always among them.
All inputs are finite; a program needn't handle non-finite values.
Results may differ from a plain program's by a relative error of at most 0.0065.
Values may be sent and summed in bfloat16 or wider, within the bound.
No kernel may reach another device: no remote copies, remote signals or barrier semaphores. Data moves between devices by JAX's collectives and lax.ppermute only.
A program may use at most 64 MiB of HBM per device.

v0:
```python
import jax
import jax.numpy as jnp
from jax import lax
from jax.sharding import PartitionSpec as P

GH = 16
PAGE = 64


def local(q_nope, q_rope, w_uk, w_uv, cache, lengths, selected):
    seq_count = lax.axis_size("seq")
    head_count = lax.axis_size("head")
    seq_rank = lax.axis_index("seq")
    head_rank = lax.axis_index("head")
    requests = q_nope.shape[0]
    head_block = q_nope.shape[1]
    latent_width = w_uk.shape[2]
    cache_width = cache.shape[2]
    tokens_here = cache.shape[1]
    pages_here = tokens_here // PAGE
    groups = selected.shape[1]
    softmax_scale = (q_nope.shape[2] + q_rope.shape[2]) ** (-0.5)
    query_latent = jnp.einsum(
        "rhn,hnl->rhl", q_nope, w_uk, preferred_element_type=jnp.float32
    ).astype(jnp.bfloat16)
    absorbed = jnp.concatenate([query_latent, q_rope], axis=2)
    queries = lax.all_gather(absorbed, "seq", axis=1, tiled=True)
    heads_here = head_block * seq_count
    position = jnp.arange(heads_here, dtype=jnp.int32)
    global_head = (
        position // head_block * head_count + head_rank
    ) * head_block + position % head_block
    group_of = global_head // GH
    group_hot = group_of[:, None] == jnp.arange(groups, dtype=jnp.int32)[None, :]
    page_number = seq_rank * pages_here + jnp.arange(pages_here, dtype=jnp.int32)
    token_index = seq_rank * tokens_here + jnp.arange(tokens_here, dtype=jnp.int32).reshape(
        pages_here, PAGE
    )
    live_token = token_index[None] < lengths[:, None, None]
    live_page = live_token[:, :, 0]
    page_blocks = cache.reshape(requests, pages_here, PAGE, cache_width)
    page_low = jnp.min(jnp.where(live_token[..., None], page_blocks, jnp.inf), axis=2).astype(
        jnp.float32
    )
    page_high = jnp.max(jnp.where(live_token[..., None], page_blocks, -jnp.inf), axis=2).astype(
        jnp.float32
    )
    page_low = jnp.where(live_page[..., None], page_low, 0.0)
    page_high = jnp.where(live_page[..., None], page_high, 0.0)
    middle = (page_low + page_high) * 0.5
    spread = (page_high - page_low) * 0.5
    query_float = queries.astype(jnp.float32)
    head_bound = softmax_scale * (
        jnp.einsum("rhd,rpd->rhp", query_float, middle, precision=lax.Precision.HIGHEST)
        + jnp.einsum("rhd,rpd->rhp", jnp.abs(query_float), spread, precision=lax.Precision.HIGHEST)
    )
    group_bound = jnp.max(
        jnp.where(group_hot.T[None, :, :, None], head_bound[:, None, :, :], -1e30), axis=2
    )
    group_bound = lax.pmax(group_bound, "head")
    bounds = jnp.where(live_page[:, None, :], group_bound, 0.0)
    picked = jnp.any(selected[:, :, :, None] == page_number[None, None, None, :], axis=2)
    head_pick = jnp.any(group_hot[None, :, :, None] & picked[:, None, :, :], axis=2)
    scores = (
        jnp.einsum("rhd,rtd->rht", queries, cache, preferred_element_type=jnp.float32)
        * softmax_scale
    )
    scores = scores.reshape(requests, heads_here, pages_here, PAGE)
    scores = jnp.where(live_token[:, None], scores, -1e30)
    page_top = jnp.max(scores, axis=3)
    weights = jnp.where(live_token[:, None], jnp.exp(scores - page_top[..., None]), 0.0).astype(
        jnp.bfloat16
    )
    page_total = jnp.sum(weights.astype(jnp.float32), axis=3)
    page_weighted = jnp.einsum(
        "rhpt,rptl->rhpl",
        weights,
        page_blocks[..., :latent_width],
        preferred_element_type=jnp.float32,
    )
    summit = jnp.max(jnp.where(head_pick, page_top, -1e30), axis=2)
    factor = jnp.where(head_pick, jnp.exp(page_top - summit[..., None]), 0.0)
    total = jnp.sum(factor * page_total, axis=2)
    weighted = jnp.einsum("rhp,rhpl->rhl", factor, page_weighted, precision=lax.Precision.HIGHEST)
    gotten = (
        lax.all_to_all(
            summit.reshape(requests, seq_count, head_block),
            "seq",
            split_axis=1,
            concat_axis=1,
            tiled=True,
        ),
        lax.all_to_all(
            total.reshape(requests, seq_count, head_block),
            "seq",
            split_axis=1,
            concat_axis=1,
            tiled=True,
        ),
        lax.all_to_all(
            weighted.reshape(requests, seq_count, head_block, latent_width),
            "seq",
            split_axis=1,
            concat_axis=1,
            tiled=True,
        ),
    )
    highest = jnp.max(gotten[0], axis=1)
    rescale = jnp.exp(gotten[0] - highest[:, None, :])
    own_total = jnp.sum(rescale * gotten[1], axis=1)
    own_weighted = jnp.sum(rescale[..., None] * gotten[2], axis=1)
    latent_out = (own_weighted / own_total[..., None]).astype(jnp.bfloat16)
    attended = jnp.einsum(
        "rhl,hlv->rhv", latent_out, w_uv, preferred_element_type=jnp.float32
    ).astype(jnp.bfloat16)
    return (attended, bounds)


def solution(mesh):
    placed = (
        P("grp", ("seq", "head"), None),
        P("grp", ("seq", "head"), None),
        P(("seq", "head"), None, None),
        P(("seq", "head"), None, None),
        P("grp", "seq", None),
        P("grp"),
        P("grp", None, None),
    )
    return jax.shard_map(
        local,
        mesh=mesh,
        in_specs=placed,
        out_specs=(P("grp", ("seq", "head"), None), P("grp", None, "seq")),
        check_vma=False,
    )
```

profile of v0, /device:TPU:0, one launch (start us, length us, event | category | flops | bytes accessed | tf_op | source)
XLA Modules:
  0.0 88.0 jit_solution(16813406923026156517)
XLA Ops:
  0.6 0.0 copy-start
  0.7 0.8 copy.102
  1.5 0.4 copy-done
  1.9 0.9 %fusion.3 = bf16[4,8,512]{2,0,1:T(4,128)(2,1)S(1)} fusion(bf16[8,128,512]{2,1,0:T(8,128)(2,1)S(1)} %copy-done, bf16[4,8,128]{2,1,0:T(8,128)(2,1)} %param.7), kind=kOutput, calls=%fused_computation.8 | convolution fusion | flops 4210688 | bytes 1089536 | tf_op jit(solution)/shard_map/rhn,hnl->rhl/dot_general | solution.py:23
  2.8 0.0 copy-start.3
  2.8 0.0 copy-start.4
  2.9 32.6 %all_gather.3 = bf16[4,64,576]{2,0,1:T(4,128)(2,1)S(1)} all-gather(bf16[4,8,576]{2,0,1:T(4,128)(2,1)S(1)} %pad_maximum_fusion), channel_id=1, replica_groups=mesh['grp'=2,'seq'=8,'head'=2] {'seq'}, dimensions={1}, use_global_device_ids=true | all-gather | bytes 331776 | tf_op jit(solution)/shard_map/all_gather | solution.py:27
  35.5 2.2 %convolution_multiply_fusion = f32[4,64,512]{2,1,0:T(8,128)S(1)} fusion(bf16[4,512,576]{1,2,0:T(8,128)(2,1)} %param.11, bf16[4,64,576]{2,0,1:T(4,128)(2,1)S(1)} %all_gather.3), kind=kOutput, calls=%fused_computation.6 | convolution fusion | flops 151126016 | bytes 3178496 | tf_op jit(solution)/shard_map/rhd,rtd->rht/dot_general | solution.py:65
  37.7 0.2 reshape.136
  37.9 0.0 copy-done.3
  37.9 0.7 compare_reduce_fusion
  38.6 0.1 and_reduce_fusion
  38.7 0.0 copy-done.4
  38.7 0.1 broadcast_compare_fusion
  38.8 0.4 fusion.6
  39.2 0.1 reshape.137
  39.3 0.6 copy.105
  39.9 5.6 %all-to-all-start = ((f32[4,8,8]{2,0,1:T(4,128)}), f32[4,8,8]{2,0,1:T(4,128)S(1)}, u32[]{:S(2)}, u32[]{:S(2)}) async-start(f32[4,8,8]{2,0,1:T(4,128)} %copy.105), calls=%async_computation | async-start | bytes 32768 | tf_op jit(solution)/shard_map/all_to_all | solution.py:86
  45.5 0.7 convert_reduce_fusion
  46.2 4.3 %copy.106 = bf16[4,512,576]{2,1,0:T(8,128)(2,1)} copy(bf16[4,512,576]{1,2,0:T(8,128)(2,1)} %param.11) | data formatting | bytes 4718592 | tf_op args[4]
  50.6 0.1 copy.114
  50.7 0.0 copy-start.1
  50.7 2.7 %select_reduce_fusion.1 = (bf16[4,8,576]{2,1,0:T(8,128)(2,1)S(1)}, bf16[4,8,576]{2,1,0:T(8,128)(2,1)S(1)}) fusion(pred[4,8,64]{2,1,0:T(8,128)(4,1)S(1)} %broadcast_compare_fusion, bf16[4,512,576]{2,1,0:T(8,128)(2,1)} %copy.106), kind=kLoop, calls=%fused_computation.3 | loop fusion | flops 4681728 | bytes 2435072 | tf_op jit(solution)/shard_map/reduce_min | solution.py:42
  53.4 0.0 copy-done.1
  53.4 1.0 %convolution_bitcast_fusion = f32[4,64,8,512]{3,1,2,0:T(8,128)S(1)} fusion(bf16[4,8,64,576]{3,2,1,0:T(8,128)(2,1)S(1)} %bitcast.20, f32[4,64,8,64]{3,2,1,0:T(8,128)S(1)} %reshape.136, f32[4,64,8]{1,2,0:T(8,128)S(1)} %fusion.6, pred[4,8,64]{2,1,0:T(8,128)(4,1)S(1)} %broadcast_compare_fusion), kind=kOutput, calls=%fused_computation.4 | convolution fusion | flops 134742016 | bytes 7360512 | tf_op jit(solution)/shard_map/rhpt,rptl->rhpl/dot_general | solution.py:75
  54.4 5.4 %fusion = f32[4,64,1,512]{3,2,1,0:T(1,128)S(1)} fusion(f32[4,64,8,1]{2,3,1,0:T(1,128)S(1)} %copy.114, f32[4,64,8,512]{3,1,2,0:T(8,128)S(1)} %convolution_bitcast_fusion), kind=kOutput, calls=%fused_computation | convolution fusion | flops 12582912 | bytes 4726784 | tf_op jit(solution)/shard_map/rhp,rhpl->rhl/dot_general | solution.py:84
  59.8 0.1 slice_reduce_fusion
  59.9 0.1 reshape.140
  60.0 0.6 copy.108
  60.6 0.0 all-to-all-done
  60.6 6.0 %all-to-all-start.2 = ((f32[4,8,8]{2,0,1:T(4,128)}), f32[4,8,8]{2,0,1:T(4,128)S(1)}, u32[]{:S(2)}, u32[]{:S(2)}) async-start(f32[4,8,8]{2,0,1:T(4,128)} %copy.108), calls=%async_computation.2 | async-start | bytes 32768 | tf_op jit(solution)/shard_map/all_to_all | solution.py:93
  66.6 0.0 copy-start.2
  66.6 0.5 fusion.10
  67.2 0.8 copy.107
  68.0 5.3 %all-to-all-done.2 = f32[4,8,8]{2,0,1:T(4,128)S(1)} async-done(((f32[4,8,8]{2,0,1:T(4,128)}), f32[4,8,8]{2,0,1:T(4,128)S(1)}, u32[]{:S(2)}, u32[]{:S(2)}) %all-to-all-start.2) | async-done | bytes 1056 | tf_op jit(solution)/shard_map/all_to_all | solution.py:93
  73.3 3.5 %all-to-all-start.1 = ((f32[4,8,8,512]{3,2,0,1:T(8,128)}), f32[4,8,8,512]{3,2,0,1:T(8,128)S(1)}, u32[]{:S(2)}, u32[]{:S(2)}) async-start(f32[4,8,8,512]{3,2,0,1:T(8,128)} %copy.107), calls=%async_computation.1 | async-start | bytes 1048576 | tf_op jit(solution)/shard_map/all_to_all | solution.py:100
  76.8 0.8 fusion.4
  77.6 0.1 select_reduce_fusion.2
  77.7 3.4 %pmax.7 = f32[4,8,8]{2,1,0:T(8,128)S(1)} all-reduce(f32[4,8,8]{2,1,0:T(8,128)S(1)} %select_reduce_fusion.2), channel_id=1, replica_groups=mesh['grp'=2,'seq'=8,'head'=2] {'head'}, use_global_device_ids=true, to_apply=%region_12.13 | all-reduce | flops 256 | bytes 2048 | tf_op jit(solution)/shard_map/pmax | solution.py:60
  81.1 0.6 broadcast_select_fusion
  81.7 5.2 %all-to-all-done.1 = f32[4,8,8,512]{3,2,0,1:T(8,128)S(1)} async-done(((f32[4,8,8,512]{3,2,0,1:T(8,128)}), f32[4,8,8,512]{3,2,0,1:T(8,128)S(1)}, u32[]{:S(2)}, u32[]{:S(2)}) %all-to-all-start.1) | async-done | bytes 524320 | tf_op jit(solution)/shard_map/all_to_all | solution.py:100
  87.0 0.1 multiply_reduce_fusion
  87.1 0.1 divide_convert_fusion
  87.2 0.0 copy-done.2
  87.2 0.2 fusion.5
  87.4 0.6 copy.113
  (11 shorter events, 0.2 us)
Async XLA Ops:
  0.6 1.2 %copy-start = (bf16[8,128,512]{2,1,0:T(8,128)(2,1)S(1)}, bf16[8,128,512]{2,1,0:T(8,128)(2,1)}, u32[]{:S(2)}) copy-start(bf16[8,128,512]{2,1,0:T(8,128)(2,1)} %param.9) | copy-start | bytes 3145732
  2.8 35.1 %copy-start.3 = (s32[4,8,32]{2,1,0:T(8,128)S(1)}, s32[4,8,32]{2,1,0:T(8,128)}, u32[]{:S(2)}) copy-start(s32[4,8,32]{2,1,0:T(8,128)} %param.13) | copy-start | bytes 12292
  2.8 35.9 %copy-start.4 = (s32[4]{0:T(128)S(1)}, s32[4]{0:T(128)}, u32[]{:S(2)}) copy-start(s32[4]{0:T(128)} %param.12) | copy-start | bytes 52
  39.9 20.7 %all-to-all-start = ((f32[4,8,8]{2,0,1:T(4,128)}), f32[4,8,8]{2,0,1:T(4,128)S(1)}, u32[]{:S(2)}, u32[]{:S(2)}) async-start(f32[4,8,8]{2,0,1:T(4,128)} %copy.105), calls=%async_computation | async-start | bytes 32768 | tf_op jit(solution)/shard_map/all_to_all | solution.py:86
  50.7 2.7 %copy-start.1 = (bf16[4,512,576]{2,1,0:T(8,128)(2,1)S(1)}, bf16[4,512,576]{2,1,0:T(8,128)(2,1)}, u32[]{:S(2)}) copy-start(bf16[4,512,576]{2,1,0:T(8,128)(2,1)} %copy.106) | copy-start | bytes 7077892
  60.6 12.6 %all-to-all-start.2 = ((f32[4,8,8]{2,0,1:T(4,128)}), f32[4,8,8]{2,0,1:T(4,128)S(1)}, u32[]{:S(2)}, u32[]{:S(2)}) async-start(f32[4,8,8]{2,0,1:T(4,128)} %copy.108), calls=%async_computation.2 | async-start | bytes 32768 | tf_op jit(solution)/shard_map/all_to_all | solution.py:93
  66.6 20.5 %copy-start.2 = (bf16[8,512,128]{2,1,0:T(8,128)(2,1)S(1)}, bf16[8,512,128]{2,1,0:T(8,128)(2,1)}, u32[]{:S(2)}) copy-start(bf16[8,512,128]{2,1,0:T(8,128)(2,1)} %param.10) | copy-start | bytes 3145732
  73.3 13.7 %all-to-all-start.1 = ((f32[4,8,8,512]{3,2,0,1:T(8,128)}), f32[4,8,8,512]{3,2,0,1:T(8,128)S(1)}, u32[]{:S(2)}, u32[]{:S(2)}) async-start(f32[4,8,8,512]{3,2,0,1:T(8,128)} %copy.107), calls=%async_computation.1 | async-start | bytes 1048576 | tf_op jit(solution)/shard_map/all_to_all | solution.py:100
where the time goes:
time: 88.6 us; the launch traced here: 88 us
  blocking collectives  36 us (41%)
  starting transfers between devices  15.1 us (17%)
  matrix products  11 us (12%)
  waiting for transfers between devices  10.5 us (12%)
  local copies, waits for them, and re-layouts  8.85 us (10%)
  other arithmetic  5.68 us (6%)
    all_gather x1, blocking collectives, local(): queries = lax.all_gather(absorbed, 'seq', axis=1, tiled=True)  32.6 us
    unnamed x13, local copies, waits for them, and re-layouts  6.15 us
    all_to_all x1, starting transfers between devices, local(): lax.all_to_all(total.reshape(requests, seq_count, head_block), 'seq', spl...  6 us
    all_to_all x1, starting transfers between devices, local(): lax.all_to_all(summit.reshape(requests, seq_count, head_block), 'seq', sp...  5.62 us
    dot_general x1, matrix products, local(): jnp.einsum('rhp,rhpl->rhl', factor, page_weighted, precision=lax.Precisio...  5.37 us
    all_to_all x1, waiting for transfers between devices, local(): lax.all_to_all(total.reshape(requests, seq_count, head_block), 'seq', spl...  5.28 us
    all_to_all x1, waiting for transfers between devices, local(): lax.all_to_all(weighted.reshape(requests, seq_count, head_block, latent_w...  5.23 us
    all_to_all x1, starting transfers between devices, local(): lax.all_to_all(weighted.reshape(requests, seq_count, head_block, latent_w...  3.49 us
  transfers between devices with their start and end apart: 3, of which 2 were waited for; matrix products, arithmetic and copies ran while one was open for 20% of the time, Pallas kernels for 0%

commit v1 on v0

v1 whole, which is shorter than its diff:
```python
import functools

import jax
import jax.numpy as jnp
from jax import lax
from jax.experimental import pallas as pl
from jax.experimental.pallas import tpu as pltpu
from jax.sharding import PartitionSpec as P

GH = 16
PAGE = 64
NEG = -1e30
BF16 = jnp.bfloat16
F32 = jnp.float32
LANES = 128
VMEM = pl.BlockSpec(memory_space=pltpu.VMEM)
SMEM = pl.BlockSpec(memory_space=pltpu.SMEM)


def params(mib=24):
    return pltpu.CompilerParams(vmem_limit_bytes=mib << 20)


def absorb_kernel(nope_ref, rope_ref, w_ref, out_ref):
    requests, heads, size = nope_ref.shape
    latent = w_ref.shape[2]
    rows = requests * heads
    nope = nope_ref[...].astype(F32).reshape(rows, size)
    head = lax.broadcasted_iota(jnp.int32, (rows, size), 0) % heads
    wide = jnp.concatenate(
        [jnp.where(head == j, nope, 0.0) for j in range(heads)], axis=1
    ).astype(BF16)
    weight = w_ref[...].reshape(heads * size, latent)
    out_ref[:, :latent] = jnp.dot(wide, weight, preferred_element_type=F32).astype(BF16)
    out_ref[:, latent:] = rope_ref[...].astype(F32).reshape(rows, rope_ref.shape[2]).astype(BF16)


def split3(x):
    high = x.astype(BF16)
    rest = x - high.astype(F32)
    middle = rest.astype(BF16)
    return high, middle, (rest - middle.astype(F32)).astype(BF16)


def queries_of(blocks, request, heads):
    rows = slice(request * heads, (request + 1) * heads)
    return jnp.concatenate([b[rows] for b in blocks], axis=0)


def group_of(offset, heads):
    source = jnp.bitwise_xor(lax.axis_index("seq"), offset)
    return (source * lax.axis_size("head") + lax.axis_index("head")) * heads // GH


def attend_kernel(scale, heads, offsets, latent, *refs):
    count = len(offsets)
    block_refs = refs[:count]
    cache_ref, selected_ref, lengths_ref, send_ref, keep_ref, sum_ref, mask_ref = refs[count:]
    requests, groups, picks = selected_ref.shape
    tokens = cache_ref.shape[2]
    pages = tokens // PAGE
    rank = lax.axis_index("seq")
    blocks = [b[...].astype(F32) for b in block_refs]
    place = selected_ref[...].reshape(requests * groups, picks) - rank * pages
    here = (place >= 0) & (place < pages)
    bits = jnp.sum(
        jnp.where(here, jnp.left_shift(1, jnp.where(here, place, 0)), 0).astype(F32),
        axis=1,
        keepdims=True,
    ).astype(jnp.int32)
    lane = lax.broadcasted_iota(jnp.int32, (groups, tokens), 1)
    for r in range(requests):
        word = bits[r * groups : (r + 1) * groups]
        picked = jnp.bitwise_and(jnp.right_shift(word, lane // PAGE), 1) == 1
        live = lane + rank * tokens < lengths_ref[r]
        mask_ref[r * groups : (r + 1) * groups, :] = jnp.where(picked & live, 1.0, 0.0)
    outs, sums = [], []
    for r in range(requests):
        query = queries_of(blocks, r, heads).astype(BF16)
        keys = cache_ref[r]
        scores = jnp.dot(query, keys, preferred_element_type=F32) * scale
        mask = jnp.concatenate(
            [
                jnp.broadcast_to(
                    mask_ref[pl.ds(r * groups + group_of(k, heads), 1), :], (heads, tokens)
                )
                for k in offsets
            ],
            axis=0,
        )
        scores = jnp.where(mask > 0.5, scores, NEG)
        top = jnp.max(scores, axis=1, keepdims=True)
        weights = jnp.where(mask > 0.5, jnp.exp(scores - top), 0.0).astype(BF16)
        total = jnp.sum(weights.astype(F32), axis=1, keepdims=True)
        weighted = lax.dot_general(
            weights, keys[:latent], (((1,), (1,)), ((), ())), preferred_element_type=F32
        )
        some = total > 0.0
        safe = jnp.where(some, total, 1.0)
        outs.append(weighted / safe)
        sums.append(jnp.where(some, top + jnp.log(safe), NEG))
    for i, k in enumerate(offsets):
        rows = slice(i * heads, (i + 1) * heads)
        out = jnp.concatenate([o[rows] for o in outs], axis=0)
        lse = jnp.concatenate([s[rows] for s in sums], axis=0)
        lse = jnp.broadcast_to(lse, (lse.shape[0], LANES))
        if k % 2:
            send_ref[k // 2, :, :latent] = out.astype(BF16)
            send_ref[k // 2, :, latent:] = packed(lse)
        else:
            keep_ref[k // 2] = out
            sum_ref[k // 2] = lse


def packed(lse):
    lane = lax.broadcasted_iota(jnp.int32, lse.shape, 1)
    high, middle, low = (p.astype(F32) for p in split3(lse))
    return jnp.where(lane == 0, high, jnp.where(lane == 1, middle, low)).astype(BF16)


def unpacked(tail):
    tail = tail.astype(F32)
    return tail[:, 0:1] + tail[:, 1:2] + tail[:, 2:3]


def merge(parts):
    top = functools.reduce(jnp.maximum, [s for _, s in parts])
    factors = [jnp.exp(s - top) for _, s in parts]
    total = functools.reduce(jnp.add, factors)
    mixed = functools.reduce(jnp.add, [f * o for f, (o, _) in zip(factors, parts)])
    return mixed / total, top + jnp.log(total)


def pair_kernel(latent, got_ref, keep_ref, sum_ref, own_ref, own_sum_ref, *send_refs):
    for i in range(got_ref.shape[0]):
        got = got_ref[i]
        out, lse = merge(
            [
                (got[:, :latent].astype(F32), unpacked(got[:, latent:])),
                (keep_ref[i], sum_ref[i][:, 0:1]),
            ]
        )
        lse = jnp.broadcast_to(lse, (lse.shape[0], LANES))
        if i == 0:
            own_ref[...] = out
            own_sum_ref[...] = lse
        else:
            send_refs[i - 1][:, :latent] = out.astype(BF16)
            send_refs[i - 1][:, latent:] = packed(lse)


def value_kernel(latent, heads, own_ref, own_sum_ref, w_ref, mine_ref, other_ref, lengths_ref, *refs):
    got_refs, (out_ref, bounds_ref) = refs[:-2], refs[-2:]
    requests = out_ref.shape[0]
    parts = [(own_ref[...], own_sum_ref[...][:, 0:1])]
    for got_ref in got_refs:
        got = got_ref[...]
        parts.append((got[:, :latent].astype(F32), unpacked(got[:, latent:])))
    mixed, _ = merge(parts)
    mixed = mixed.astype(BF16).astype(F32)
    rows = mixed.shape[0]
    head = lax.broadcasted_iota(jnp.int32, (rows, latent), 0) % heads
    out = jnp.zeros((rows, w_ref.shape[2]), F32)
    for j in range(heads):
        out += jnp.dot(
            jnp.where(head == j, mixed, 0.0).astype(BF16), w_ref[j], preferred_element_type=F32
        )
    out_ref[...] = out.reshape(out_ref.shape).astype(BF16)
    groups, pages = bounds_ref.shape[1:]
    first = (
        lax.axis_index("seq") * pages + lax.broadcasted_iota(jnp.int32, (groups, pages), 1)
    ) * PAGE
    for r in range(requests):
        bounds_ref[r] = jnp.where(
            first < lengths_ref[r], jnp.maximum(mine_ref[r], other_ref[r]), 0.0
        )


def bounds_kernel(scale, heads, offsets, *refs):
    count = len(offsets)
    block_refs = refs[:count]
    cache_ref, lengths_ref, out_ref = refs[count:]
    requests, groups, pages = out_ref.shape
    width, tokens = cache_ref.shape[1:]
    rank = lax.axis_index("seq")
    blocks = [b[...].astype(F32) for b in block_refs]
    row = lax.broadcasted_iota(jnp.int32, (tokens, width), 0)
    group = lax.broadcasted_iota(jnp.int32, (groups, pages), 0)
    for r in range(requests):
        slots = cache_ref[r].astype(F32).T
        slots = slots.reshape(pages, PAGE, width)
        live = (row + rank * tokens < lengths_ref[r]).reshape(pages, PAGE, width)
        slots = jnp.where(live, slots, slots[:, 0:1, :])
        low = jnp.min(slots, axis=1).astype(BF16)
        high = jnp.max(slots, axis=1).astype(BF16)
        query = queries_of(blocks, r, heads)
        dims = (((1,), (1,)), ((), ()))
        bound = lax.dot_general(
            jnp.maximum(query, 0.0).astype(BF16), high, dims, preferred_element_type=F32
        ) + lax.dot_general(
            jnp.minimum(query, 0.0).astype(BF16), low, dims, preferred_element_type=F32
        )
        bound = bound * scale
        best = jnp.full((groups, pages), NEG, F32)
        for i, k in enumerate(offsets):
            peak = jnp.max(bound[i * heads : (i + 1) * heads], axis=0, keepdims=True)
            best = jnp.where(group == group_of(k, heads), jnp.maximum(best, peak), best)
        out_ref[r] = best


def local(q_nope, q_rope, w_uk, w_uv, cache, lengths, selected):
    seq_count = lax.axis_size("seq")
    head_count = lax.axis_size("head")
    requests, heads, _ = q_nope.shape
    latent = w_uk.shape[2]
    width = cache.shape[2]
    tokens = cache.shape[1]
    pages = tokens // PAGE
    groups = selected.shape[1]
    rows = requests * heads
    scale = (q_nope.shape[2] + q_rope.shape[2]) ** (-0.5)
    assert seq_count & (seq_count - 1) == 0 and GH % heads == 0
    offsets = tuple(range(seq_count))
    far = tuple(reversed(range(2, seq_count, 2)))
    half = seq_count // 2
    slots = jnp.swapaxes(cache, 1, 2)

    def swap(x, k):
        return lax.ppermute(x, "seq", [(i, i ^ k) for i in range(seq_count)])

    mine = pl.pallas_call(
        absorb_kernel,
        out_shape=jax.ShapeDtypeStruct((rows, width), BF16),
        in_specs=[VMEM] * 3,
        out_specs=VMEM,
        compiler_params=params(),
        name="absorb",
    )(q_nope, q_rope, w_uk)
    block = {0: mine}
    for k in far:
        block[k] = swap(mine, k)
    block[1] = swap(mine, 1)
    for k in far:
        block[k + 1] = swap(block[k], 1)
    blocks = [block[k] for k in offsets]

    send, keep, sums = pl.pallas_call(
        functools.partial(attend_kernel, scale, heads, offsets, latent),
        out_shape=(
            jax.ShapeDtypeStruct((half, rows, latent + LANES), BF16),
            jax.ShapeDtypeStruct((half, rows, latent), F32),
            jax.ShapeDtypeStruct((half, rows, LANES), F32),
        ),
        in_specs=[VMEM] * (seq_count + 2) + [SMEM],
        out_specs=(VMEM,) * 3,
        scratch_shapes=[pltpu.VMEM((requests * groups, tokens), F32)],
        compiler_params=params(),
        name="attend",
    )(*blocks, slots, selected, lengths)
    got = swap(send, 1)

    bounds = pl.pallas_call(
        functools.partial(bounds_kernel, scale, heads, offsets),
        out_shape=jax.ShapeDtypeStruct((requests, groups, pages), F32),
        in_specs=[VMEM] * (seq_count + 1) + [SMEM],
        out_specs=VMEM,
        compiler_params=params(),
        name="page_bounds",
    )(*blocks, slots, lengths)
    others = lax.ppermute(
        bounds, "head", [(i, (i + 1) % head_count) for i in range(head_count)]
    )

    shape = jax.ShapeDtypeStruct((rows, latent + LANES), BF16)
    own, own_sum, *sends = pl.pallas_call(
        functools.partial(pair_kernel, latent),
        out_shape=(
            jax.ShapeDtypeStruct((rows, latent), F32),
            jax.ShapeDtypeStruct((rows, LANES), F32),
        )
        + (shape,) * (half - 1),
        in_specs=[VMEM] * 3,
        out_specs=(VMEM,) * (half + 1),
        compiler_params=params(),
        name="merge_pair",
    )(got, keep, sums)
    gots = {k: swap(sends[k // 2 - 1], k) for k in far}

    return pl.pallas_call(
        functools.partial(value_kernel, latent, heads),
        out_shape=(
            jax.ShapeDtypeStruct((requests, heads, w_uv.shape[2]), BF16),
            jax.ShapeDtypeStruct((requests, groups, pages), F32),
        ),
        in_specs=[VMEM] * 5 + [SMEM] + [VMEM] * (half - 1),
        out_specs=(VMEM, VMEM),
        compiler_params=params(),
        name="merge_and_value",
    )(own, own_sum, w_uv, bounds, others, lengths, *[gots[k] for k in far])


def solution(mesh):
    assert mesh.shape["head"] == 2
    placed = (
        P("grp", ("seq", "head"), None),
        P("grp", ("seq", "head"), None),
        P(("seq", "head"), None, None),
        P(("seq", "head"), None, None),
        P("grp", "seq", None),
        P("grp"),
        P("grp", None, None),
    )
    return jax.shard_map(
        local,
        mesh=mesh,
        in_specs=placed,
        out_specs=(P("grp", ("seq", "head"), None), P("grp", None, "seq")),
        check_vma=False,
    )
```

time: 88.6 us -> 40.1 us (0.45)
  blocking collectives: 36 us -> 0 us
  matrix products: 11 us -> 0 us
  Pallas kernels: 0 us -> 6.84 us
  other arithmetic: 5.68 us -> 0 us
  local copies, waits for them, and re-layouts: 8.85 us -> 5.65 us
  starting transfers between devices: 15.1 us -> 16 us
    all_gather x1 -> x0, blocking collectives: 32.6 us -> none  [local(): queries = lax.all_gather(absorbed, 'seq', axis=1, tiled=True)]
    ppermute x0 -> x12, starting transfers between devices: none -> 16 us  [the longest x11 16 us: swap(): return lax.ppermute(x, 'seq', [(i, i ^ k) for i in range(seq_count)])]
    all_to_all x3 -> x0, starting transfers between devices: 15.1 us -> none  [the longest x1 6 us: local(): lax.all_to_all(total.reshape(requests, seq_count, head_block), 'seq', spl...]
    dot_general x7 -> x0, matrix products: 11 us -> none  [the longest x1 5.37 us: local(): jnp.einsum('rhp,rhpl->rhl', factor, page_weighted, precision=lax.Precisio...]
    ppermute x0 -> x12, waiting for transfers between devices: none -> 10.5 us  [the longest x11 9.34 us: swap(): return lax.ppermute(x, 'seq', [(i, i ^ k) for i in range(seq_count)])]
    all_to_all x3 -> x0, waiting for transfers between devices: 10.5 us -> none  [the longest x1 5.28 us: local(): lax.all_to_all(total.reshape(requests, seq_count, head_block), 'seq', spl...]
    pallas_call x0 -> x5, Pallas kernels: none -> 6.84 us  [the longest x1 2.45 us: local(): pl.pallas_call(functools.partial(bounds_kernel, scale, heads, offsets), o...]
    pmax x1 -> x0, blocking collectives: 3.36 us -> none  [local(): group_bound = lax.pmax(group_bound, 'head')]
  transfers between devices with their start and end apart: 3 -> 12, of which waited for: 2 -> 5; matrix products, arithmetic and copies ran while one was open for 20% -> 0% of each run, Pallas kernels for 0% -> 6%
where the time goes in v1:
time: 40.1 us; the launch traced here: 39.7 us
  starting transfers between devices  16 us (40%)
  waiting for transfers between devices  10.5 us (26%)
  Pallas kernels  6.84 us (17%)
  local copies, waits for them, and re-layouts  5.65 us (14%)
  between operations  0.69 us (2%)
    ppermute x11, starting transfers between devices, swap(): return lax.ppermute(x, 'seq', [(i, i ^ k) for i in range(seq_count)])  16 us
    ppermute x11, waiting for transfers between devices, swap(): return lax.ppermute(x, 'seq', [(i, i ^ k) for i in range(seq_count)])  9.34 us
    unnamed x16, local copies, waits for them, and re-layouts  5.65 us
    pallas_call x1, Pallas kernels, local(): pl.pallas_call(functools.partial(bounds_kernel, scale, heads, offsets), o...  2.45 us
    pallas_call x1, Pallas kernels, local(): pl.pallas_call(functools.partial(attend_kernel, scale, heads, offsets, la...  2.33 us
    pallas_call x1, Pallas kernels, local(): pl.pallas_call(functools.partial(value_kernel, latent, heads), out_shape=...  1.57 us
    ppermute x1, waiting for transfers between devices, local(): lax.ppermute(bounds, 'head', [(i, (i + 1) % head_count) for i in range(he...  1.17 us
  transfers between devices with their start and end apart: 12, of which 5 were waited for; matrix products, arithmetic and copies ran while one was open for 0% of the time, Pallas kernels for 6%

profile of v1, /device:TPU:0, one launch (start us, length us, event | category | flops | bytes accessed | tf_op | source)
XLA Modules:
  0.0 39.7 jit_solution(810086245920360216)
XLA Ops:
  0.6 0.0 copy-start.3
  0.6 1.2 %copy-done.3 = bf16[8,128,512]{2,1,0:T(8,128)(2,1)S(1)} copy-done((bf16[8,128,512]{2,1,0:T(8,128)(2,1)S(1)}, bf16[8,128,512]{2,1,0:T(8,128)(2,1)}, u32[]{:S(2)}) %copy-start.3) | copy-done | bytes 1048600
  1.9 0.0 copy-start.5
  1.9 0.7 %copy-done.5 = bf16[4,8,128]{2,1,0:T(8,128)(2,1)S(1)} copy-done((bf16[4,8,128]{2,1,0:T(8,128)(2,1)S(1)}, bf16[4,8,128]{2,1,0:T(8,128)(2,1)}, u32[]{:S(2)}) %copy-start.5) | copy-done | bytes 8216
  2.6 0.0 copy-start.6
  2.6 0.7 %copy-done.6 = bf16[4,8,64]{2,1,0:T(8,128)(2,1)S(1)} copy-done((bf16[4,8,64]{2,1,0:T(8,128)(2,1)S(1)}, bf16[4,8,64]{2,1,0:T(8,128)(2,1)}, u32[]{:S(2)}) %copy-start.6) | copy-done | bytes 4120
  3.3 0.3 absorb.1.refs_0_
  3.5 5.1 %collective-permute-start.5 = (bf16[32,576]{1,0:T(8,128)(2,1)S(1)}, bf16[32,576]{1,0:T(8,128)(2,1)S(1)}, u32[]{:S(2)}, u32[]{:S(2)}) collective-permute-start(bf16[32,576]{1,0:T(8,128)(2,1)S(1)} %absorb.1.refs_0_), channel_id=1, source_target_pairs={{0,12},{2,14},{4,8},{6,10},{8,4},{10,6},{12,0},{14,2},{1,13},{3,15... | collective-permute-start | bytes 110600 | tf_op jit(solution)/shard_map/ppermute | solution.py:229
  8.6 0.0 collective-permute-start.3
  8.6 0.6 %collective-permute-start.1 = (bf16[32,576]{1,0:T(8,128)(2,1)S(1)}, bf16[32,576]{1,0:T(8,128)(2,1)S(1)}, u32[]{:S(2)}, u32[]{:S(2)}) collective-permute-start(bf16[32,576]{1,0:T(8,128)(2,1)S(1)} %absorb.1.refs_0_), channel_id=1, source_target_pairs={{0,4},{2,6},{4,0},{6,2},{8,12},{10,14},{12,8},{14,10},{1,5},{3,7},... | collective-permute-start | bytes 110600 | tf_op jit(solution)/shard_map/ppermute | solution.py:229
  9.2 1.7 %collective-permute-start = (bf16[32,576]{1,0:T(8,128)(2,1)S(1)}, bf16[32,576]{1,0:T(8,128)(2,1)S(1)}, u32[]{:S(2)}, u32[]{:S(2)}) collective-permute-start(bf16[32,576]{1,0:T(8,128)(2,1)S(1)} %absorb.1.refs_0_), channel_id=1, source_target_pairs={{0,2},{2,0},{4,6},{6,4},{8,10},{10,8},{12,14},{14,12},{1,3},{3,1},... | collective-permute-start | bytes 110600 | tf_op jit(solution)/shard_map/ppermute | solution.py:229
  10.9 0.0 collective-permute-done.5.refs_6_
  10.9 1.6 %collective-permute-start.6 = (bf16[32,576]{1,0:T(8,128)(2,1)S(1)}, bf16[32,576]{1,0:T(8,128)(2,1)S(1)}, u32[]{:S(2)}, u32[]{:S(2)}) collective-permute-start(bf16[32,576]{1,0:T(8,128)(2,1)S(1)} %collective-permute-done.5.refs_6_), channel_id=1, source_target_pairs={{0,2},{2,0},{4,6},{6,4},{8,10},{10,8},{12,14},{14,12},{1,3},{3,1},... | collective-permute-start | bytes 110600 | tf_op jit(solution)/shard_map/ppermute | solution.py:229
  12.5 1.0 %collective-permute-done.3.refs_4_ = bf16[32,576]{1,0:T(8,128)(2,1)S(1)} collective-permute-done((bf16[32,576]{1,0:T(8,128)(2,1)S(1)}, bf16[32,576]{1,0:T(8,128)(2,1)S(1)}, u32[]{:S(2)}, u32[]{:S(2)}) %collective-permute-start.3) | collective-permute-done | bytes 36896 | tf_op jit(solution)/shard_map/ppermute | solution.py:229
  13.5 1.5 %collective-permute-start.4 = (bf16[32,576]{1,0:T(8,128)(2,1)S(1)}, bf16[32,576]{1,0:T(8,128)(2,1)S(1)}, u32[]{:S(2)}, u32[]{:S(2)}) collective-permute-start(bf16[32,576]{1,0:T(8,128)(2,1)S(1)} %collective-permute-done.3.refs_4_), channel_id=1, source_target_pairs={{0,2},{2,0},{4,6},{6,4},{8,10},{10,8},{12,14},{14,12},{1,3},{3,1},... | collective-permute-start | bytes 110600 | tf_op jit(solution)/shard_map/ppermute | solution.py:229
  15.0 0.0 collective-permute-done.1.refs_2_
  15.0 0.5 %collective-permute-start.2 = (bf16[32,576]{1,0:T(8,128)(2,1)S(1)}, bf16[32,576]{1,0:T(8,128)(2,1)S(1)}, u32[]{:S(2)}, u32[]{:S(2)}) collective-permute-start(bf16[32,576]{1,0:T(8,128)(2,1)S(1)} %collective-permute-done.1.refs_2_), channel_id=1, source_target_pairs={{0,2},{2,0},{4,6},{6,4},{8,10},{10,8},{12,14},{14,12},{1,3},{3,1},... | collective-permute-start | bytes 110600 | tf_op jit(solution)/shard_map/ppermute | solution.py:229
  15.5 0.0 collective-permute-done.refs_1_
  15.5 0.0 collective-permute-done.6.refs_7_
  15.5 2.0 %collective-permute-done.4.refs_5_ = bf16[32,576]{1,0:T(8,128)(2,1)S(1)} collective-permute-done((bf16[32,576]{1,0:T(8,128)(2,1)S(1)}, bf16[32,576]{1,0:T(8,128)(2,1)S(1)}, u32[]{:S(2)}, u32[]{:S(2)}) %collective-permute-start.4) | collective-permute-done | bytes 36896 | tf_op jit(solution)/shard_map/ppermute | solution.py:229
  17.5 1.5 %collective-permute-done.2.refs_3_ = bf16[32,576]{1,0:T(8,128)(2,1)S(1)} collective-permute-done((bf16[32,576]{1,0:T(8,128)(2,1)S(1)}, bf16[32,576]{1,0:T(8,128)(2,1)S(1)}, u32[]{:S(2)}, u32[]{:S(2)}) %collective-permute-start.2) | collective-permute-done | bytes 36896 | tf_op jit(solution)/shard_map/ppermute | solution.py:229
  19.0 0.0 copy-start
  19.0 1.7 %copy-done = bf16[4,512,576]{1,2,0:T(8,128)(2,1)S(1)} copy-done((bf16[4,512,576]{1,2,0:T(8,128)(2,1)S(1)}, bf16[4,512,576]{1,2,0:T(8,128)(2,1)}, u32[]{:S(2)}) %copy-start) | copy-done | bytes 2359320
  20.7 0.0 copy-start.4
  20.7 0.7 %copy-done.4 = s32[4,8,32]{2,1,0:T(8,128)S(1)} copy-done((s32[4,8,32]{2,1,0:T(8,128)S(1)}, s32[4,8,32]{2,1,0:T(8,128)}, u32[]{:S(2)}) %copy-start.4) | copy-done | bytes 4120
  21.4 0.0 copy-start.7
  21.4 0.7 %copy-done.7 = s32[4]{0:T(128)S(1)} copy-done((s32[4]{0:T(128)S(1)}, s32[4]{0:T(128)}, u32[]{:S(2)}) %copy-start.7) | copy-done | bytes 40
  22.1 0.0 copy-start.1
  22.1 0.0 copy-start.2
  22.1 2.3 %attend.1 = (bf16[4,32,640]{2,1,0:T(8,128)(2,1)S(1)}, f32[4,32,512]{2,1,0:T(8,128)S(1)}, f32[4,32,128]{2,1,0:T(8,128)S(1)}) custom-call(bf16[32,576]{1,0:T(8,128)(2,1)S(1)} %absorb.1.refs_0_, bf16[32,576]{1,0:T(8,128)(2,1)S(1)} %collective-permute-done.refs_1_, bf16[32,576]{1,0:T(8,128)(2,1)S(1)} %collective-permute-done.1.refs_2_, ...), custom_call_target="tpu_custom_call" | custom-call | tf_op jit(solution)/shard_map/attend/pallas_call | solution.py:247
  24.4 0.5 %collective-permute-start.7 = (bf16[4,32,640]{2,1,0:T(8,128)(2,1)S(1)}, bf16[4,32,640]{2,1,0:T(8,128)(2,1)S(1)}, u32[]{:S(2)}, u32[]{:S(2)}) collective-permute-start(bf16[4,32,640]{2,1,0:T(8,128)(2,1)S(1)} %get-tuple-element.10), channel_id=1, source_target_pairs={{0,2},{2,0},{4,6},{6,4},{8,10},{10,8},{12,14},{14,12},{1,3},{3,1},... | collective-permute-start | bytes 491528 | tf_op jit(solution)/shard_map/ppermute | solution.py:229
  24.9 4.8 %collective-permute-done.7.got_ref = bf16[4,32,640]{2,1,0:T(8,128)(2,1)S(1)} collective-permute-done((bf16[4,32,640]{2,1,0:T(8,128)(2,1)S(1)}, bf16[4,32,640]{2,1,0:T(8,128)(2,1)S(1)}, u32[]{:S(2)}, u32[]{:S(2)}) %collective-permute-start.7) | collective-permute-done | bytes 163872 | tf_op jit(solution)/shard_map/ppermute | solution.py:229
  29.8 0.2 merge_pair.1
  30.0 1.7 %collective-permute-start.9 = (bf16[32,640]{1,0:T(8,128)(2,1)S(1)}, bf16[32,640]{1,0:T(8,128)(2,1)S(1)}, u32[]{:S(2)}, u32[]{:S(2)}) collective-permute-start(bf16[32,640]{1,0:T(8,128)(2,1)S(1)} %get-tuple-element.15), channel_id=1, source_target_pairs={{0,12},{2,14},{4,8},{6,10},{8,4},{10,6},{12,0},{14,2},{1,13},{3,15... | collective-permute-start | bytes 122888 | tf_op jit(solution)/shard_map/ppermute | solution.py:229
  31.6 0.0 collective-permute-start.10
  31.6 2.8 %collective-permute-start.11 = (bf16[32,640]{1,0:T(8,128)(2,1)S(1)}, bf16[32,640]{1,0:T(8,128)(2,1)S(1)}, u32[]{:S(2)}, u32[]{:S(2)}) collective-permute-start(bf16[32,640]{1,0:T(8,128)(2,1)S(1)} %get-tuple-element.17), channel_id=1, source_target_pairs={{0,4},{2,6},{4,0},{6,2},{8,12},{10,14},{12,8},{14,10},{1,5},{3,7},... | collective-permute-start | bytes 122888 | tf_op jit(solution)/shard_map/ppermute | solution.py:229
  34.4 0.0 copy-done.1
  34.4 2.4 %page_bounds.1.mine_ref = f32[4,8,8]{2,1,0:T(8,128)S(1)} custom-call(bf16[32,576]{1,0:T(8,128)(2,1)S(1)} %absorb.1.refs_0_, bf16[32,576]{1,0:T(8,128)(2,1)S(1)} %collective-permute-done.refs_1_, bf16[32,576]{1,0:T(8,128)(2,1)S(1)} %collective-permute-done.1.refs_2_, bf16[32,576]{1,0:T(8,128)(2,1)S(1)} %collective-permute-done.2.refs_3_, ...), custom_call_target="tpu_custom_call" | custom-call | tf_op jit(solution)/shard_map/page_bounds/pallas_call | solution.py:262
  36.9 0.1 collective-permute-start.8
  37.0 1.2 %collective-permute-done.8.other_ref = f32[4,8,8]{2,1,0:T(8,128)S(1)} collective-permute-done((f32[4,8,8]{2,1,0:T(8,128)S(1)}, f32[4,8,8]{2,1,0:T(8,128)S(1)}, u32[]{:S(2)}, u32[]{:S(2)}) %collective-permute-start.8) | collective-permute-done | bytes 1056 | tf_op jit(solution)/shard_map/ppermute | solution.py:270
  38.1 0.0 collective-permute-done.9.refs_0_
  38.1 0.0 collective-permute-done.10.refs_1_
  38.1 0.0 collective-permute-done.11.refs_2_
  38.2 0.0 copy-done.2
  38.2 1.6 %merge_and_value.1 = (bf16[4,8,128]{2,1,0:T(8,128)(2,1)}, f32[4,8,8]{2,1,0:T(8,128)}) custom-call(f32[32,512]{1,0:T(8,128)S(1)} %get-tuple-element.13.own_ref, f32[32,128]{1,0:T(8,128)S(1)} %get-tuple-element.14.own_sum_ref, bf16[8,512,128]{2,1,0:T(8,128)(2,1)S(1)} %copy-done.2, f32[4,8,8]{2,1,0:T(8,128)S(1)} %page_bounds.1.mine_ref, ...), custom_call_target="tpu_custom_call" | custom-call | tf_op jit(solution)/shard_map/merge_and_value/pallas_call | solution.py:289
Async XLA Ops:
  0.6 1.2 %copy-start.3 = (bf16[8,128,512]{2,1,0:T(8,128)(2,1)S(1)}, bf16[8,128,512]{2,1,0:T(8,128)(2,1)}, u32[]{:S(2)}) copy-start(bf16[8,128,512]{2,1,0:T(8,128)(2,1)} %w_ref.2) | copy-start | bytes 3145732
  1.9 0.7 %copy-start.5 = (bf16[4,8,128]{2,1,0:T(8,128)(2,1)S(1)}, bf16[4,8,128]{2,1,0:T(8,128)(2,1)}, u32[]{:S(2)}) copy-start(bf16[4,8,128]{2,1,0:T(8,128)(2,1)} %nope_ref.1) | copy-start | bytes 24580
  2.6 0.7 %copy-start.6 = (bf16[4,8,64]{2,1,0:T(8,128)(2,1)S(1)}, bf16[4,8,64]{2,1,0:T(8,128)(2,1)}, u32[]{:S(2)}) copy-start(bf16[4,8,64]{2,1,0:T(8,128)(2,1)} %rope_ref.1) | copy-start | bytes 12292
  3.5 7.4 %collective-permute-start.5 = (bf16[32,576]{1,0:T(8,128)(2,1)S(1)}, bf16[32,576]{1,0:T(8,128)(2,1)S(1)}, u32[]{:S(2)}, u32[]{:S(2)}) collective-permute-start(bf16[32,576]{1,0:T(8,128)(2,1)S(1)} %absorb.1.refs_0_), channel_id=1, source_target_pairs={{0,12},{2,14},{4,8},{6,10},{8,4},{10,6},{12,0},{14,2},{1,13},{3,15... | collective-permute-start | bytes 110600 | tf_op jit(solution)/shard_map/ppermute | solution.py:229
  8.6 4.9 %collective-permute-start.3 = (bf16[32,576]{1,0:T(8,128)(2,1)S(1)}, bf16[32,576]{1,0:T(8,128)(2,1)S(1)}, u32[]{:S(2)}, u32[]{:S(2)}) collective-permute-start(bf16[32,576]{1,0:T(8,128)(2,1)S(1)} %absorb.1.refs_0_), channel_id=1, source_target_pairs={{0,8},{2,10},{4,12},{6,14},{8,0},{10,2},{12,4},{14,6},{1,9},{3,11}... | collective-permute-start | bytes 110600 | tf_op jit(solution)/shard_map/ppermute | solution.py:229
  8.6 6.4 %collective-permute-start.1 = (bf16[32,576]{1,0:T(8,128)(2,1)S(1)}, bf16[32,576]{1,0:T(8,128)(2,1)S(1)}, u32[]{:S(2)}, u32[]{:S(2)}) collective-permute-start(bf16[32,576]{1,0:T(8,128)(2,1)S(1)} %absorb.1.refs_0_), channel_id=1, source_target_pairs={{0,4},{2,6},{4,0},{6,2},{8,12},{10,14},{12,8},{14,10},{1,5},{3,7},... | collective-permute-start | bytes 110600 | tf_op jit(solution)/shard_map/ppermute | solution.py:229
  9.2 6.3 %collective-permute-start = (bf16[32,576]{1,0:T(8,128)(2,1)S(1)}, bf16[32,576]{1,0:T(8,128)(2,1)S(1)}, u32[]{:S(2)}, u32[]{:S(2)}) collective-permute-start(bf16[32,576]{1,0:T(8,128)(2,1)S(1)} %absorb.1.refs_0_), channel_id=1, source_target_pairs={{0,2},{2,0},{4,6},{6,4},{8,10},{10,8},{12,14},{14,12},{1,3},{3,1},... | collective-permute-start | bytes 110600 | tf_op jit(solution)/shard_map/ppermute | solution.py:229
  10.9 4.6 %collective-permute-start.6 = (bf16[32,576]{1,0:T(8,128)(2,1)S(1)}, bf16[32,576]{1,0:T(8,128)(2,1)S(1)}, u32[]{:S(2)}, u32[]{:S(2)}) collective-permute-start(bf16[32,576]{1,0:T(8,128)(2,1)S(1)} %collective-permute-done.5.refs_6_), channel_id=1, source_target_pairs={{0,2},{2,0},{4,6},{6,4},{8,10},{10,8},{12,14},{14,12},{1,3},{3,1},... | collective-permute-start | bytes 110600 | tf_op jit(solution)/shard_map/ppermute | solution.py:229
  13.5 4.0 %collective-permute-start.4 = (bf16[32,576]{1,0:T(8,128)(2,1)S(1)}, bf16[32,576]{1,0:T(8,128)(2,1)S(1)}, u32[]{:S(2)}, u32[]{:S(2)}) collective-permute-start(bf16[32,576]{1,0:T(8,128)(2,1)S(1)} %collective-permute-done.3.refs_4_), channel_id=1, source_target_pairs={{0,2},{2,0},{4,6},{6,4},{8,10},{10,8},{12,14},{14,12},{1,3},{3,1},... | collective-permute-start | bytes 110600 | tf_op jit(solution)/shard_map/ppermute | solution.py:229
  15.0 4.0 %collective-permute-start.2 = (bf16[32,576]{1,0:T(8,128)(2,1)S(1)}, bf16[32,576]{1,0:T(8,128)(2,1)S(1)}, u32[]{:S(2)}, u32[]{:S(2)}) collective-permute-start(bf16[32,576]{1,0:T(8,128)(2,1)S(1)} %collective-permute-done.1.refs_2_), channel_id=1, source_target_pairs={{0,2},{2,0},{4,6},{6,4},{8,10},{10,8},{12,14},{14,12},{1,3},{3,1},... | collective-permute-start | bytes 110600 | tf_op jit(solution)/shard_map/ppermute | solution.py:229
  19.0 1.7 %copy-start = (bf16[4,512,576]{1,2,0:T(8,128)(2,1)S(1)}, bf16[4,512,576]{1,2,0:T(8,128)(2,1)}, u32[]{:S(2)}) copy-start(bf16[4,512,576]{1,2,0:T(8,128)(2,1)} %param.11) | copy-start | bytes 7077892
  20.7 0.7 %copy-start.4 = (s32[4,8,32]{2,1,0:T(8,128)S(1)}, s32[4,8,32]{2,1,0:T(8,128)}, u32[]{:S(2)}) copy-start(s32[4,8,32]{2,1,0:T(8,128)} %refs_9_.2) | copy-start | bytes 12292
  21.4 0.7 %copy-start.7 = (s32[4]{0:T(128)S(1)}, s32[4]{0:T(128)}, u32[]{:S(2)}) copy-start(s32[4]{0:T(128)} %lengths_ref.1) | copy-start | bytes 52
  22.1 12.4 %copy-start.1 = (bf16[4,512,576]{1,2,0:T(8,128)(2,1)S(1)}, bf16[4,512,576]{1,2,0:T(8,128)(2,1)}, u32[]{:S(2)}) copy-start(bf16[4,512,576]{1,2,0:T(8,128)(2,1)} %param.11) | copy-start | bytes 7077892
  22.1 16.1 %copy-start.2 = (bf16[8,512,128]{2,1,0:T(8,128)(2,1)S(1)}, bf16[8,512,128]{2,1,0:T(8,128)(2,1)}, u32[]{:S(2)}) copy-start(bf16[8,512,128]{2,1,0:T(8,128)(2,1)} %w_ref.3) | copy-start | bytes 3145732
  24.4 5.4 %collective-permute-start.7 = (bf16[4,32,640]{2,1,0:T(8,128)(2,1)S(1)}, bf16[4,32,640]{2,1,0:T(8,128)(2,1)S(1)}, u32[]{:S(2)}, u32[]{:S(2)}) collective-permute-start(bf16[4,32,640]{2,1,0:T(8,128)(2,1)S(1)} %get-tuple-element.10), channel_id=1, source_target_pairs={{0,2},{2,0},{4,6},{6,4},{8,10},{10,8},{12,14},{14,12},{1,3},{3,1},... | collective-permute-start | bytes 491528 | tf_op jit(solution)/shard_map/ppermute | solution.py:229
  30.0 8.2 %collective-permute-start.9 = (bf16[32,640]{1,0:T(8,128)(2,1)S(1)}, bf16[32,640]{1,0:T(8,128)(2,1)S(1)}, u32[]{:S(2)}, u32[]{:S(2)}) collective-permute-start(bf16[32,640]{1,0:T(8,128)(2,1)S(1)} %get-tuple-element.15), channel_id=1, source_target_pairs={{0,12},{2,14},{4,8},{6,10},{8,4},{10,6},{12,0},{14,2},{1,13},{3,15... | collective-permute-start | bytes 122888 | tf_op jit(solution)/shard_map/ppermute | solution.py:229
  31.6 6.5 %collective-permute-start.10 = (bf16[32,640]{1,0:T(8,128)(2,1)S(1)}, bf16[32,640]{1,0:T(8,128)(2,1)S(1)}, u32[]{:S(2)}, u32[]{:S(2)}) collective-permute-start(bf16[32,640]{1,0:T(8,128)(2,1)S(1)} %get-tuple-element.16), channel_id=1, source_target_pairs={{0,8},{2,10},{4,12},{6,14},{8,0},{10,2},{12,4},{14,6},{1,9},{3,11}... | collective-permute-start | bytes 122888 | tf_op jit(solution)/shard_map/ppermute | solution.py:229
  31.6 6.5 %collective-permute-start.11 = (bf16[32,640]{1,0:T(8,128)(2,1)S(1)}, bf16[32,640]{1,0:T(8,128)(2,1)S(1)}, u32[]{:S(2)}, u32[]{:S(2)}) collective-permute-start(bf16[32,640]{1,0:T(8,128)(2,1)S(1)} %get-tuple-element.17), channel_id=1, source_target_pairs={{0,4},{2,6},{4,0},{6,2},{8,12},{10,14},{12,8},{14,10},{1,5},{3,7},... | collective-permute-start | bytes 122888 | tf_op jit(solution)/shard_map/ppermute | solution.py:229
  36.9 1.2 %collective-permute-start.8 = (f32[4,8,8]{2,1,0:T(8,128)S(1)}, f32[4,8,8]{2,1,0:T(8,128)S(1)}, u32[]{:S(2)}, u32[]{:S(2)}) collective-permute-start(f32[4,8,8]{2,1,0:T(8,128)S(1)} %page_bounds.1.mine_ref), channel_id=1, source_target_pairs={{0,1},{1,0},{2,3},{3,2},{4,5},{5,4},{6,7},{7,6},{8,9},{9,8},{10,11... | collective-permute-start | bytes 3080 | tf_op jit(solution)/shard_map/ppermute | solution.py:270

commit v2 on v1

--- a/solution.py
+++ b/solution.py
@@ -15,52 +15,69 @@
 LANES = 128
 VMEM = pl.BlockSpec(memory_space=pltpu.VMEM)
 SMEM = pl.BlockSpec(memory_space=pltpu.SMEM)
+HBM = pl.BlockSpec(memory_space=pltpu.HBM)
+ANY = pl.BlockSpec(memory_space=pl.ANY)
 
 
 def params(mib=24):
     return pltpu.CompilerParams(vmem_limit_bytes=mib << 20)
 
 
-def absorb_kernel(nope_ref, rope_ref, w_ref, out_ref):
+def absorb_kernel(nope_hbm, rope_hbm, w_hbm, out_ref, nope_ref, rope_ref, w_ref, sems):
     requests, heads, size = nope_ref.shape
     latent = w_ref.shape[2]
     rows = requests * heads
+    step = 2 if heads % 2 == 0 else 1
+    pieces = heads // step
+    small = [
+        pltpu.make_async_copy(nope_hbm, nope_ref, sems.at[pieces]),
+        pltpu.make_async_copy(rope_hbm, rope_ref, sems.at[pieces + 1]),
+    ]
+    large = [
+        pltpu.make_async_copy(
+            w_hbm.at[pl.ds(i * step, step)], w_ref.at[pl.ds(i * step, step)], sems.at[i]
+        )
+        for i in range(pieces)
+    ]
+    for copy in small + large:
+        copy.start()
+    for copy in small:
+        copy.wait()
     nope = nope_ref[...].astype(F32).reshape(rows, size)
     head = lax.broadcasted_iota(jnp.int32, (rows, size), 0) % heads
-    wide = jnp.concatenate(
-        [jnp.where(head == j, nope, 0.0) for j in range(heads)], axis=1
-    ).astype(BF16)
-    weight = w_ref[...].reshape(heads * size, latent)
-    out_ref[:, :latent] = jnp.dot(wide, weight, preferred_element_type=F32).astype(BF16)
     out_ref[:, latent:] = rope_ref[...].astype(F32).reshape(rows, rope_ref.shape[2]).astype(BF16)
-
-
-def split3(x):
-    high = x.astype(BF16)
-    rest = x - high.astype(F32)
-    middle = rest.astype(BF16)
-    return high, middle, (rest - middle.astype(F32)).astype(BF16)
-
-
-def queries_of(blocks, request, heads):
-    rows = slice(request * heads, (request + 1) * heads)
-    return jnp.concatenate([b[rows] for b in blocks], axis=0)
-
-
-def group_of(offset, heads):
-    source = jnp.bitwise_xor(lax.axis_index("seq"), offset)
-    return (source * lax.axis_size("head") + lax.axis_index("head")) * heads // GH
-
-
-def attend_kernel(scale, heads, offsets, latent, *refs):
-    count = len(offsets)
-    block_refs = refs[:count]
-    cache_ref, selected_ref, lengths_ref, send_ref, keep_ref, sum_ref, mask_ref = refs[count:]
+    total = jnp.zeros((rows, latent), F32)
+    for i, copy in enumerate(large):
+        wide = jnp.concatenate(
+            [jnp.where(head == i * step + j, nope, 0.0) for j in range(step)], axis=1
+        ).astype(BF16)
+        copy.wait()
+        weight = w_ref[i * step : (i + 1) * step].reshape(step * size, latent)
+        total += jnp.dot(wide, weight, preferred_element_type=F32)
+    out_ref[:, :latent] = total.astype(BF16)
+
+
+def stage_kernel(
+    cache_hbm, w_hbm, selected_hbm, lengths_hbm, after_ref,
+    cache_ref, w_ref, mask_ref, low_ref, high_ref, selected_ref, lengths_ref, sems,
+):
     requests, groups, picks = selected_ref.shape
-    tokens = cache_ref.shape[2]
+    width, tokens = cache_ref.shape[1:]
     pages = tokens // PAGE
     rank = lax.axis_index("seq")
-    blocks = [b[...].astype(F32) for b in block_refs]
+    copies = [
+        pltpu.make_async_copy(selected_hbm, selected_ref, sems.at[0]),
+        pltpu.make_async_copy(lengths_hbm, lengths_ref, sems.at[1]),
+        *(
+            pltpu.make_async_copy(cache_hbm.at[r], cache_ref.at[r], sems.at[3 + r])
+            for r in range(requests)
+        ),
+        pltpu.make_async_copy(w_hbm, w_ref, sems.at[2]),
+    ]
+    for copy in copies:
+        copy.start()
+    copies[0].wait()
+    copies[1].wait()
     place = selected_ref[...].reshape(requests * groups, picks) - rank * pages
     here = (place >= 0) & (place < pages)
     bits = jnp.sum(
@@ -74,6 +91,42 @@
         picked = jnp.bitwise_and(jnp.right_shift(word, lane // PAGE), 1) == 1
         live = lane + rank * tokens < lengths_ref[r]
         mask_ref[r * groups : (r + 1) * groups, :] = jnp.where(picked & live, 1.0, 0.0)
+    row = lax.broadcasted_iota(jnp.int32, (tokens, width), 0) + rank * tokens
+    for r in range(requests):
+        copies[2 + r].wait()
+        slots = cache_ref[r].astype(F32).T
+        live = row < lengths_ref[r]
+        slots = slots.reshape(pages, PAGE, width)
+        slots = jnp.where(live.reshape(pages, PAGE, width), slots, slots[:, 0:1, :])
+        low_ref[r] = jnp.min(slots, axis=1)
+        high_ref[r] = jnp.max(slots, axis=1)
+    copies[-1].wait()
+
+
+def split3(x):
+    high = x.astype(BF16)
+    rest = x - high.astype(F32)
+    middle = rest.astype(BF16)
+    return high, middle, (rest - middle.astype(F32)).astype(BF16)
+
+
+def queries_of(blocks, request, heads):
+    rows = slice(request * heads, (request + 1) * heads)
+    return jnp.concatenate([b[rows] for b in blocks], axis=0)
+
+
+def group_of(offset, heads):
+    source = jnp.bitwise_xor(lax.axis_index("seq"), offset)
+    return (source * lax.axis_size("head") + lax.axis_index("head")) * heads // GH
+
+
+def attend_kernel(scale, heads, offsets, latent, *refs):
+    count = len(offsets)
+    block_refs = refs[:count]
+    cache_ref, mask_ref, send_ref, keep_ref, sum_ref = refs[count:]
+    requests, _, tokens = cache_ref.shape
+    groups = mask_ref.shape[0] // requests
+    blocks = [b[...].astype(F32) for b in block_refs]
     outs, sums = [], []
     for r in range(requests):
         query = queries_of(blocks, r, heads).astype(BF16)
@@ -131,7 +184,7 @@
     return mixed / total, top + jnp.log(total)
 
 
-def pair_kernel(latent, got_ref, keep_ref, sum_ref, own_ref, own_sum_ref, *send_refs):
+def pair_kernel(latent, got_ref, keep_ref, sum_ref, after_ref, own_ref, own_sum_ref, *send_refs):
     for i in range(got_ref.shape[0]):
         got = got_ref[i]
         out, lse = merge(
@@ -149,24 +202,32 @@
             send_refs[i - 1][:, latent:] = packed(lse)
 
 
-def value_kernel(latent, heads, own_ref, own_sum_ref, w_ref, mine_ref, other_ref, lengths_ref, *refs):
-    got_refs, (out_ref, bounds_ref) = refs[:-2], refs[-2:]
-    requests = out_ref.shape[0]
+def value_kernel(latent, heads, own_ref, own_sum_ref, w_ref, *refs):
+    got_refs, out_ref = refs[:-1], refs[-1]
     parts = [(own_ref[...], own_sum_ref[...][:, 0:1])]
     for got_ref in got_refs:
         got = got_ref[...]
         parts.append((got[:, :latent].astype(F32), unpacked(got[:, latent:])))
-    mixed, _ = merge(parts)
-    mixed = mixed.astype(BF16).astype(F32)
-    rows = mixed.shape[0]
-    head = lax.broadcasted_iota(jnp.int32, (rows, latent), 0) % heads
-    out = jnp.zeros((rows, w_ref.shape[2]), F32)
-    for j in range(heads):
-        out += jnp.dot(
-            jnp.where(head == j, mixed, 0.0).astype(BF16), w_ref[j], preferred_element_type=F32
-        )
+    mixed = merge(parts)[0].astype(BF16)
+    size = w_ref.shape[2]
+    head = lax.broadcasted_iota(jnp.int32, (mixed.shape[0], size), 0) % heads
+    out = jnp.zeros((mixed.shape[0], size), F32)
+    step = 2 if heads % 2 == 0 else 1
+    for i in range(0, heads, step):
+        weight = jnp.concatenate([w_ref[i + j] for j in range(step)], axis=1)
+        both = jnp.dot(mixed, weight, preferred_element_type=F32)
+        for j in range(step):
+            out = jnp.where(head == i + j, both[:, j * size : (j + 1) * size], out)
     out_ref[...] = out.reshape(out_ref.shape).astype(BF16)
-    groups, pages = bounds_ref.shape[1:]
+
+
+def largest_kernel(
+    mine_ref, other_ref, lengths_hbm, after_ref, bounds_ref, lengths_ref, sem
+):
+    requests, groups, pages = bounds_ref.shape
+    copy = pltpu.make_async_copy(lengths_hbm, lengths_ref, sem)
+    copy.start()
+    copy.wait()
     first = (
         lax.axis_index("seq") * pages + lax.broadcasted_iota(jnp.int32, (groups, pages), 1)
     ) * PAGE
@@ -179,26 +240,23 @@
 def bounds_kernel(scale, heads, offsets, *refs):
     count = len(offsets)
     block_refs = refs[:count]
-    cache_ref, lengths_ref, out_ref = refs[count:]
+    low_ref, high_ref, after_ref, out_ref = refs[count:]
     requests, groups, pages = out_ref.shape
-    width, tokens = cache_ref.shape[1:]
-    rank = lax.axis_index("seq")
     blocks = [b[...].astype(F32) for b in block_refs]
-    row = lax.broadcasted_iota(jnp.int32, (tokens, width), 0)
     group = lax.broadcasted_iota(jnp.int32, (groups, pages), 0)
+    dims = (((1,), (1,)), ((), ()))
     for r in range(requests):
-        slots = cache_ref[r].astype(F32).T
-        slots = slots.reshape(pages, PAGE, width)
-        live = (row + rank * tokens < lengths_ref[r]).reshape(pages, PAGE, width)
-        slots = jnp.where(live, slots, slots[:, 0:1, :])
-        low = jnp.min(slots, axis=1).astype(BF16)
-        high = jnp.max(slots, axis=1).astype(BF16)
         query = queries_of(blocks, r, heads)
-        dims = (((1,), (1,)), ((), ()))
         bound = lax.dot_general(
-            jnp.maximum(query, 0.0).astype(BF16), high, dims, preferred_element_type=F32
+            jnp.maximum(query, 0.0).astype(BF16),
+            high_ref[r].astype(BF16),
+            dims,
+            preferred_element_type=F32,
         ) + lax.dot_general(
-            jnp.minimum(query, 0.0).astype(BF16), low, dims, preferred_element_type=F32
+            jnp.minimum(query, 0.0).astype(BF16),
+            low_ref[r].astype(BF16),
+            dims,
+            preferred_element_type=F32,
         )
         bound = bound * scale
         best = jnp.full((groups, pages), NEG, F32)
@@ -225,14 +283,25 @@
     half = seq_count // 2
     slots = jnp.swapaxes(cache, 1, 2)
 
+    q_nope, q_rope, w_uk, w_uv, slots, lengths, selected = (
+        pltpu.with_memory_space_constraint(x, pltpu.HBM)
+        for x in (q_nope, q_rope, w_uk, w_uv, slots, lengths, selected)
+    )
+
     def swap(x, k):
         return lax.ppermute(x, "seq", [(i, i ^ k) for i in range(seq_count)])
 
     mine = pl.pallas_call(
         absorb_kernel,
         out_shape=jax.ShapeDtypeStruct((rows, width), BF16),
-        in_specs=[VMEM] * 3,
+        in_specs=[HBM] * 3,
         out_specs=VMEM,
+        scratch_shapes=[
+            pltpu.VMEM(q_nope.shape, BF16),
+            pltpu.VMEM(q_rope.shape, BF16),
+            pltpu.VMEM(w_uk.shape, BF16),
+            pltpu.SemaphoreType.DMA((heads + 2,)),
+        ],
         compiler_params=params(),
         name="absorb",
     )(q_nope, q_rope, w_uk)
@@ -244,6 +313,26 @@
         block[k + 1] = swap(block[k], 1)
     blocks = [block[k] for k in offsets]
 
+    keys, w_value, mask, low, high = pl.pallas_call(
+        stage_kernel,
+        out_shape=(
+            jax.ShapeDtypeStruct(slots.shape, BF16),
+            jax.ShapeDtypeStruct(w_uv.shape, BF16),
+            jax.ShapeDtypeStruct((requests * groups, tokens), F32),
+            jax.ShapeDtypeStruct((requests, pages, width), F32),
+            jax.ShapeDtypeStruct((requests, pages, width), F32),
+        ),
+        in_specs=[HBM] * 4 + [ANY],
+        out_specs=(VMEM,) * 5,
+        scratch_shapes=[
+            pltpu.VMEM(selected.shape, jnp.int32),
+            pltpu.SMEM(lengths.shape, jnp.int32),
+            pltpu.SemaphoreType.DMA((3 + requests,)),
+        ],
+        compiler_params=params(),
+        name="stage_cache",
+    )(slots, w_uv, selected, lengths, block[far[-1]])
+
     send, keep, sums = pl.pallas_call(
         functools.partial(attend_kernel, scale, heads, offsets, latent),
         out_shape=(
@@ -251,22 +340,21 @@
             jax.ShapeDtypeStruct((half, rows, latent), F32),
             jax.ShapeDtypeStruct((half, rows, LANES), F32),
         ),
-        in_specs=[VMEM] * (seq_count + 2) + [SMEM],
+        in_specs=[VMEM] * (seq_count + 2),
         out_specs=(VMEM,) * 3,
-        scratch_shapes=[pltpu.VMEM((requests * groups, tokens), F32)],
         compiler_params=params(),
         name="attend",
-    )(*blocks, slots, selected, lengths)
+    )(*blocks, keys, mask)
     got = swap(send, 1)
 
     bounds = pl.pallas_call(
         functools.partial(bounds_kernel, scale, heads, offsets),
         out_shape=jax.ShapeDtypeStruct((requests, groups, pages), F32),
-        in_specs=[VMEM] * (seq_count + 1) + [SMEM],
+        in_specs=[VMEM] * (seq_count + 2) + [ANY],
         out_specs=VMEM,
         compiler_params=params(),
         name="page_bounds",
-    )(*blocks, slots, lengths)
+    )(*blocks, low, high, sums)
     others = lax.ppermute(
         bounds, "head", [(i, (i + 1) % head_count) for i in range(head_count)]
     )
@@ -279,24 +367,32 @@
             jax.ShapeDtypeStruct((rows, LANES), F32),
         )
         + (shape,) * (half - 1),
-        in_specs=[VMEM] * 3,
+        in_specs=[VMEM] * 3 + [ANY],
         out_specs=(VMEM,) * (half + 1),
         compiler_params=params(),
         name="merge_pair",
-    )(got, keep, sums)
+    )(got, keep, sums, others)
     gots = {k: swap(sends[k // 2 - 1], k) for k in far}
 
-    return pl.pallas_call(
+    largest = pl.pallas_call(
+        largest_kernel,
+        out_shape=jax.ShapeDtypeStruct((requests, groups, pages), F32),
+        in_specs=[VMEM] * 2 + [HBM, ANY],
+        out_specs=VMEM,
+        scratch_shapes=[pltpu.SMEM(lengths.shape, jnp.int32), pltpu.SemaphoreType.DMA(())],
+        compiler_params=params(),
+        name="group_bounds",
+    )(bounds, others, lengths, own_sum)
+
+    attended = pl.pallas_call(
         functools.partial(value_kernel, latent, heads),
-        out_shape=(
-            jax.ShapeDtypeStruct((requests, heads, w_uv.shape[2]), BF16),
-            jax.ShapeDtypeStruct((requests, groups, pages), F32),
-        ),
-        in_specs=[VMEM] * 5 + [SMEM] + [VMEM] * (half - 1),
-        out_specs=(VMEM, VMEM),
+        out_shape=jax.ShapeDtypeStruct((requests, heads, w_uv.shape[2]), BF16),
+        in_specs=[VMEM] * (half + 2),
+        out_specs=VMEM,
         compiler_params=params(),
         name="merge_and_value",
-    )(own, own_sum, w_uv, bounds, others, lengths, *[gots[k] for k in far])
+    )(own, own_sum, w_value, *[gots[k] for k in far])
+    return attended, largest
 
 
 def solution(mesh):

time: 40.1 us -> 33.2 us (0.83)
  local copies, waits for them, and re-layouts: 5.65 us -> 0 us
  waiting for transfers between devices: 10.5 us -> 6.95 us
  Pallas kernels: 6.84 us -> 8.86 us
    unnamed x16 -> x0, local copies, waits for them, and re-layouts: 5.65 us -> none
    pallas_call x0 -> x2, Pallas kernels: none -> 4.05 us  [the longest x1 2.76 us: local(): pl.pallas_call(stage_kernel, out_shape=(jax.ShapeDtypeStruct(slots.shape,...]
    ppermute x11, waiting for transfers between devices: 9.34 us -> 5.78 us  [swap(): return lax.ppermute(x, 'seq', [(i, i ^ k) for i in range(seq_count)])]
    pallas_call x1, Pallas kernels: 2.45 us -> 0.33 us  [local(): pl.pallas_call(functools.partial(bounds_kernel, scale, heads, offsets), o...]
    pallas_call x1, Pallas kernels: 0.27 us -> 1.46 us  [local(): pl.pallas_call(absorb_kernel, out_shape=jax.ShapeDtypeStruct((rows, width...]
    pallas_call x1, Pallas kernels: 1.57 us -> 1.02 us  [local(): pl.pallas_call(functools.partial(value_kernel, latent, heads), out_shape=...]
    pallas_call x1, Pallas kernels: 2.33 us -> 1.78 us  [local(): pl.pallas_call(functools.partial(attend_kernel, scale, heads, offsets, la...]
  transfers between devices with their start and end apart: 12 -> 12, of which waited for: 5 -> 6; matrix products, arithmetic and copies ran while one was open for 0% -> 0% of each run, Pallas kernels for 6% -> 13%
where the time goes in v2:
time: 33.2 us; the launch traced here: 32.9 us
  starting transfers between devices  16.4 us (49%)
  Pallas kernels  8.86 us (27%)
  waiting for transfers between devices  6.95 us (21%)
  between operations  0.71 us (2%)
    ppermute x11, starting transfers between devices, swap(): return lax.ppermute(x, 'seq', [(i, i ^ k) for i in range(seq_count)])  16.3 us
    ppermute x11, waiting for transfers between devices, swap(): return lax.ppermute(x, 'seq', [(i, i ^ k) for i in range(seq_count)])  5.78 us
    pallas_call x1, Pallas kernels, local(): pl.pallas_call(stage_kernel, out_shape=(jax.ShapeDtypeStruct(slots.shape,...  2.76 us
    pallas_call x1, Pallas kernels, local(): pl.pallas_call(functools.partial(attend_kernel, scale, heads, offsets, la...  1.78 us
    pallas_call x1, Pallas kernels, local(): pl.pallas_call(absorb_kernel, out_shape=jax.ShapeDtypeStruct((rows, width...  1.46 us
    pallas_call x1, Pallas kernels, local(): pl.pallas_call(largest_kernel, out_shape=jax.ShapeDtypeStruct((requests,...  1.29 us
    ppermute x1, waiting for transfers between devices, local(): lax.ppermute(bounds, 'head', [(i, (i + 1) % head_count) for i in range(he...  1.17 us
    pallas_call x1, Pallas kernels, local(): pl.pallas_call(functools.partial(value_kernel, latent, heads), out_shape=...  1.02 us
  transfers between devices with their start and end apart: 12, of which 6 were waited for; matrix products, arithmetic and copies ran while one was open for 0% of the time, Pallas kernels for 13%

profile of v2, /device:TPU:0, one launch (start us, length us, event | category | flops | bytes accessed | tf_op | source)
XLA Modules:
  0.0 32.9 jit_solution(10042394227972427949)
XLA Ops:
  0.6 1.5 %absorb.1.refs_0_ = bf16[32,576]{1,0:T(8,128)(2,1)S(1)} custom-call(bf16[4,8,128]{2,1,0:T(8,128)(2,1)} %nope_hbm.1, bf16[4,8,64]{2,1,0:T(8,128)(2,1)} %rope_hbm.1, bf16[8,128,512]{2,1,0:T(8,128)(2,1)} %w_hbm.2), custom_call_target="tpu_custom_call" | custom-call | tf_op jit(solution)/shard_map/absorb/pallas_call | solution.py:294
  2.1 5.1 %collective-permute-start.5 = (bf16[32,576]{1,0:T(8,128)(2,1)S(1)}, bf16[32,576]{1,0:T(8,128)(2,1)S(1)}, u32[]{:S(2)}, u32[]{:S(2)}) collective-permute-start(bf16[32,576]{1,0:T(8,128)(2,1)S(1)} %absorb.1.refs_0_), channel_id=1, source_target_pairs={{0,12},{2,14},{4,8},{6,10},{8,4},{10,6},{12,0},{14,2},{1,13},{3,15... | collective-permute-start | bytes 110600 | tf_op jit(solution)/shard_map/ppermute | solution.py:292
  7.2 0.0 collective-permute-start.3
  7.2 0.6 %collective-permute-start.1 = (bf16[32,576]{1,0:T(8,128)(2,1)S(1)}, bf16[32,576]{1,0:T(8,128)(2,1)S(1)}, u32[]{:S(2)}, u32[]{:S(2)}) collective-permute-start(bf16[32,576]{1,0:T(8,128)(2,1)S(1)} %absorb.1.refs_0_), channel_id=1, source_target_pairs={{0,4},{2,6},{4,0},{6,2},{8,12},{10,14},{12,8},{14,10},{1,5},{3,7},... | collective-permute-start | bytes 110600 | tf_op jit(solution)/shard_map/ppermute | solution.py:292
  7.9 1.7 %collective-permute-start = (bf16[32,576]{1,0:T(8,128)(2,1)S(1)}, bf16[32,576]{1,0:T(8,128)(2,1)S(1)}, u32[]{:S(2)}, u32[]{:S(2)}) collective-permute-start(bf16[32,576]{1,0:T(8,128)(2,1)S(1)} %absorb.1.refs_0_), channel_id=1, source_target_pairs={{0,2},{2,0},{4,6},{6,4},{8,10},{10,8},{12,14},{14,12},{1,3},{3,1},... | collective-permute-start | bytes 110600 | tf_op jit(solution)/shard_map/ppermute | solution.py:292
  9.5 0.0 collective-permute-done.5.refs_6_
  9.5 1.6 %collective-permute-start.6 = (bf16[32,576]{1,0:T(8,128)(2,1)S(1)}, bf16[32,576]{1,0:T(8,128)(2,1)S(1)}, u32[]{:S(2)}, u32[]{:S(2)}) collective-permute-start(bf16[32,576]{1,0:T(8,128)(2,1)S(1)} %collective-permute-done.5.refs_6_), channel_id=1, source_target_pairs={{0,2},{2,0},{4,6},{6,4},{8,10},{10,8},{12,14},{14,12},{1,3},{3,1},... | collective-permute-start | bytes 110600 | tf_op jit(solution)/shard_map/ppermute | solution.py:292
  11.1 1.0 %collective-permute-done.3.refs_4_ = bf16[32,576]{1,0:T(8,128)(2,1)S(1)} collective-permute-done((bf16[32,576]{1,0:T(8,128)(2,1)S(1)}, bf16[32,576]{1,0:T(8,128)(2,1)S(1)}, u32[]{:S(2)}, u32[]{:S(2)}) %collective-permute-start.3) | collective-permute-done | bytes 36896 | tf_op jit(solution)/shard_map/ppermute | solution.py:292
  12.1 1.5 %collective-permute-start.4 = (bf16[32,576]{1,0:T(8,128)(2,1)S(1)}, bf16[32,576]{1,0:T(8,128)(2,1)S(1)}, u32[]{:S(2)}, u32[]{:S(2)}) collective-permute-start(bf16[32,576]{1,0:T(8,128)(2,1)S(1)} %collective-permute-done.3.refs_4_), channel_id=1, source_target_pairs={{0,2},{2,0},{4,6},{6,4},{8,10},{10,8},{12,14},{14,12},{1,3},{3,1},... | collective-permute-start | bytes 110600 | tf_op jit(solution)/shard_map/ppermute | solution.py:292
  13.6 0.0 collective-permute-done.1.after_ref.refs_2_
  13.6 0.5 %collective-permute-start.2 = (bf16[32,576]{1,0:T(8,128)(2,1)S(1)}, bf16[32,576]{1,0:T(8,128)(2,1)S(1)}, u32[]{:S(2)}, u32[]{:S(2)}) collective-permute-start(bf16[32,576]{1,0:T(8,128)(2,1)S(1)} %collective-permute-done.1.after_ref.refs_2_), channel_id=1, source_target_pairs={{0,2},{2,0},{4,6},{6,4},{8,10},{10,8},{12,14},{14,12},{1,3},{3,1},... | collective-permute-start | bytes 110600 | tf_op jit(solution)/shard_map/ppermute | solution.py:292
  14.1 2.8 %stage_cache.1 = (bf16[4,576,512]{2,1,0:T(8,128)(2,1)S(1)}, bf16[8,512,128]{2,1,0:T(8,128)(2,1)S(1)}, f32[32,512]{1,0:T(8,128)S(1)}, f32[4,8,576]{2,1,0:T(8,128)S(1)}, f32[4,8,576]{2,1,0:T(8,128)S(1)}) custom-call(bf16[4,576,512]{2,1,0:T(8,128)(2,1)} %bitcast.1, bf16[8,512,128]{2,1,0:T(8,128)(2,1)} %w_hbm.3, s32[4,8,32]{2,1,0:T(8,128)} %selected_hbm.1, ...), custom_call_target="tpu_custom_call" | custom-call | tf_op jit(solution)/shard_map/stage_cache/pallas_call | solution.py:316
  16.9 0.0 collective-permute-done.refs_1_
  16.9 0.0 collective-permute-done.6.refs_7_
  16.9 0.0 collective-permute-done.4.refs_5_
  16.9 0.7 %collective-permute-done.2.refs_3_ = bf16[32,576]{1,0:T(8,128)(2,1)S(1)} collective-permute-done((bf16[32,576]{1,0:T(8,128)(2,1)S(1)}, bf16[32,576]{1,0:T(8,128)(2,1)S(1)}, u32[]{:S(2)}, u32[]{:S(2)}) %collective-permute-start.2) | collective-permute-done | bytes 36896 | tf_op jit(solution)/shard_map/ppermute | solution.py:292
  17.6 1.8 %attend.1 = (bf16[4,32,640]{2,1,0:T(8,128)(2,1)S(1)}, f32[4,32,512]{2,1,0:T(8,128)S(1)}, f32[4,32,128]{2,1,0:T(8,128)S(1)}) custom-call(bf16[32,576]{1,0:T(8,128)(2,1)S(1)} %absorb.1.refs_0_, bf16[32,576]{1,0:T(8,128)(2,1)S(1)} %collective-permute-done.refs_1_, bf16[32,576]{1,0:T(8,128)(2,1)S(1)} %collective-permute-done.1.after_ref.refs_2_, ...), custom_call_target="tpu_custom_call" | custom-call | tf_op jit(solution)/shard_map/attend/pallas_call | solution.py:336
  19.4 0.9 %collective-permute-start.7 = (bf16[4,32,640]{2,1,0:T(8,128)(2,1)S(1)}, bf16[4,32,640]{2,1,0:T(8,128)(2,1)S(1)}, u32[]{:S(2)}, u32[]{:S(2)}) collective-permute-start(bf16[4,32,640]{2,1,0:T(8,128)(2,1)S(1)} %get-tuple-element.17), channel_id=1, source_target_pairs={{0,2},{2,0},{4,6},{6,4},{8,10},{10,8},{12,14},{14,12},{1,3},{3,1},... | collective-permute-start | bytes 491528 | tf_op jit(solution)/shard_map/ppermute | solution.py:292
  20.3 0.3 page_bounds.1.mine_ref
  20.6 0.1 collective-permute-start.8
  20.7 1.2 %collective-permute-done.8.after_ref.other_ref = f32[4,8,8]{2,1,0:T(8,128)S(1)} collective-permute-done((f32[4,8,8]{2,1,0:T(8,128)S(1)}, f32[4,8,8]{2,1,0:T(8,128)S(1)}, u32[]{:S(2)}, u32[]{:S(2)}) %collective-permute-start.8) | collective-permute-done | bytes 1056 | tf_op jit(solution)/shard_map/ppermute | solution.py:358
  21.9 2.9 %collective-permute-done.7.got_ref = bf16[4,32,640]{2,1,0:T(8,128)(2,1)S(1)} collective-permute-done((bf16[4,32,640]{2,1,0:T(8,128)(2,1)S(1)}, bf16[4,32,640]{2,1,0:T(8,128)(2,1)S(1)}, u32[]{:S(2)}, u32[]{:S(2)}) %collective-permute-start.7) | collective-permute-done | bytes 163872 | tf_op jit(solution)/shard_map/ppermute | solution.py:292
  24.8 0.2 merge_pair.1
  25.0 2.0 %collective-permute-start.9 = (bf16[32,640]{1,0:T(8,128)(2,1)S(1)}, bf16[32,640]{1,0:T(8,128)(2,1)S(1)}, u32[]{:S(2)}, u32[]{:S(2)}) collective-permute-start(bf16[32,640]{1,0:T(8,128)(2,1)S(1)} %get-tuple-element.25), channel_id=1, source_target_pairs={{0,12},{2,14},{4,8},{6,10},{8,4},{10,6},{12,0},{14,2},{1,13},{3,15... | collective-permute-start | bytes 122888 | tf_op jit(solution)/shard_map/ppermute | solution.py:292
  27.0 0.0 collective-permute-start.10
  27.0 2.5 %collective-permute-start.11 = (bf16[32,640]{1,0:T(8,128)(2,1)S(1)}, bf16[32,640]{1,0:T(8,128)(2,1)S(1)}, u32[]{:S(2)}, u32[]{:S(2)}) collective-permute-start(bf16[32,640]{1,0:T(8,128)(2,1)S(1)} %get-tuple-element.27), channel_id=1, source_target_pairs={{0,4},{2,6},{4,0},{6,2},{8,12},{10,14},{12,8},{14,10},{1,5},{3,7},... | collective-permute-start | bytes 122888 | tf_op jit(solution)/shard_map/ppermute | solution.py:292
  29.5 1.3 %group_bounds.1 = f32[4,8,8]{2,1,0:T(8,128)} custom-call(f32[4,8,8]{2,1,0:T(8,128)S(1)} %page_bounds.1.mine_ref, f32[4,8,8]{2,1,0:T(8,128)S(1)} %collective-permute-done.8.after_ref.other_ref, s32[4]{0:T(128)} %lengths_hbm.3, f32[32,128]{1,0:T(8,128)S(1)} %get-tuple-element.23.own_sum_ref.after_ref), custom_call_target="tpu_custom_call" | custom-call | tf_op jit(solution)/shard_map/group_bounds/pallas_call | solution.py:377
  30.8 0.1 collective-permute-done.9.refs_0_
  30.9 1.0 %collective-permute-done.10.refs_1_ = bf16[32,640]{1,0:T(8,128)(2,1)S(1)} collective-permute-done((bf16[32,640]{1,0:T(8,128)(2,1)S(1)}, bf16[32,640]{1,0:T(8,128)(2,1)S(1)}, u32[]{:S(2)}, u32[]{:S(2)}) %collective-permute-start.10) | collective-permute-done | bytes 40992 | tf_op jit(solution)/shard_map/ppermute | solution.py:292
  31.9 0.0 collective-permute-done.11.refs_2_
  31.9 1.0 %merge_and_value.1 = bf16[4,8,128]{2,1,0:T(8,128)(2,1)} custom-call(f32[32,512]{1,0:T(8,128)S(1)} %get-tuple-element.22.own_ref, f32[32,128]{1,0:T(8,128)S(1)} %get-tuple-element.23.own_sum_ref.after_ref, bf16[8,512,128]{2,1,0:T(8,128)(2,1)S(1)} %get-tuple-element.24.w_ref, bf16[32,640]{1,0:T(8,128)(2,1)S(1)} %collective-permute-done.9.refs_0_, ...), custom_call_target="tpu_custom_call" | custom-call | tf_op jit(solution)/shard_map/merge_and_value/pallas_call | solution.py:387
Async XLA Ops:
  2.1 7.4 %collective-permute-start.5 = (bf16[32,576]{1,0:T(8,128)(2,1)S(1)}, bf16[32,576]{1,0:T(8,128)(2,1)S(1)}, u32[]{:S(2)}, u32[]{:S(2)}) collective-permute-start(bf16[32,576]{1,0:T(8,128)(2,1)S(1)} %absorb.1.refs_0_), channel_id=1, source_target_pairs={{0,12},{2,14},{4,8},{6,10},{8,4},{10,6},{12,0},{14,2},{1,13},{3,15... | collective-permute-start | bytes 110600 | tf_op jit(solution)/shard_map/ppermute | solution.py:292
  7.2 4.9 %collective-permute-start.3 = (bf16[32,576]{1,0:T(8,128)(2,1)S(1)}, bf16[32,576]{1,0:T(8,128)(2,1)S(1)}, u32[]{:S(2)}, u32[]{:S(2)}) collective-permute-start(bf16[32,576]{1,0:T(8,128)(2,1)S(1)} %absorb.1.refs_0_), channel_id=1, source_target_pairs={{0,8},{2,10},{4,12},{6,14},{8,0},{10,2},{12,4},{14,6},{1,9},{3,11}... | collective-permute-start | bytes 110600 | tf_op jit(solution)/shard_map/ppermute | solution.py:292
  7.2 6.4 %collective-permute-start.1 = (bf16[32,576]{1,0:T(8,128)(2,1)S(1)}, bf16[32,576]{1,0:T(8,128)(2,1)S(1)}, u32[]{:S(2)}, u32[]{:S(2)}) collective-permute-start(bf16[32,576]{1,0:T(8,128)(2,1)S(1)} %absorb.1.refs_0_), channel_id=1, source_target_pairs={{0,4},{2,6},{4,0},{6,2},{8,12},{10,14},{12,8},{14,10},{1,5},{3,7},... | collective-permute-start | bytes 110600 | tf_op jit(solution)/shard_map/ppermute | solution.py:292
  7.9 9.1 %collective-permute-start = (bf16[32,576]{1,0:T(8,128)(2,1)S(1)}, bf16[32,576]{1,0:T(8,128)(2,1)S(1)}, u32[]{:S(2)}, u32[]{:S(2)}) collective-permute-start(bf16[32,576]{1,0:T(8,128)(2,1)S(1)} %absorb.1.refs_0_), channel_id=1, source_target_pairs={{0,2},{2,0},{4,6},{6,4},{8,10},{10,8},{12,14},{14,12},{1,3},{3,1},... | collective-permute-start | bytes 110600 | tf_op jit(solution)/shard_map/ppermute | solution.py:292
  9.5 7.4 %collective-permute-start.6 = (bf16[32,576]{1,0:T(8,128)(2,1)S(1)}, bf16[32,576]{1,0:T(8,128)(2,1)S(1)}, u32[]{:S(2)}, u32[]{:S(2)}) collective-permute-start(bf16[32,576]{1,0:T(8,128)(2,1)S(1)} %collective-permute-done.5.refs_6_), channel_id=1, source_target_pairs={{0,2},{2,0},{4,6},{6,4},{8,10},{10,8},{12,14},{14,12},{1,3},{3,1},... | collective-permute-start | bytes 110600 | tf_op jit(solution)/shard_map/ppermute | solution.py:292
  12.1 4.8 %collective-permute-start.4 = (bf16[32,576]{1,0:T(8,128)(2,1)S(1)}, bf16[32,576]{1,0:T(8,128)(2,1)S(1)}, u32[]{:S(2)}, u32[]{:S(2)}) collective-permute-start(bf16[32,576]{1,0:T(8,128)(2,1)S(1)} %collective-permute-done.3.refs_4_), channel_id=1, source_target_pairs={{0,2},{2,0},{4,6},{6,4},{8,10},{10,8},{12,14},{14,12},{1,3},{3,1},... | collective-permute-start | bytes 110600 | tf_op jit(solution)/shard_map/ppermute | solution.py:292
  13.6 4.0 %collective-permute-start.2 = (bf16[32,576]{1,0:T(8,128)(2,1)S(1)}, bf16[32,576]{1,0:T(8,128)(2,1)S(1)}, u32[]{:S(2)}, u32[]{:S(2)}) collective-permute-start(bf16[32,576]{1,0:T(8,128)(2,1)S(1)} %collective-permute-done.1.after_ref.refs_2_), channel_id=1, source_target_pairs={{0,2},{2,0},{4,6},{6,4},{8,10},{10,8},{12,14},{14,12},{1,3},{3,1},... | collective-permute-start | bytes 110600 | tf_op jit(solution)/shard_map/ppermute | solution.py:292
  19.4 5.4 %collective-permute-start.7 = (bf16[4,32,640]{2,1,0:T(8,128)(2,1)S(1)}, bf16[4,32,640]{2,1,0:T(8,128)(2,1)S(1)}, u32[]{:S(2)}, u32[]{:S(2)}) collective-permute-start(bf16[4,32,640]{2,1,0:T(8,128)(2,1)S(1)} %get-tuple-element.17), channel_id=1, source_target_pairs={{0,2},{2,0},{4,6},{6,4},{8,10},{10,8},{12,14},{14,12},{1,3},{3,1},... | collective-permute-start | bytes 491528 | tf_op jit(solution)/shard_map/ppermute | solution.py:292
  20.6 1.2 %collective-permute-start.8 = (f32[4,8,8]{2,1,0:T(8,128)S(1)}, f32[4,8,8]{2,1,0:T(8,128)S(1)}, u32[]{:S(2)}, u32[]{:S(2)}) collective-permute-start(f32[4,8,8]{2,1,0:T(8,128)S(1)} %page_bounds.1.mine_ref), channel_id=1, source_target_pairs={{0,1},{1,0},{2,3},{3,2},{4,5},{5,4},{6,7},{7,6},{8,9},{9,8},{10,11... | collective-permute-start | bytes 3080 | tf_op jit(solution)/shard_map/ppermute | solution.py:358
  25.0 5.9 %collective-permute-start.9 = (bf16[32,640]{1,0:T(8,128)(2,1)S(1)}, bf16[32,640]{1,0:T(8,128)(2,1)S(1)}, u32[]{:S(2)}, u32[]{:S(2)}) collective-permute-start(bf16[32,640]{1,0:T(8,128)(2,1)S(1)} %get-tuple-element.25), channel_id=1, source_target_pairs={{0,12},{2,14},{4,8},{6,10},{8,4},{10,6},{12,0},{14,2},{1,13},{3,15... | collective-permute-start | bytes 122888 | tf_op jit(solution)/shard_map/ppermute | solution.py:292
  27.0 4.9 %collective-permute-start.10 = (bf16[32,640]{1,0:T(8,128)(2,1)S(1)}, bf16[32,640]{1,0:T(8,128)(2,1)S(1)}, u32[]{:S(2)}, u32[]{:S(2)}) collective-permute-start(bf16[32,640]{1,0:T(8,128)(2,1)S(1)} %get-tuple-element.26), channel_id=1, source_target_pairs={{0,8},{2,10},{4,12},{6,14},{8,0},{10,2},{12,4},{14,6},{1,9},{3,11}... | collective-permute-start | bytes 122888 | tf_op jit(solution)/shard_map/ppermute | solution.py:292
  27.0 4.9 %collective-permute-start.11 = (bf16[32,640]{1,0:T(8,128)(2,1)S(1)}, bf16[32,640]{1,0:T(8,128)(2,1)S(1)}, u32[]{:S(2)}, u32[]{:S(2)}) collective-permute-start(bf16[32,640]{1,0:T(8,128)(2,1)S(1)} %get-tuple-element.27), channel_id=1, source_target_pairs={{0,4},{2,6},{4,0},{6,2},{8,12},{10,14},{12,8},{14,10},{1,5},{3,7},... | collective-permute-start | bytes 122888 | tf_op jit(solution)/shard_map/ppermute | solution.py:292

commit v3 on v2

--- a/solution.py
+++ b/solution.py
@@ -59,7 +59,7 @@
 
 def stage_kernel(
     cache_hbm, w_hbm, selected_hbm, lengths_hbm, after_ref,
-    cache_ref, w_ref, mask_ref, low_ref, high_ref, selected_ref, lengths_ref, sems,
+    cache_ref, w_ref, mask_ref, low_ref, high_ref, live_ref, selected_ref, lengths_ref, sems,
 ):
     requests, groups, picks = selected_ref.shape
     width, tokens = cache_ref.shape[1:]
@@ -91,8 +91,10 @@
         picked = jnp.bitwise_and(jnp.right_shift(word, lane // PAGE), 1) == 1
         live = lane + rank * tokens < lengths_ref[r]
         mask_ref[r * groups : (r + 1) * groups, :] = jnp.where(picked & live, 1.0, 0.0)
+    first = (rank * pages + lax.broadcasted_iota(jnp.int32, (groups, pages), 1)) * PAGE
     row = lax.broadcasted_iota(jnp.int32, (tokens, width), 0) + rank * tokens
     for r in range(requests):
+        live_ref[r] = jnp.where(first < lengths_ref[r], 1.0, 0.0)
         copies[2 + r].wait()
         slots = cache_ref[r].astype(F32).T
         live = row < lengths_ref[r]
@@ -115,15 +117,20 @@
     return jnp.concatenate([b[rows] for b in blocks], axis=0)
 
 
+def crossings(offset):
+    return (1 if offset >> 1 else 0) + (offset & 1)
+
+
 def group_of(offset, heads):
     source = jnp.bitwise_xor(lax.axis_index("seq"), offset)
-    return (source * lax.axis_size("head") + lax.axis_index("head")) * heads // GH
+    core = jnp.bitwise_xor(lax.axis_index("head"), crossings(offset) & 1)
+    return (source * lax.axis_size("head") + core) * heads // GH
 
 
 def attend_kernel(scale, heads, offsets, latent, *refs):
     count = len(offsets)
     block_refs = refs[:count]
-    cache_ref, mask_ref, send_ref, keep_ref, sum_ref = refs[count:]
+    cache_ref, mask_ref, *out_refs = refs[count:]
     requests, _, tokens = cache_ref.shape
     groups = mask_ref.shape[0] // requests
     blocks = [b[...].astype(F32) for b in block_refs]
@@ -156,24 +163,29 @@
         rows = slice(i * heads, (i + 1) * heads)
         out = jnp.concatenate([o[rows] for o in outs], axis=0)
         lse = jnp.concatenate([s[rows] for s in sums], axis=0)
-        lse = jnp.broadcast_to(lse, (lse.shape[0], LANES))
-        if k % 2:
-            send_ref[k // 2, :, :latent] = out.astype(BF16)
-            send_ref[k // 2, :, latent:] = packed(lse)
-        else:
-            keep_ref[k // 2] = out
-            sum_ref[k // 2] = lse
+        fill(out_refs[i], out, lse)
+
+
+def fill(ref, out, lse):
+    latent = out.shape[1]
+    lse = jnp.broadcast_to(lse, (lse.shape[0], LANES))
+    ref[:, :latent] = out.astype(ref.dtype)
+    ref[:, latent:] = packed(lse) if ref.dtype == BF16 else lse
+
+
+def read(ref, latent):
+    tail = ref[:, latent:].astype(F32)
+    if ref.dtype == BF16:
+        lse = tail[:, 0:1] + tail[:, 1:2] + tail[:, 2:3]
+    else:
+        lse = tail[:, 0:1]
+    return ref[:, :latent].astype(F32), lse
 
 
 def packed(lse):
     lane = lax.broadcasted_iota(jnp.int32, lse.shape, 1)
     high, middle, low = (p.astype(F32) for p in split3(lse))
     return jnp.where(lane == 0, high, jnp.where(lane == 1, middle, low)).astype(BF16)
-
-
-def unpacked(tail):
-    tail = tail.astype(F32)
-    return tail[:, 0:1] + tail[:, 1:2] + tail[:, 2:3]
 
 
 def merge(parts):
@@ -184,31 +196,13 @@
     return mixed / total, top + jnp.log(total)
 
 
-def pair_kernel(latent, got_ref, keep_ref, sum_ref, after_ref, own_ref, own_sum_ref, *send_refs):
-    for i in range(got_ref.shape[0]):
-        got = got_ref[i]
-        out, lse = merge(
-            [
-                (got[:, :latent].astype(F32), unpacked(got[:, latent:])),
-                (keep_ref[i], sum_ref[i][:, 0:1]),
-            ]
-        )
-        lse = jnp.broadcast_to(lse, (lse.shape[0], LANES))
-        if i == 0:
-            own_ref[...] = out
-            own_sum_ref[...] = lse
-        else:
-            send_refs[i - 1][:, :latent] = out.astype(BF16)
-            send_refs[i - 1][:, latent:] = packed(lse)
-
-
-def value_kernel(latent, heads, own_ref, own_sum_ref, w_ref, *refs):
-    got_refs, out_ref = refs[:-1], refs[-1]
-    parts = [(own_ref[...], own_sum_ref[...][:, 0:1])]
-    for got_ref in got_refs:
-        got = got_ref[...]
-        parts.append((got[:, :latent].astype(F32), unpacked(got[:, latent:])))
-    mixed = merge(parts)[0].astype(BF16)
+def pair_kernel(latent, got_ref, keep_ref, out_ref):
+    fill(out_ref, *merge([read(got_ref, latent), read(keep_ref, latent)]))
+
+
+def value_kernel(latent, heads, w_ref, *refs):
+    part_refs, out_ref = refs[:-1], refs[-1]
+    mixed = merge([read(ref, latent) for ref in part_refs])[0].astype(BF16)
     size = w_ref.shape[2]
     head = lax.broadcasted_iota(jnp.int32, (mixed.shape[0], size), 0) % heads
     out = jnp.zeros((mixed.shape[0], size), F32)
@@ -221,20 +215,10 @@
     out_ref[...] = out.reshape(out_ref.shape).astype(BF16)
 
 
-def largest_kernel(
-    mine_ref, other_ref, lengths_hbm, after_ref, bounds_ref, lengths_ref, sem
-):
-    requests, groups, pages = bounds_ref.shape
-    copy = pltpu.make_async_copy(lengths_hbm, lengths_ref, sem)
-    copy.start()
-    copy.wait()
-    first = (
-        lax.axis_index("seq") * pages + lax.broadcasted_iota(jnp.int32, (groups, pages), 1)
-    ) * PAGE
-    for r in range(requests):
-        bounds_ref[r] = jnp.where(
-            first < lengths_ref[r], jnp.maximum(mine_ref[r], other_ref[r]), 0.0
-        )
+def largest_kernel(mine_ref, other_ref, live_ref, bounds_ref):
+    bounds_ref[...] = jnp.where(
+        live_ref[...] > 0.5, jnp.maximum(mine_ref[...], other_ref[...]), 0.0
+    )
 
 
 def bounds_kernel(scale, heads, offsets, *refs):
@@ -289,7 +273,12 @@
     )
 
     def swap(x, k):
-        return lax.ppermute(x, "seq", [(i, i ^ k) for i in range(seq_count)])
+        pairs = [
+            (i * head_count + c, (i ^ k) * head_count + (c ^ 1))
+            for i in range(seq_count)
+            for c in range(head_count)
+        ]
+        return lax.ppermute(x, ("seq", "head"), pairs)
 
     mine = pl.pallas_call(
         absorb_kernel,
@@ -313,7 +302,7 @@
         block[k + 1] = swap(block[k], 1)
     blocks = [block[k] for k in offsets]
 
-    keys, w_value, mask, low, high = pl.pallas_call(
+    keys, w_value, mask, low, high, live = pl.pallas_call(
         stage_kernel,
         out_shape=(
             jax.ShapeDtypeStruct(slots.shape, BF16),
@@ -321,9 +310,10 @@
             jax.ShapeDtypeStruct((requests * groups, tokens), F32),
             jax.ShapeDtypeStruct((requests, pages, width), F32),
             jax.ShapeDtypeStruct((requests, pages, width), F32),
+            jax.ShapeDtypeStruct((requests, groups, pages), F32),
         ),
         in_specs=[HBM] * 4 + [ANY],
-        out_specs=(VMEM,) * 5,
+        out_specs=(VMEM,) * 6,
         scratch_shapes=[
             pltpu.VMEM(selected.shape, jnp.int32),
             pltpu.SMEM(lengths.shape, jnp.int32),
@@ -333,19 +323,30 @@
         name="stage_cache",
     )(slots, w_uv, selected, lengths, block[far[-1]])
 
-    send, keep, sums = pl.pallas_call(
+    parts = pl.pallas_call(
         functools.partial(attend_kernel, scale, heads, offsets, latent),
-        out_shape=(
-            jax.ShapeDtypeStruct((half, rows, latent + LANES), BF16),
-            jax.ShapeDtypeStruct((half, rows, latent), F32),
-            jax.ShapeDtypeStruct((half, rows, LANES), F32),
+        out_shape=tuple(
+            jax.ShapeDtypeStruct((rows, latent + LANES), BF16 if k % 2 else F32) for k in offsets
         ),
         in_specs=[VMEM] * (seq_count + 2),
-        out_specs=(VMEM,) * 3,
+        out_specs=(VMEM,) * seq_count,
         compiler_params=params(),
         name="attend",
     )(*blocks, keys, mask)
-    got = swap(send, 1)
+
+    got = {k: swap(parts[k + 1], 1) for k in far + (0,)}
+    send = {
+        k: pl.pallas_call(
+            functools.partial(pair_kernel, latent),
+            out_shape=jax.ShapeDtypeStruct((rows, latent + LANES), BF16),
+            in_specs=[VMEM] * 2,
+            out_specs=VMEM,
+            compiler_params=params(),
+            name="merge_pair",
+        )(got[k], parts[k])
+        for k in far
+    }
+    arrived = [swap(send[k], k) for k in far]
 
     bounds = pl.pallas_call(
         functools.partial(bounds_kernel, scale, heads, offsets),
@@ -354,35 +355,16 @@
         out_specs=VMEM,
         compiler_params=params(),
         name="page_bounds",
-    )(*blocks, low, high, sums)
-    others = lax.ppermute(
-        bounds, "head", [(i, (i + 1) % head_count) for i in range(head_count)]
-    )
-
-    shape = jax.ShapeDtypeStruct((rows, latent + LANES), BF16)
-    own, own_sum, *sends = pl.pallas_call(
-        functools.partial(pair_kernel, latent),
-        out_shape=(
-            jax.ShapeDtypeStruct((rows, latent), F32),
-            jax.ShapeDtypeStruct((rows, LANES), F32),
-        )
-        + (shape,) * (half - 1),
-        in_specs=[VMEM] * 3 + [ANY],
-        out_specs=(VMEM,) * (half + 1),
-        compiler_params=params(),
-        name="merge_pair",
-    )(got, keep, sums, others)
-    gots = {k: swap(sends[k // 2 - 1], k) for k in far}
-
+    )(*blocks, low, high, send[far[-1]])
+    others = lax.ppermute(bounds, "head", [(i, i ^ 1) for i in range(head_count)])
     largest = pl.pallas_call(
         largest_kernel,
         out_shape=jax.ShapeDtypeStruct((requests, groups, pages), F32),
-        in_specs=[VMEM] * 2 + [HBM, ANY],
+        in_specs=[VMEM] * 3,
         out_specs=VMEM,
-        scratch_shapes=[pltpu.SMEM(lengths.shape, jnp.int32), pltpu.SemaphoreType.DMA(())],
         compiler_params=params(),
         name="group_bounds",
-    )(bounds, others, lengths, own_sum)
+    )(bounds, others, live)
 
     attended = pl.pallas_call(
         functools.partial(value_kernel, latent, heads),
@@ -391,7 +373,7 @@
         out_specs=VMEM,
         compiler_params=params(),
         name="merge_and_value",
-    )(own, own_sum, w_value, *[gots[k] for k in far])
+    )(w_value, parts[0], got[0], *arrived)
     return attended, largest
 
 

time: 33.2 us -> 31.3 us (0.943)
  waiting for transfers between devices: 6.95 us -> 3.59 us
  starting transfers between devices: 16.4 us -> 18.2 us
  Pallas kernels: 8.86 us -> 8.47 us
    ppermute x12 -> x15, waiting for transfers between devices: 6.95 us -> 3.59 us  [the longest x14 2.75 us: swap(): return lax.ppermute(x, ('seq', 'head'), pairs)]
    ppermute x12 -> x15, starting transfers between devices: 16.4 us -> 18.2 us  [the longest x14 17.5 us: swap(): return lax.ppermute(x, ('seq', 'head'), pairs)]
    pallas_call x1, Pallas kernels: 1.29 us -> 0.61 us  [local(): pl.pallas_call(largest_kernel, out_shape=jax.ShapeDtypeStruct((requests,...]
  transfers between devices with their start and end apart: 12 -> 15, of which waited for: 6 -> 6; matrix products, arithmetic and copies ran while one was open for 0% -> 0% of each run, Pallas kernels for 13% -> 14%
where the time goes in v3:
time: 31.3 us; the launch traced here: 30.9 us
  starting transfers between devices  18.2 us (58%)
  Pallas kernels  8.47 us (27%)
  waiting for transfers between devices  3.59 us (11%)
  between operations  0.73 us (2%)
    ppermute x14, starting transfers between devices, swap(): return lax.ppermute(x, ('seq', 'head'), pairs)  17.5 us
    pallas_call x1, Pallas kernels, local(): pl.pallas_call(stage_kernel, out_shape=(jax.ShapeDtypeStruct(slots.shape,...  2.76 us
    ppermute x14, waiting for transfers between devices, swap(): return lax.ppermute(x, ('seq', 'head'), pairs)  2.75 us
    pallas_call x1, Pallas kernels, local(): pl.pallas_call(functools.partial(attend_kernel, scale, heads, offsets, la...  1.78 us
    pallas_call x1, Pallas kernels, local(): pl.pallas_call(absorb_kernel, out_shape=jax.ShapeDtypeStruct((rows, width...  1.46 us
    pallas_call x1, Pallas kernels, local(): pl.pallas_call(functools.partial(value_kernel, latent, heads), out_shape=...  1.02 us
    ppermute x1, waiting for transfers between devices, local(): lax.ppermute(bounds, 'head', [(i, i ^ 1) for i in range(head_count)])  0.84 us
    ppermute x1, starting transfers between devices, local(): lax.ppermute(bounds, 'head', [(i, i ^ 1) for i in range(head_count)])  0.63 us
  transfers between devices with their start and end apart: 15, of which 6 were waited for; matrix products, arithmetic and copies ran while one was open for 0% of the time, Pallas kernels for 14%

profile of v3, /device:TPU:0, one launch (start us, length us, event | category | flops | bytes accessed | tf_op | source)
XLA Modules:
  0.0 30.9 jit_solution(16741097112080993415)
XLA Ops:
  0.6 1.5 %absorb.1.refs_0_ = bf16[32,576]{1,0:T(8,128)(2,1)S(1)} custom-call(bf16[4,8,128]{2,1,0:T(8,128)(2,1)} %nope_hbm.1, bf16[4,8,64]{2,1,0:T(8,128)(2,1)} %rope_hbm.1, bf16[8,128,512]{2,1,0:T(8,128)(2,1)} %w_hbm.2), custom_call_target="tpu_custom_call" | custom-call | tf_op jit(solution)/shard_map/absorb/pallas_call | solution.py:283
  2.1 4.6 %collective-permute-start.5 = (bf16[32,576]{1,0:T(8,128)(2,1)S(1)}, bf16[32,576]{1,0:T(8,128)(2,1)S(1)}, u32[]{:S(2)}, u32[]{:S(2)}) collective-permute-start(bf16[32,576]{1,0:T(8,128)(2,1)S(1)} %absorb.1.refs_0_), channel_id=1, source_target_pairs={{0,13},{1,12},{2,15},{3,14},{4,9},{5,8},{6,11},{7,10},{8,5},{9,4},... | collective-permute-start | bytes 110600 | tf_op jit(solution)/shard_map/ppermute | solution.py:281
  6.7 0.0 collective-permute-start.3
  6.7 0.9 %collective-permute-start = (bf16[32,576]{1,0:T(8,128)(2,1)S(1)}, bf16[32,576]{1,0:T(8,128)(2,1)S(1)}, u32[]{:S(2)}, u32[]{:S(2)}) collective-permute-start(bf16[32,576]{1,0:T(8,128)(2,1)S(1)} %absorb.1.refs_0_), channel_id=1, source_target_pairs={{0,5},{1,4},{2,7},{3,6},{4,1},{5,0},{6,3},{7,2},{8,13},{9,12},{10,... | collective-permute-start | bytes 110600 | tf_op jit(solution)/shard_map/ppermute | solution.py:281
  7.6 1.4 %collective-permute-start.1 = (bf16[32,576]{1,0:T(8,128)(2,1)S(1)}, bf16[32,576]{1,0:T(8,128)(2,1)S(1)}, u32[]{:S(2)}, u32[]{:S(2)}) collective-permute-start(bf16[32,576]{1,0:T(8,128)(2,1)S(1)} %absorb.1.refs_0_), channel_id=1, source_target_pairs={{0,3},{1,2},{2,1},{3,0},{4,7},{5,6},{6,5},{7,4},{8,11},{9,10},{10,... | collective-permute-start | bytes 110600 | tf_op jit(solution)/shard_map/ppermute | solution.py:281
  9.0 0.0 collective-permute-done.5.refs_6_
  9.0 1.4 %collective-permute-start.6 = (bf16[32,576]{1,0:T(8,128)(2,1)S(1)}, bf16[32,576]{1,0:T(8,128)(2,1)S(1)}, u32[]{:S(2)}, u32[]{:S(2)}) collective-permute-start(bf16[32,576]{1,0:T(8,128)(2,1)S(1)} %collective-permute-done.5.refs_6_), channel_id=1, source_target_pairs={{0,3},{1,2},{2,1},{3,0},{4,7},{5,6},{6,5},{7,4},{8,11},{9,10},{10,... | collective-permute-start | bytes 110600 | tf_op jit(solution)/shard_map/ppermute | solution.py:281
  10.3 1.1 %collective-permute-done.3.refs_4_ = bf16[32,576]{1,0:T(8,128)(2,1)S(1)} collective-permute-done((bf16[32,576]{1,0:T(8,128)(2,1)S(1)}, bf16[32,576]{1,0:T(8,128)(2,1)S(1)}, u32[]{:S(2)}, u32[]{:S(2)}) %collective-permute-start.3) | collective-permute-done | bytes 36896 | tf_op jit(solution)/shard_map/ppermute | solution.py:281
  11.4 1.4 %collective-permute-start.4 = (bf16[32,576]{1,0:T(8,128)(2,1)S(1)}, bf16[32,576]{1,0:T(8,128)(2,1)S(1)}, u32[]{:S(2)}, u32[]{:S(2)}) collective-permute-start(bf16[32,576]{1,0:T(8,128)(2,1)S(1)} %collective-permute-done.3.refs_4_), channel_id=1, source_target_pairs={{0,3},{1,2},{2,1},{3,0},{4,7},{5,6},{6,5},{7,4},{8,11},{9,10},{10,... | collective-permute-start | bytes 110600 | tf_op jit(solution)/shard_map/ppermute | solution.py:281
  12.8 0.0 collective-permute-done.after_ref.refs_2_
  12.8 0.3 %collective-permute-start.2 = (bf16[32,576]{1,0:T(8,128)(2,1)S(1)}, bf16[32,576]{1,0:T(8,128)(2,1)S(1)}, u32[]{:S(2)}, u32[]{:S(2)}) collective-permute-start(bf16[32,576]{1,0:T(8,128)(2,1)S(1)} %collective-permute-done.after_ref.refs_2_), channel_id=1, source_target_pairs={{0,3},{1,2},{2,1},{3,0},{4,7},{5,6},{6,5},{7,4},{8,11},{9,10},{10,... | collective-permute-start | bytes 110600 | tf_op jit(solution)/shard_map/ppermute | solution.py:281
  13.1 2.8 %stage_cache.1 = (bf16[4,576,512]{2,1,0:T(8,128)(2,1)S(1)}, bf16[8,512,128]{2,1,0:T(8,128)(2,1)S(1)}, f32[32,512]{1,0:T(8,128)S(1)}, f32[4,8,576]{2,1,0:T(8,128)...) custom-call(bf16[4,576,512]{2,1,0:T(8,128)(2,1)} %bitcast.1, bf16[8,512,128]{2,1,0:T(8,128)(2,1)} %w_hbm.3, ...), custom_call_target="tpu_custom_call" | custom-call | tf_op jit(solution)/shard_map/stage_cache/pallas_call | solution.py:305
  15.9 0.0 collective-permute-done.1.refs_1_
  15.9 0.0 collective-permute-done.6.refs_7_
  15.9 0.0 collective-permute-done.4.refs_5_
  15.9 0.4 %collective-permute-done.2.refs_3_ = bf16[32,576]{1,0:T(8,128)(2,1)S(1)} collective-permute-done((bf16[32,576]{1,0:T(8,128)(2,1)S(1)}, bf16[32,576]{1,0:T(8,128)(2,1)S(1)}, u32[]{:S(2)}, u32[]{:S(2)}) %collective-permute-start.2) | collective-permute-done | bytes 36896 | tf_op jit(solution)/shard_map/ppermute | solution.py:281
  16.3 1.8 %attend.1 = (f32[32,640]{1,0:T(8,128)S(1)}, bf16[32,640]{1,0:T(8,128)(2,1)S(1)}, f32[32,640]{1,0:T(8,128)S(1)}, bf16[32,640]{1,0:T(8,128)(2,1)S(1)}, f32[32,640]...) custom-call(bf16[32,576]{1,0:T(8,128)(2,1)S(1)} %absorb.1.refs_0_, ...), custom_call_target="tpu_custom_call" | custom-call | tf_op jit(solution)/shard_map/attend/pallas_call | solution.py:326
  18.1 1.1 %collective-permute-start.8 = (bf16[32,640]{1,0:T(8,128)(2,1)S(1)}, bf16[32,640]{1,0:T(8,128)(2,1)S(1)}, u32[]{:S(2)}, u32[]{:S(2)}) collective-permute-start(bf16[32,640]{1,0:T(8,128)(2,1)S(1)} %get-tuple-element.21), channel_id=1, source_target_pairs={{0,3},{1,2},{2,1},{3,0},{4,7},{5,6},{6,5},{7,4},{8,11},{9,10},{10,... | collective-permute-start | bytes 122888 | tf_op jit(solution)/shard_map/ppermute | solution.py:281
  19.2 0.7 %collective-permute-start.10 = (bf16[32,640]{1,0:T(8,128)(2,1)S(1)}, bf16[32,640]{1,0:T(8,128)(2,1)S(1)}, u32[]{:S(2)}, u32[]{:S(2)}) collective-permute-start(bf16[32,640]{1,0:T(8,128)(2,1)S(1)} %get-tuple-element.23), channel_id=1, source_target_pairs={{0,3},{1,2},{2,1},{3,0},{4,7},{5,6},{6,5},{7,4},{8,11},{9,10},{10,... | collective-permute-start | bytes 122888 | tf_op jit(solution)/shard_map/ppermute | solution.py:281
  19.9 1.0 %collective-permute-start.12 = (bf16[32,640]{1,0:T(8,128)(2,1)S(1)}, bf16[32,640]{1,0:T(8,128)(2,1)S(1)}, u32[]{:S(2)}, u32[]{:S(2)}) collective-permute-start(bf16[32,640]{1,0:T(8,128)(2,1)S(1)} %get-tuple-element.25), channel_id=1, source_target_pairs={{0,3},{1,2},{2,1},{3,0},{4,7},{5,6},{6,5},{7,4},{8,11},{9,10},{10,... | collective-permute-start | bytes 122888 | tf_op jit(solution)/shard_map/ppermute | solution.py:281
  20.9 0.7 %collective-permute-start.7 = (bf16[32,640]{1,0:T(8,128)(2,1)S(1)}, bf16[32,640]{1,0:T(8,128)(2,1)S(1)}, u32[]{:S(2)}, u32[]{:S(2)}) collective-permute-start(bf16[32,640]{1,0:T(8,128)(2,1)S(1)} %get-tuple-element.20), channel_id=1, source_target_pairs={{0,3},{1,2},{2,1},{3,0},{4,7},{5,6},{6,5},{7,4},{8,11},{9,10},{10,... | collective-permute-start | bytes 122888 | tf_op jit(solution)/shard_map/ppermute | solution.py:281
  21.7 0.1 collective-permute-done.8.got_ref
  21.7 0.2 merge_pair.3
  21.9 2.8 %collective-permute-start.9 = (bf16[32,640]{1,0:T(8,128)(2,1)S(1)}, bf16[32,640]{1,0:T(8,128)(2,1)S(1)}, u32[]{:S(2)}, u32[]{:S(2)}) collective-permute-start(bf16[32,640]{1,0:T(8,128)(2,1)S(1)} %merge_pair.3), channel_id=1, source_target_pairs={{0,13},{1,12},{2,15},{3,14},{4,9},{5,8},{6,11},{7,10},{8,5},{9,4},... | collective-permute-start | bytes 122888 | tf_op jit(solution)/shard_map/ppermute | solution.py:281
  24.7 0.0 collective-permute-done.10.got_ref
  24.7 0.2 merge_pair.4
  24.9 0.1 collective-permute-start.11
  25.0 0.0 collective-permute-done.12.got_ref
  25.0 0.2 merge_pair.5.refs_10_
  25.2 1.1 %collective-permute-start.13 = (bf16[32,640]{1,0:T(8,128)(2,1)S(1)}, bf16[32,640]{1,0:T(8,128)(2,1)S(1)}, u32[]{:S(2)}, u32[]{:S(2)}) collective-permute-start(bf16[32,640]{1,0:T(8,128)(2,1)S(1)} %merge_pair.5.refs_10_), channel_id=1, source_target_pairs={{0,5},{1,4},{2,7},{3,6},{4,1},{5,0},{6,3},{7,2},{8,13},{9,12},{10,... | collective-permute-start | bytes 122888 | tf_op jit(solution)/shard_map/ppermute | solution.py:281
  26.3 0.3 %page_bounds.1.mine_ref = f32[4,8,8]{2,1,0:T(8,128)S(1)} custom-call(bf16[32,576]{1,0:T(8,128)(2,1)S(1)} %absorb.1.refs_0_, bf16[32,576]{1,0:T(8,128)(2,1)S(1)} %collective-permute-done.1.refs_1_, bf16[32,576]{1,0:T(8,128)(2,1)S(1)} %collective-permute-done.after_ref.refs_2_, bf16[32,576]{1,0:T(8,128)(2,1)S(1)} %collective-permute-done.2.refs_3_, ...), custom_call_target="tpu_custom_call" | custom-call | tf_op jit(solution)/shard_map/page_bounds/pallas_call | solution.py:351
  26.6 0.6 %collective-permute-start.14 = (f32[4,8,8]{2,1,0:T(8,128)S(1)}, f32[4,8,8]{2,1,0:T(8,128)S(1)}, u32[]{:S(2)}, u32[]{:S(2)}) collective-permute-start(f32[4,8,8]{2,1,0:T(8,128)S(1)} %page_bounds.1.mine_ref), channel_id=1, source_target_pairs={{0,1},{1,0},{2,3},{3,2},{4,5},{5,4},{6,7},{7,6},{8,9},{9,8},{10,11... | collective-permute-start | bytes 3080 | tf_op jit(solution)/shard_map/ppermute | solution.py:359
  27.3 0.8 %collective-permute-done.14.other_ref = f32[4,8,8]{2,1,0:T(8,128)S(1)} collective-permute-done((f32[4,8,8]{2,1,0:T(8,128)S(1)}, f32[4,8,8]{2,1,0:T(8,128)S(1)}, u32[]{:S(2)}, u32[]{:S(2)}) %collective-permute-start.14) | collective-permute-done | bytes 1056 | tf_op jit(solution)/shard_map/ppermute | solution.py:359
  28.1 0.6 %group_bounds.1 = f32[4,8,8]{2,1,0:T(8,128)} custom-call(f32[4,8,8]{2,1,0:T(8,128)S(1)} %page_bounds.1.mine_ref, f32[4,8,8]{2,1,0:T(8,128)S(1)} %collective-permute-done.14.other_ref, f32[4,8,8]{2,1,0:T(8,128)S(1)} %get-tuple-element.29.live_ref), custom_call_target="tpu_custom_call" | custom-call | tf_op jit(solution)/shard_map/group_bounds/pallas_call | solution.py:360
  28.7 0.0 collective-permute-done.7.refs_1_
  28.7 0.0 collective-permute-done.9.refs_2_
  28.7 1.0 %collective-permute-done.11.refs_3_ = bf16[32,640]{1,0:T(8,128)(2,1)S(1)} collective-permute-done((bf16[32,640]{1,0:T(8,128)(2,1)S(1)}, bf16[32,640]{1,0:T(8,128)(2,1)S(1)}, u32[]{:S(2)}, u32[]{:S(2)}) %collective-permute-start.11) | collective-permute-done | bytes 40992 | tf_op jit(solution)/shard_map/ppermute | solution.py:281
  29.7 0.2 collective-permute-done.13.refs_4_
  29.9 1.0 %merge_and_value.1 = bf16[4,8,128]{2,1,0:T(8,128)(2,1)} custom-call(bf16[8,512,128]{2,1,0:T(8,128)(2,1)S(1)} %get-tuple-element.16.w_ref, f32[32,640]{1,0:T(8,128)S(1)} %get-tuple-element.19.refs_0_, bf16[32,640]{1,0:T(8,128)(2,1)S(1)} %collective-permute-done.7.refs_1_, bf16[32,640]{1,0:T(8,128)(2,1)S(1)} %collective-permute-done.9.refs_2_, ...), custom_call_target="tpu_custom_call" | custom-call | tf_op jit(solution)/shard_map/merge_and_value/pallas_call | solution.py:369
Async XLA Ops:
  2.1 6.9 %collective-permute-start.5 = (bf16[32,576]{1,0:T(8,128)(2,1)S(1)}, bf16[32,576]{1,0:T(8,128)(2,1)S(1)}, u32[]{:S(2)}, u32[]{:S(2)}) collective-permute-start(bf16[32,576]{1,0:T(8,128)(2,1)S(1)} %absorb.1.refs_0_), channel_id=1, source_target_pairs={{0,13},{1,12},{2,15},{3,14},{4,9},{5,8},{6,11},{7,10},{8,5},{9,4},... | collective-permute-start | bytes 110600 | tf_op jit(solution)/shard_map/ppermute | solution.py:281
  6.7 4.7 %collective-permute-start.3 = (bf16[32,576]{1,0:T(8,128)(2,1)S(1)}, bf16[32,576]{1,0:T(8,128)(2,1)S(1)}, u32[]{:S(2)}, u32[]{:S(2)}) collective-permute-start(bf16[32,576]{1,0:T(8,128)(2,1)S(1)} %absorb.1.refs_0_), channel_id=1, source_target_pairs={{0,9},{1,8},{2,11},{3,10},{4,13},{5,12},{6,15},{7,14},{8,1},{9,0},... | collective-permute-start | bytes 110600 | tf_op jit(solution)/shard_map/ppermute | solution.py:281
  6.7 6.1 %collective-permute-start = (bf16[32,576]{1,0:T(8,128)(2,1)S(1)}, bf16[32,576]{1,0:T(8,128)(2,1)S(1)}, u32[]{:S(2)}, u32[]{:S(2)}) collective-permute-start(bf16[32,576]{1,0:T(8,128)(2,1)S(1)} %absorb.1.refs_0_), channel_id=1, source_target_pairs={{0,5},{1,4},{2,7},{3,6},{4,1},{5,0},{6,3},{7,2},{8,13},{9,12},{10,... | collective-permute-start | bytes 110600 | tf_op jit(solution)/shard_map/ppermute | solution.py:281
  7.6 8.3 %collective-permute-start.1 = (bf16[32,576]{1,0:T(8,128)(2,1)S(1)}, bf16[32,576]{1,0:T(8,128)(2,1)S(1)}, u32[]{:S(2)}, u32[]{:S(2)}) collective-permute-start(bf16[32,576]{1,0:T(8,128)(2,1)S(1)} %absorb.1.refs_0_), channel_id=1, source_target_pairs={{0,3},{1,2},{2,1},{3,0},{4,7},{5,6},{6,5},{7,4},{8,11},{9,10},{10,... | collective-permute-start | bytes 110600 | tf_op jit(solution)/shard_map/ppermute | solution.py:281
  9.0 6.9 %collective-permute-start.6 = (bf16[32,576]{1,0:T(8,128)(2,1)S(1)}, bf16[32,576]{1,0:T(8,128)(2,1)S(1)}, u32[]{:S(2)}, u32[]{:S(2)}) collective-permute-start(bf16[32,576]{1,0:T(8,128)(2,1)S(1)} %collective-permute-done.5.refs_6_), channel_id=1, source_target_pairs={{0,3},{1,2},{2,1},{3,0},{4,7},{5,6},{6,5},{7,4},{8,11},{9,10},{10,... | collective-permute-start | bytes 110600 | tf_op jit(solution)/shard_map/ppermute | solution.py:281
  11.4 4.5 %collective-permute-start.4 = (bf16[32,576]{1,0:T(8,128)(2,1)S(1)}, bf16[32,576]{1,0:T(8,128)(2,1)S(1)}, u32[]{:S(2)}, u32[]{:S(2)}) collective-permute-start(bf16[32,576]{1,0:T(8,128)(2,1)S(1)} %collective-permute-done.3.refs_4_), channel_id=1, source_target_pairs={{0,3},{1,2},{2,1},{3,0},{4,7},{5,6},{6,5},{7,4},{8,11},{9,10},{10,... | collective-permute-start | bytes 110600 | tf_op jit(solution)/shard_map/ppermute | solution.py:281
  12.8 3.5 %collective-permute-start.2 = (bf16[32,576]{1,0:T(8,128)(2,1)S(1)}, bf16[32,576]{1,0:T(8,128)(2,1)S(1)}, u32[]{:S(2)}, u32[]{:S(2)}) collective-permute-start(bf16[32,576]{1,0:T(8,128)(2,1)S(1)} %collective-permute-done.after_ref.refs_2_), channel_id=1, source_target_pairs={{0,3},{1,2},{2,1},{3,0},{4,7},{5,6},{6,5},{7,4},{8,11},{9,10},{10,... | collective-permute-start | bytes 110600 | tf_op jit(solution)/shard_map/ppermute | solution.py:281
  18.1 3.6 %collective-permute-start.8 = (bf16[32,640]{1,0:T(8,128)(2,1)S(1)}, bf16[32,640]{1,0:T(8,128)(2,1)S(1)}, u32[]{:S(2)}, u32[]{:S(2)}) collective-permute-start(bf16[32,640]{1,0:T(8,128)(2,1)S(1)} %get-tuple-element.21), channel_id=1, source_target_pairs={{0,3},{1,2},{2,1},{3,0},{4,7},{5,6},{6,5},{7,4},{8,11},{9,10},{10,... | collective-permute-start | bytes 122888 | tf_op jit(solution)/shard_map/ppermute | solution.py:281
  19.2 5.6 %collective-permute-start.10 = (bf16[32,640]{1,0:T(8,128)(2,1)S(1)}, bf16[32,640]{1,0:T(8,128)(2,1)S(1)}, u32[]{:S(2)}, u32[]{:S(2)}) collective-permute-start(bf16[32,640]{1,0:T(8,128)(2,1)S(1)} %get-tuple-element.23), channel_id=1, source_target_pairs={{0,3},{1,2},{2,1},{3,0},{4,7},{5,6},{6,5},{7,4},{8,11},{9,10},{10,... | collective-permute-start | bytes 122888 | tf_op jit(solution)/shard_map/ppermute | solution.py:281
  19.9 5.1 %collective-permute-start.12 = (bf16[32,640]{1,0:T(8,128)(2,1)S(1)}, bf16[32,640]{1,0:T(8,128)(2,1)S(1)}, u32[]{:S(2)}, u32[]{:S(2)}) collective-permute-start(bf16[32,640]{1,0:T(8,128)(2,1)S(1)} %get-tuple-element.25), channel_id=1, source_target_pairs={{0,3},{1,2},{2,1},{3,0},{4,7},{5,6},{6,5},{7,4},{8,11},{9,10},{10,... | collective-permute-start | bytes 122888 | tf_op jit(solution)/shard_map/ppermute | solution.py:281
  20.9 7.8 %collective-permute-start.7 = (bf16[32,640]{1,0:T(8,128)(2,1)S(1)}, bf16[32,640]{1,0:T(8,128)(2,1)S(1)}, u32[]{:S(2)}, u32[]{:S(2)}) collective-permute-start(bf16[32,640]{1,0:T(8,128)(2,1)S(1)} %get-tuple-element.20), channel_id=1, source_target_pairs={{0,3},{1,2},{2,1},{3,0},{4,7},{5,6},{6,5},{7,4},{8,11},{9,10},{10,... | collective-permute-start | bytes 122888 | tf_op jit(solution)/shard_map/ppermute | solution.py:281
  21.9 6.8 %collective-permute-start.9 = (bf16[32,640]{1,0:T(8,128)(2,1)S(1)}, bf16[32,640]{1,0:T(8,128)(2,1)S(1)}, u32[]{:S(2)}, u32[]{:S(2)}) collective-permute-start(bf16[32,640]{1,0:T(8,128)(2,1)S(1)} %merge_pair.3), channel_id=1, source_target_pairs={{0,13},{1,12},{2,15},{3,14},{4,9},{5,8},{6,11},{7,10},{8,5},{9,4},... | collective-permute-start | bytes 122888 | tf_op jit(solution)/shard_map/ppermute | solution.py:281
  24.9 4.8 %collective-permute-start.11 = (bf16[32,640]{1,0:T(8,128)(2,1)S(1)}, bf16[32,640]{1,0:T(8,128)(2,1)S(1)}, u32[]{:S(2)}, u32[]{:S(2)}) collective-permute-start(bf16[32,640]{1,0:T(8,128)(2,1)S(1)} %merge_pair.4), channel_id=1, source_target_pairs={{0,9},{1,8},{2,11},{3,10},{4,13},{5,12},{6,15},{7,14},{8,1},{9,0},... | collective-permute-start | bytes 122888 | tf_op jit(solution)/shard_map/ppermute | solution.py:281
  25.2 4.7 %collective-permute-start.13 = (bf16[32,640]{1,0:T(8,128)(2,1)S(1)}, bf16[32,640]{1,0:T(8,128)(2,1)S(1)}, u32[]{:S(2)}, u32[]{:S(2)}) collective-permute-start(bf16[32,640]{1,0:T(8,128)(2,1)S(1)} %merge_pair.5.refs_10_), channel_id=1, source_target_pairs={{0,5},{1,4},{2,7},{3,6},{4,1},{5,0},{6,3},{7,2},{8,13},{9,12},{10,... | collective-permute-start | bytes 122888 | tf_op jit(solution)/shard_map/ppermute | solution.py:281
  26.6 1.5 %collective-permute-start.14 = (f32[4,8,8]{2,1,0:T(8,128)S(1)}, f32[4,8,8]{2,1,0:T(8,128)S(1)}, u32[]{:S(2)}, u32[]{:S(2)}) collective-permute-start(f32[4,8,8]{2,1,0:T(8,128)S(1)} %page_bounds.1.mine_ref), channel_id=1, source_target_pairs={{0,1},{1,0},{2,3},{3,2},{4,5},{5,4},{6,7},{7,6},{8,9},{9,8},{10,11... | collective-permute-start | bytes 3080 | tf_op jit(solution)/shard_map/ppermute | solution.py:359

commit v4 on v3

--- a/solution.py
+++ b/solution.py
@@ -13,6 +13,7 @@
 BF16 = jnp.bfloat16
 F32 = jnp.float32
 LANES = 128
+LOG2E = 1.4426950408889634
 VMEM = pl.BlockSpec(memory_space=pltpu.VMEM)
 SMEM = pl.BlockSpec(memory_space=pltpu.SMEM)
 HBM = pl.BlockSpec(memory_space=pltpu.HBM)
@@ -58,8 +59,8 @@
 
 
 def stage_kernel(
-    cache_hbm, w_hbm, selected_hbm, lengths_hbm, after_ref,
-    cache_ref, w_ref, mask_ref, low_ref, high_ref, live_ref, selected_ref, lengths_ref, sems,
+    cache_hbm, selected_hbm, lengths_hbm, after_ref,
+    cache_ref, slots_ref, mask_ref, low_ref, high_ref, live_ref, selected_ref, lengths_ref, sems,
 ):
     requests, groups, picks = selected_ref.shape
     width, tokens = cache_ref.shape[1:]
@@ -69,10 +70,9 @@
         pltpu.make_async_copy(selected_hbm, selected_ref, sems.at[0]),
         pltpu.make_async_copy(lengths_hbm, lengths_ref, sems.at[1]),
         *(
-            pltpu.make_async_copy(cache_hbm.at[r], cache_ref.at[r], sems.at[3 + r])
+            pltpu.make_async_copy(cache_hbm.at[r], cache_ref.at[r], sems.at[2 + r])
             for r in range(requests)
         ),
-        pltpu.make_async_copy(w_hbm, w_ref, sems.at[2]),
     ]
     for copy in copies:
         copy.start()
@@ -96,13 +96,14 @@
     for r in range(requests):
         live_ref[r] = jnp.where(first < lengths_ref[r], 1.0, 0.0)
         copies[2 + r].wait()
-        slots = cache_ref[r].astype(F32).T
+        slots = cache_ref[r].T
+        slots_ref[r] = slots[:, : slots_ref.shape[2]]
+        slots = slots.astype(F32)
         live = row < lengths_ref[r]
         slots = slots.reshape(pages, PAGE, width)
         slots = jnp.where(live.reshape(pages, PAGE, width), slots, slots[:, 0:1, :])
         low_ref[r] = jnp.min(slots, axis=1)
         high_ref[r] = jnp.max(slots, axis=1)
-    copies[-1].wait()
 
 
 def split3(x):
@@ -130,7 +131,7 @@
 def attend_kernel(scale, heads, offsets, latent, *refs):
     count = len(offsets)
     block_refs = refs[:count]
-    cache_ref, mask_ref, *out_refs = refs[count:]
+    cache_ref, slots_ref, mask_ref, *out_refs = refs[count:]
     requests, _, tokens = cache_ref.shape
     groups = mask_ref.shape[0] // requests
     blocks = [b[...].astype(F32) for b in block_refs]
@@ -138,7 +139,7 @@
     for r in range(requests):
         query = queries_of(blocks, r, heads).astype(BF16)
         keys = cache_ref[r]
-        scores = jnp.dot(query, keys, preferred_element_type=F32) * scale
+        scores = jnp.dot(query, keys, preferred_element_type=F32)
         mask = jnp.concatenate(
             [
                 jnp.broadcast_to(
@@ -150,15 +151,11 @@
         )
         scores = jnp.where(mask > 0.5, scores, NEG)
         top = jnp.max(scores, axis=1, keepdims=True)
-        weights = jnp.where(mask > 0.5, jnp.exp(scores - top), 0.0).astype(BF16)
+        weights = jnp.exp2((scores - top) * (scale * LOG2E)).astype(BF16)
         total = jnp.sum(weights.astype(F32), axis=1, keepdims=True)
-        weighted = lax.dot_general(
-            weights, keys[:latent], (((1,), (1,)), ((), ())), preferred_element_type=F32
-        )
-        some = total > 0.0
-        safe = jnp.where(some, total, 1.0)
-        outs.append(weighted / safe)
-        sums.append(jnp.where(some, top + jnp.log(safe), NEG))
+        weighted = jnp.dot(weights, slots_ref[r], preferred_element_type=F32)
+        outs.append(weighted * (1.0 / total))
+        sums.append(top * scale + jnp.log(total))
     for i, k in enumerate(offsets):
         rows = slice(i * heads, (i + 1) * heads)
         out = jnp.concatenate([o[rows] for o in outs], axis=0)
@@ -267,14 +264,14 @@
     half = seq_count // 2
     slots = jnp.swapaxes(cache, 1, 2)
 
-    q_nope, q_rope, w_uk, w_uv, slots, lengths, selected = (
+    q_nope, q_rope, w_uk, slots, lengths, selected = (
         pltpu.with_memory_space_constraint(x, pltpu.HBM)
-        for x in (q_nope, q_rope, w_uk, w_uv, slots, lengths, selected)
+        for x in (q_nope, q_rope, w_uk, slots, lengths, selected)
     )
 
-    def swap(x, k):
+    def swap(x, k, flip=1):
         pairs = [
-            (i * head_count + c, (i ^ k) * head_count + (c ^ 1))
+            (i * head_count + c, (i ^ k) * head_count + (c ^ flip))
             for i in range(seq_count)
             for c in range(head_count)
         ]
@@ -297,42 +294,44 @@
     block = {0: mine}
     for k in far:
         block[k] = swap(mine, k)
+    near = far[-1]
+    block[near + 1] = swap(mine, near + 1, 0)
     block[1] = swap(mine, 1)
-    for k in far:
+    for k in far[:-1]:
         block[k + 1] = swap(block[k], 1)
     blocks = [block[k] for k in offsets]
 
-    keys, w_value, mask, low, high, live = pl.pallas_call(
+    keys, values, mask, low, high, live = pl.pallas_call(
         stage_kernel,
         out_shape=(
             jax.ShapeDtypeStruct(slots.shape, BF16),
-            jax.ShapeDtypeStruct(w_uv.shape, BF16),
+            jax.ShapeDtypeStruct((requests, tokens, latent), BF16),
             jax.ShapeDtypeStruct((requests * groups, tokens), F32),
             jax.ShapeDtypeStruct((requests, pages, width), F32),
             jax.ShapeDtypeStruct((requests, pages, width), F32),
             jax.ShapeDtypeStruct((requests, groups, pages), F32),
         ),
-        in_specs=[HBM] * 4 + [ANY],
+        in_specs=[HBM] * 3 + [ANY],
         out_specs=(VMEM,) * 6,
         scratch_shapes=[
             pltpu.VMEM(selected.shape, jnp.int32),
             pltpu.SMEM(lengths.shape, jnp.int32),
-            pltpu.SemaphoreType.DMA((3 + requests,)),
+            pltpu.SemaphoreType.DMA((2 + requests,)),
         ],
         compiler_params=params(),
         name="stage_cache",
-    )(slots, w_uv, selected, lengths, block[far[-1]])
+    )(slots, selected, lengths, block[near])
 
     parts = pl.pallas_call(
         functools.partial(attend_kernel, scale, heads, offsets, latent),
         out_shape=tuple(
             jax.ShapeDtypeStruct((rows, latent + LANES), BF16 if k % 2 else F32) for k in offsets
         ),
-        in_specs=[VMEM] * (seq_count + 2),
+        in_specs=[VMEM] * (seq_count + 3),
         out_specs=(VMEM,) * seq_count,
         compiler_params=params(),
         name="attend",
-    )(*blocks, keys, mask)
+    )(*blocks, keys, values, mask)
 
     got = {k: swap(parts[k + 1], 1) for k in far + (0,)}
     send = {
@@ -373,7 +372,7 @@
         out_specs=VMEM,
         compiler_params=params(),
         name="merge_and_value",
-    )(w_value, parts[0], got[0], *arrived)
+    )(w_uv, parts[0], got[0], *arrived)
     return attended, largest
 
 

time: 31.3 us -> 30.8 us (0.984)
  waiting for transfers between devices: 3.59 us -> 2.63 us
  starting transfers between devices: 18.2 us -> 18.9 us
    ppermute x14, starting transfers between devices: 17.5 us -> 18.8 us  [swap(): return lax.ppermute(x, ('seq', 'head'), pairs)]
    ppermute x14, waiting for transfers between devices: 2.75 us -> 1.46 us  [swap(): return lax.ppermute(x, ('seq', 'head'), pairs)]
    ppermute x1, starting transfers between devices: 0.63 us -> 0.07 us  [local(): lax.ppermute(bounds, 'head', [(i, i ^ 1) for i in range(head_count)])]
    ppermute x1, waiting for transfers between devices: 0.84 us -> 1.17 us  [local(): lax.ppermute(bounds, 'head', [(i, i ^ 1) for i in range(head_count)])]
  transfers between devices with their start and end apart: 15 -> 15, of which waited for: 6 -> 4; matrix products, arithmetic and copies ran while one was open for 0% -> 0% of each run, Pallas kernels for 14% -> 14%
where the time goes in v4:
time: 30.8 us; the launch traced here: 30.5 us
  starting transfers between devices  18.9 us (61%)
  Pallas kernels  8.22 us (27%)
  waiting for transfers between devices  2.63 us (9%)
  between operations  0.72 us (2%)
    ppermute x14, starting transfers between devices, swap(): return lax.ppermute(x, ('seq', 'head'), pairs)  18.8 us
    pallas_call x1, Pallas kernels, local(): pl.pallas_call(stage_kernel, out_shape=(jax.ShapeDtypeStruct(slots.shape,...  2.66 us
    pallas_call x1, Pallas kernels, local(): pl.pallas_call(functools.partial(attend_kernel, scale, heads, offsets, la...  1.62 us
    pallas_call x1, Pallas kernels, local(): pl.pallas_call(absorb_kernel, out_shape=jax.ShapeDtypeStruct((rows, width...  1.46 us
    ppermute x14, waiting for transfers between devices, swap(): return lax.ppermute(x, ('seq', 'head'), pairs)  1.46 us
    ppermute x1, waiting for transfers between devices, local(): lax.ppermute(bounds, 'head', [(i, i ^ 1) for i in range(head_count)])  1.17 us
    pallas_call x1, Pallas kernels, local(): pl.pallas_call(functools.partial(value_kernel, latent, heads), out_shape=...  1.02 us
  transfers between devices with their start and end apart: 15, of which 4 were waited for; matrix products, arithmetic and copies ran while one was open for 0% of the time, Pallas kernels for 14%

profile of v4, /device:TPU:0, one launch (start us, length us, event | category | flops | bytes accessed | tf_op | source)
XLA Modules:
  0.0 30.5 jit_solution(6552744212857044035)
XLA Ops:
  0.6 1.5 %absorb.1.refs_0_ = bf16[32,576]{1,0:T(8,128)(2,1)S(1)} custom-call(bf16[4,8,128]{2,1,0:T(8,128)(2,1)} %nope_hbm.1, bf16[4,8,64]{2,1,0:T(8,128)(2,1)} %rope_hbm.1, bf16[8,128,512]{2,1,0:T(8,128)(2,1)} %w_hbm.1), custom_call_target="tpu_custom_call" | custom-call | tf_op jit(solution)/shard_map/absorb/pallas_call | solution.py:280
  2.1 4.6 %collective-permute-start.5 = (bf16[32,576]{1,0:T(8,128)(2,1)S(1)}, bf16[32,576]{1,0:T(8,128)(2,1)S(1)}, u32[]{:S(2)}, u32[]{:S(2)}) collective-permute-start(bf16[32,576]{1,0:T(8,128)(2,1)S(1)} %absorb.1.refs_0_), channel_id=1, source_target_pairs={{0,13},{1,12},{2,15},{3,14},{4,9},{5,8},{6,11},{7,10},{8,5},{9,4},... | collective-permute-start | bytes 110600 | tf_op jit(solution)/shard_map/ppermute | solution.py:278
  6.7 0.0 collective-permute-start.3
  6.7 0.9 %collective-permute-start.1 = (bf16[32,576]{1,0:T(8,128)(2,1)S(1)}, bf16[32,576]{1,0:T(8,128)(2,1)S(1)}, u32[]{:S(2)}, u32[]{:S(2)}) collective-permute-start(bf16[32,576]{1,0:T(8,128)(2,1)S(1)} %absorb.1.refs_0_), channel_id=1, source_target_pairs={{0,5},{1,4},{2,7},{3,6},{4,1},{5,0},{6,3},{7,2},{8,13},{9,12},{10,... | collective-permute-start | bytes 110600 | tf_op jit(solution)/shard_map/ppermute | solution.py:278
  7.6 2.3 %collective-permute-start.2 = (bf16[32,576]{1,0:T(8,128)(2,1)S(1)}, bf16[32,576]{1,0:T(8,128)(2,1)S(1)}, u32[]{:S(2)}, u32[]{:S(2)}) collective-permute-start(bf16[32,576]{1,0:T(8,128)(2,1)S(1)} %absorb.1.refs_0_), channel_id=1, source_target_pairs={{0,6},{1,7},{2,4},{3,5},{4,2},{5,3},{6,0},{7,1},{8,14},{9,15},{10,... | collective-permute-start | bytes 110600 | tf_op jit(solution)/shard_map/ppermute | solution.py:278
  9.9 0.0 collective-permute-start
  9.9 0.0 collective-permute-done.5.refs_6_
  9.9 1.7 %collective-permute-start.6 = (bf16[32,576]{1,0:T(8,128)(2,1)S(1)}, bf16[32,576]{1,0:T(8,128)(2,1)S(1)}, u32[]{:S(2)}, u32[]{:S(2)}) collective-permute-start(bf16[32,576]{1,0:T(8,128)(2,1)S(1)} %collective-permute-done.5.refs_6_), channel_id=1, source_target_pairs={{0,3},{1,2},{2,1},{3,0},{4,7},{5,6},{6,5},{7,4},{8,11},{9,10},{10,... | collective-permute-start | bytes 110600 | tf_op jit(solution)/shard_map/ppermute | solution.py:278
  11.7 0.0 collective-permute-done.3.refs_4_
  11.7 1.1 %collective-permute-start.4 = (bf16[32,576]{1,0:T(8,128)(2,1)S(1)}, bf16[32,576]{1,0:T(8,128)(2,1)S(1)}, u32[]{:S(2)}, u32[]{:S(2)}) collective-permute-start(bf16[32,576]{1,0:T(8,128)(2,1)S(1)} %collective-permute-done.3.refs_4_), channel_id=1, source_target_pairs={{0,3},{1,2},{2,1},{3,0},{4,7},{5,6},{6,5},{7,4},{8,11},{9,10},{10,... | collective-permute-start | bytes 110600 | tf_op jit(solution)/shard_map/ppermute | solution.py:278
  12.8 0.0 collective-permute-done.1.after_ref.refs_2_
  12.8 2.7 %stage_cache.1 = (bf16[4,576,512]{2,1,0:T(8,128)(2,1)S(1)}, bf16[4,512,512]{2,1,0:T(8,128)(2,1)S(1)}, f32[32,512]{1,0:T(8,128)S(1)}, f32[4,8,576]{2,1,0:T(8,128)...) custom-call(bf16[4,576,512]{2,1,0:T(8,128)(2,1)} %bitcast.1, s32[4,8,32]{2,1,0:T(8,128)} %selected_hbm.1, ...), custom_call_target="tpu_custom_call" | custom-call | tf_op jit(solution)/shard_map/stage_cache/pallas_call | solution.py:304
  15.5 0.0 collective-permute-done.2.refs_3_
  15.5 0.0 collective-permute-done.refs_1_
  15.5 0.0 collective-permute-done.6.refs_7_
  15.5 0.2 collective-permute-done.4.refs_5_
  15.7 0.0 copy-start
  15.7 1.6 %attend.1 = (f32[32,640]{1,0:T(8,128)S(1)}, bf16[32,640]{1,0:T(8,128)(2,1)S(1)}, f32[32,640]{1,0:T(8,128)S(1)}, bf16[32,640]{1,0:T(8,128)(2,1)S(1)}, f32[32,640]...) custom-call(bf16[32,576]{1,0:T(8,128)(2,1)S(1)} %absorb.1.refs_0_, ...), custom_call_target="tpu_custom_call" | custom-call | tf_op jit(solution)/shard_map/attend/pallas_call | solution.py:325
  17.3 0.6 %collective-permute-start.8 = (bf16[32,640]{1,0:T(8,128)(2,1)S(1)}, bf16[32,640]{1,0:T(8,128)(2,1)S(1)}, u32[]{:S(2)}, u32[]{:S(2)}) collective-permute-start(bf16[32,640]{1,0:T(8,128)(2,1)S(1)} %get-tuple-element.21), channel_id=1, source_target_pairs={{0,3},{1,2},{2,1},{3,0},{4,7},{5,6},{6,5},{7,4},{8,11},{9,10},{10,... | collective-permute-start | bytes 122888 | tf_op jit(solution)/shard_map/ppermute | solution.py:278
  17.9 1.2 %collective-permute-start.10 = (bf16[32,640]{1,0:T(8,128)(2,1)S(1)}, bf16[32,640]{1,0:T(8,128)(2,1)S(1)}, u32[]{:S(2)}, u32[]{:S(2)}) collective-permute-start(bf16[32,640]{1,0:T(8,128)(2,1)S(1)} %get-tuple-element.23), channel_id=1, source_target_pairs={{0,3},{1,2},{2,1},{3,0},{4,7},{5,6},{6,5},{7,4},{8,11},{9,10},{10,... | collective-permute-start | bytes 122888 | tf_op jit(solution)/shard_map/ppermute | solution.py:278
  19.1 0.6 %collective-permute-start.12 = (bf16[32,640]{1,0:T(8,128)(2,1)S(1)}, bf16[32,640]{1,0:T(8,128)(2,1)S(1)}, u32[]{:S(2)}, u32[]{:S(2)}) collective-permute-start(bf16[32,640]{1,0:T(8,128)(2,1)S(1)} %get-tuple-element.25), channel_id=1, source_target_pairs={{0,3},{1,2},{2,1},{3,0},{4,7},{5,6},{6,5},{7,4},{8,11},{9,10},{10,... | collective-permute-start | bytes 122888 | tf_op jit(solution)/shard_map/ppermute | solution.py:278
  19.6 1.2 %collective-permute-start.7 = (bf16[32,640]{1,0:T(8,128)(2,1)S(1)}, bf16[32,640]{1,0:T(8,128)(2,1)S(1)}, u32[]{:S(2)}, u32[]{:S(2)}) collective-permute-start(bf16[32,640]{1,0:T(8,128)(2,1)S(1)} %get-tuple-element.20), channel_id=1, source_target_pairs={{0,3},{1,2},{2,1},{3,0},{4,7},{5,6},{6,5},{7,4},{8,11},{9,10},{10,... | collective-permute-start | bytes 122888 | tf_op jit(solution)/shard_map/ppermute | solution.py:278
  20.8 0.1 collective-permute-done.8.got_ref
  20.9 0.2 merge_pair.3
  21.1 2.7 %collective-permute-start.9 = (bf16[32,640]{1,0:T(8,128)(2,1)S(1)}, bf16[32,640]{1,0:T(8,128)(2,1)S(1)}, u32[]{:S(2)}, u32[]{:S(2)}) collective-permute-start(bf16[32,640]{1,0:T(8,128)(2,1)S(1)} %merge_pair.3), channel_id=1, source_target_pairs={{0,13},{1,12},{2,15},{3,14},{4,9},{5,8},{6,11},{7,10},{8,5},{9,4},... | collective-permute-start | bytes 122888 | tf_op jit(solution)/shard_map/ppermute | solution.py:278
  23.7 0.0 collective-permute-done.10.got_ref
  23.7 0.2 merge_pair.4
  23.9 0.4 %collective-permute-start.11 = (bf16[32,640]{1,0:T(8,128)(2,1)S(1)}, bf16[32,640]{1,0:T(8,128)(2,1)S(1)}, u32[]{:S(2)}, u32[]{:S(2)}) collective-permute-start(bf16[32,640]{1,0:T(8,128)(2,1)S(1)} %merge_pair.4), channel_id=1, source_target_pairs={{0,9},{1,8},{2,11},{3,10},{4,13},{5,12},{6,15},{7,14},{8,1},{9,0},... | collective-permute-start | bytes 122888 | tf_op jit(solution)/shard_map/ppermute | solution.py:278
  24.3 0.0 collective-permute-done.12.got_ref
  24.3 0.2 merge_pair.5.refs_10_
  24.5 1.6 %collective-permute-start.13 = (bf16[32,640]{1,0:T(8,128)(2,1)S(1)}, bf16[32,640]{1,0:T(8,128)(2,1)S(1)}, u32[]{:S(2)}, u32[]{:S(2)}) collective-permute-start(bf16[32,640]{1,0:T(8,128)(2,1)S(1)} %merge_pair.5.refs_10_), channel_id=1, source_target_pairs={{0,5},{1,4},{2,7},{3,6},{4,1},{5,0},{6,3},{7,2},{8,13},{9,12},{10,... | collective-permute-start | bytes 122888 | tf_op jit(solution)/shard_map/ppermute | solution.py:278
  26.1 0.3 %page_bounds.1.mine_ref = f32[4,8,8]{2,1,0:T(8,128)S(1)} custom-call(bf16[32,576]{1,0:T(8,128)(2,1)S(1)} %absorb.1.refs_0_, bf16[32,576]{1,0:T(8,128)(2,1)S(1)} %collective-permute-done.refs_1_, bf16[32,576]{1,0:T(8,128)(2,1)S(1)} %collective-permute-done.1.after_ref.refs_2_, bf16[32,576]{1,0:T(8,128)(2,1)S(1)} %collective-permute-done.2.refs_3_, ...), custom_call_target="tpu_custom_call" | custom-call | tf_op jit(solution)/shard_map/page_bounds/pallas_call | solution.py:350
  26.4 0.1 collective-permute-start.14
  26.5 1.2 %collective-permute-done.14.other_ref = f32[4,8,8]{2,1,0:T(8,128)S(1)} collective-permute-done((f32[4,8,8]{2,1,0:T(8,128)S(1)}, f32[4,8,8]{2,1,0:T(8,128)S(1)}, u32[]{:S(2)}, u32[]{:S(2)}) %collective-permute-start.14) | collective-permute-done | bytes 1056 | tf_op jit(solution)/shard_map/ppermute | solution.py:358
  27.6 0.6 %group_bounds.1 = f32[4,8,8]{2,1,0:T(8,128)} custom-call(f32[4,8,8]{2,1,0:T(8,128)S(1)} %page_bounds.1.mine_ref, f32[4,8,8]{2,1,0:T(8,128)S(1)} %collective-permute-done.14.other_ref, f32[4,8,8]{2,1,0:T(8,128)S(1)} %get-tuple-element.29.live_ref), custom_call_target="tpu_custom_call" | custom-call | tf_op jit(solution)/shard_map/group_bounds/pallas_call | solution.py:359
  28.3 0.0 collective-permute-done.7.refs_1_
  28.3 0.0 collective-permute-done.9.refs_2_
  28.3 1.2 %collective-permute-done.11.refs_3_ = bf16[32,640]{1,0:T(8,128)(2,1)S(1)} collective-permute-done((bf16[32,640]{1,0:T(8,128)(2,1)S(1)}, bf16[32,640]{1,0:T(8,128)(2,1)S(1)}, u32[]{:S(2)}, u32[]{:S(2)}) %collective-permute-start.11) | collective-permute-done | bytes 40992 | tf_op jit(solution)/shard_map/ppermute | solution.py:278
  29.4 0.0 collective-permute-done.13.refs_4_
  29.4 0.0 copy-done
  29.4 1.0 %merge_and_value.1 = bf16[4,8,128]{2,1,0:T(8,128)(2,1)} custom-call(bf16[8,512,128]{2,1,0:T(8,128)(2,1)S(1)} %copy-done, f32[32,640]{1,0:T(8,128)S(1)} %get-tuple-element.19.refs_0_, bf16[32,640]{1,0:T(8,128)(2,1)S(1)} %collective-permute-done.7.refs_1_, bf16[32,640]{1,0:T(8,128)(2,1)S(1)} %collective-permute-done.9.refs_2_, ...), custom_call_target="tpu_custom_call" | custom-call | tf_op jit(solution)/shard_map/merge_and_value/pallas_call | solution.py:368
Async XLA Ops:
  2.1 7.8 %collective-permute-start.5 = (bf16[32,576]{1,0:T(8,128)(2,1)S(1)}, bf16[32,576]{1,0:T(8,128)(2,1)S(1)}, u32[]{:S(2)}, u32[]{:S(2)}) collective-permute-start(bf16[32,576]{1,0:T(8,128)(2,1)S(1)} %absorb.1.refs_0_), channel_id=1, source_target_pairs={{0,13},{1,12},{2,15},{3,14},{4,9},{5,8},{6,11},{7,10},{8,5},{9,4},... | collective-permute-start | bytes 110600 | tf_op jit(solution)/shard_map/ppermute | solution.py:278
  6.7 5.0 %collective-permute-start.3 = (bf16[32,576]{1,0:T(8,128)(2,1)S(1)}, bf16[32,576]{1,0:T(8,128)(2,1)S(1)}, u32[]{:S(2)}, u32[]{:S(2)}) collective-permute-start(bf16[32,576]{1,0:T(8,128)(2,1)S(1)} %absorb.1.refs_0_), channel_id=1, source_target_pairs={{0,9},{1,8},{2,11},{3,10},{4,13},{5,12},{6,15},{7,14},{8,1},{9,0},... | collective-permute-start | bytes 110600 | tf_op jit(solution)/shard_map/ppermute | solution.py:278
  6.7 6.1 %collective-permute-start.1 = (bf16[32,576]{1,0:T(8,128)(2,1)S(1)}, bf16[32,576]{1,0:T(8,128)(2,1)S(1)}, u32[]{:S(2)}, u32[]{:S(2)}) collective-permute-start(bf16[32,576]{1,0:T(8,128)(2,1)S(1)} %absorb.1.refs_0_), channel_id=1, source_target_pairs={{0,5},{1,4},{2,7},{3,6},{4,1},{5,0},{6,3},{7,2},{8,13},{9,12},{10,... | collective-permute-start | bytes 110600 | tf_op jit(solution)/shard_map/ppermute | solution.py:278
  7.6 7.9 %collective-permute-start.2 = (bf16[32,576]{1,0:T(8,128)(2,1)S(1)}, bf16[32,576]{1,0:T(8,128)(2,1)S(1)}, u32[]{:S(2)}, u32[]{:S(2)}) collective-permute-start(bf16[32,576]{1,0:T(8,128)(2,1)S(1)} %absorb.1.refs_0_), channel_id=1, source_target_pairs={{0,6},{1,7},{2,4},{3,5},{4,2},{5,3},{6,0},{7,1},{8,14},{9,15},{10,... | collective-permute-start | bytes 110600 | tf_op jit(solution)/shard_map/ppermute | solution.py:278
  9.9 5.5 %collective-permute-start = (bf16[32,576]{1,0:T(8,128)(2,1)S(1)}, bf16[32,576]{1,0:T(8,128)(2,1)S(1)}, u32[]{:S(2)}, u32[]{:S(2)}) collective-permute-start(bf16[32,576]{1,0:T(8,128)(2,1)S(1)} %absorb.1.refs_0_), channel_id=1, source_target_pairs={{0,3},{1,2},{2,1},{3,0},{4,7},{5,6},{6,5},{7,4},{8,11},{9,10},{10,... | collective-permute-start | bytes 110600 | tf_op jit(solution)/shard_map/ppermute | solution.py:278
  9.9 5.6 %collective-permute-start.6 = (bf16[32,576]{1,0:T(8,128)(2,1)S(1)}, bf16[32,576]{1,0:T(8,128)(2,1)S(1)}, u32[]{:S(2)}, u32[]{:S(2)}) collective-permute-start(bf16[32,576]{1,0:T(8,128)(2,1)S(1)} %collective-permute-done.5.refs_6_), channel_id=1, source_target_pairs={{0,3},{1,2},{2,1},{3,0},{4,7},{5,6},{6,5},{7,4},{8,11},{9,10},{10,... | collective-permute-start | bytes 110600 | tf_op jit(solution)/shard_map/ppermute | solution.py:278
  11.7 4.0 %collective-permute-start.4 = (bf16[32,576]{1,0:T(8,128)(2,1)S(1)}, bf16[32,576]{1,0:T(8,128)(2,1)S(1)}, u32[]{:S(2)}, u32[]{:S(2)}) collective-permute-start(bf16[32,576]{1,0:T(8,128)(2,1)S(1)} %collective-permute-done.3.refs_4_), channel_id=1, source_target_pairs={{0,3},{1,2},{2,1},{3,0},{4,7},{5,6},{6,5},{7,4},{8,11},{9,10},{10,... | collective-permute-start | bytes 110600 | tf_op jit(solution)/shard_map/ppermute | solution.py:278
  15.7 13.8 %copy-start = (bf16[8,512,128]{2,1,0:T(8,128)(2,1)S(1)}, bf16[8,512,128]{2,1,0:T(8,128)(2,1)}, u32[]{:S(2)}) copy-start(bf16[8,512,128]{2,1,0:T(8,128)(2,1)} %w_ref.1) | copy-start | bytes 3145732
  17.3 3.6 %collective-permute-start.8 = (bf16[32,640]{1,0:T(8,128)(2,1)S(1)}, bf16[32,640]{1,0:T(8,128)(2,1)S(1)}, u32[]{:S(2)}, u32[]{:S(2)}) collective-permute-start(bf16[32,640]{1,0:T(8,128)(2,1)S(1)} %get-tuple-element.21), channel_id=1, source_target_pairs={{0,3},{1,2},{2,1},{3,0},{4,7},{5,6},{6,5},{7,4},{8,11},{9,10},{10,... | collective-permute-start | bytes 122888 | tf_op jit(solution)/shard_map/ppermute | solution.py:278
  17.9 5.8 %collective-permute-start.10 = (bf16[32,640]{1,0:T(8,128)(2,1)S(1)}, bf16[32,640]{1,0:T(8,128)(2,1)S(1)}, u32[]{:S(2)}, u32[]{:S(2)}) collective-permute-start(bf16[32,640]{1,0:T(8,128)(2,1)S(1)} %get-tuple-element.23), channel_id=1, source_target_pairs={{0,3},{1,2},{2,1},{3,0},{4,7},{5,6},{6,5},{7,4},{8,11},{9,10},{10,... | collective-permute-start | bytes 122888 | tf_op jit(solution)/shard_map/ppermute | solution.py:278
  19.1 5.3 %collective-permute-start.12 = (bf16[32,640]{1,0:T(8,128)(2,1)S(1)}, bf16[32,640]{1,0:T(8,128)(2,1)S(1)}, u32[]{:S(2)}, u32[]{:S(2)}) collective-permute-start(bf16[32,640]{1,0:T(8,128)(2,1)S(1)} %get-tuple-element.25), channel_id=1, source_target_pairs={{0,3},{1,2},{2,1},{3,0},{4,7},{5,6},{6,5},{7,4},{8,11},{9,10},{10,... | collective-permute-start | bytes 122888 | tf_op jit(solution)/shard_map/ppermute | solution.py:278
  19.6 8.6 %collective-permute-start.7 = (bf16[32,640]{1,0:T(8,128)(2,1)S(1)}, bf16[32,640]{1,0:T(8,128)(2,1)S(1)}, u32[]{:S(2)}, u32[]{:S(2)}) collective-permute-start(bf16[32,640]{1,0:T(8,128)(2,1)S(1)} %get-tuple-element.20), channel_id=1, source_target_pairs={{0,3},{1,2},{2,1},{3,0},{4,7},{5,6},{6,5},{7,4},{8,11},{9,10},{10,... | collective-permute-start | bytes 122888 | tf_op jit(solution)/shard_map/ppermute | solution.py:278
  21.1 7.2 %collective-permute-start.9 = (bf16[32,640]{1,0:T(8,128)(2,1)S(1)}, bf16[32,640]{1,0:T(8,128)(2,1)S(1)}, u32[]{:S(2)}, u32[]{:S(2)}) collective-permute-start(bf16[32,640]{1,0:T(8,128)(2,1)S(1)} %merge_pair.3), channel_id=1, source_target_pairs={{0,13},{1,12},{2,15},{3,14},{4,9},{5,8},{6,11},{7,10},{8,5},{9,4},... | collective-permute-start | bytes 122888 | tf_op jit(solution)/shard_map/ppermute | solution.py:278
  23.9 5.5 %collective-permute-start.11 = (bf16[32,640]{1,0:T(8,128)(2,1)S(1)}, bf16[32,640]{1,0:T(8,128)(2,1)S(1)}, u32[]{:S(2)}, u32[]{:S(2)}) collective-permute-start(bf16[32,640]{1,0:T(8,128)(2,1)S(1)} %merge_pair.4), channel_id=1, source_target_pairs={{0,9},{1,8},{2,11},{3,10},{4,13},{5,12},{6,15},{7,14},{8,1},{9,0},... | collective-permute-start | bytes 122888 | tf_op jit(solution)/shard_map/ppermute | solution.py:278
  24.5 4.9 %collective-permute-start.13 = (bf16[32,640]{1,0:T(8,128)(2,1)S(1)}, bf16[32,640]{1,0:T(8,128)(2,1)S(1)}, u32[]{:S(2)}, u32[]{:S(2)}) collective-permute-start(bf16[32,640]{1,0:T(8,128)(2,1)S(1)} %merge_pair.5.refs_10_), channel_id=1, source_target_pairs={{0,5},{1,4},{2,7},{3,6},{4,1},{5,0},{6,3},{7,2},{8,13},{9,12},{10,... | collective-permute-start | bytes 122888 | tf_op jit(solution)/shard_map/ppermute | solution.py:278
  26.4 1.2 %collective-permute-start.14 = (f32[4,8,8]{2,1,0:T(8,128)S(1)}, f32[4,8,8]{2,1,0:T(8,128)S(1)}, u32[]{:S(2)}, u32[]{:S(2)}) collective-permute-start(f32[4,8,8]{2,1,0:T(8,128)S(1)} %page_bounds.1.mine_ref), channel_id=1, source_target_pairs={{0,1},{1,0},{2,3},{3,2},{4,5},{5,4},{6,7},{7,6},{8,9},{9,8},{10,11... | collective-permute-start | bytes 3080 | tf_op jit(solution)/shard_map/ppermute | solution.py:358

commit v5 on v4

--- a/solution.py
+++ b/solution.py
@@ -135,11 +135,14 @@
     requests, _, tokens = cache_ref.shape
     groups = mask_ref.shape[0] // requests
     blocks = [b[...].astype(F32) for b in block_refs]
-    outs, sums = [], []
+    scores = [
+        jnp.dot(
+            queries_of(blocks, r, heads).astype(BF16), cache_ref[r], preferred_element_type=F32
+        )
+        for r in range(requests)
+    ]
+    weights, shares, sums = [], [], []
     for r in range(requests):
-        query = queries_of(blocks, r, heads).astype(BF16)
-        keys = cache_ref[r]
-        scores = jnp.dot(query, keys, preferred_element_type=F32)
         mask = jnp.concatenate(
             [
                 jnp.broadcast_to(
@@ -149,13 +152,17 @@
             ],
             axis=0,
         )
-        scores = jnp.where(mask > 0.5, scores, NEG)
-        top = jnp.max(scores, axis=1, keepdims=True)
-        weights = jnp.exp2((scores - top) * (scale * LOG2E)).astype(BF16)
-        total = jnp.sum(weights.astype(F32), axis=1, keepdims=True)
-        weighted = jnp.dot(weights, slots_ref[r], preferred_element_type=F32)
-        outs.append(weighted * (1.0 / total))
+        masked = jnp.where(mask > 0.5, scores[r], NEG)
+        top = jnp.max(masked, axis=1, keepdims=True)
+        weight = jnp.exp2((masked - top) * (scale * LOG2E)).astype(BF16)
+        total = jnp.sum(weight.astype(F32), axis=1, keepdims=True)
+        weights.append(weight)
+        shares.append(1.0 / total)
         sums.append(top * scale + jnp.log(total))
+    outs = [
+        jnp.dot(weights[r], slots_ref[r], preferred_element_type=F32) * shares[r]
+        for r in range(requests)
+    ]
     for i, k in enumerate(offsets):
         rows = slice(i * heads, (i + 1) * heads)
         out = jnp.concatenate([o[rows] for o in outs], axis=0)

time: 30.8 us -> 30.1 us (0.977)
  Pallas kernels: 8.22 us -> 7.54 us
    pallas_call x1, Pallas kernels: 1.62 us -> 0.94 us  [local(): pl.pallas_call(functools.partial(attend_kernel, scale, heads, offsets, la...]
  transfers between devices with their start and end apart: 15 -> 15, of which waited for: 4 -> 3; matrix products, arithmetic and copies ran while one was open for 0% -> 0% of each run, Pallas kernels for 14% -> 14%
where the time goes in v5:
time: 30.1 us; the launch traced here: 29.8 us
  starting transfers between devices  19 us (63%)
  Pallas kernels  7.54 us (25%)
  waiting for transfers between devices  2.59 us (9%)
  between operations  0.72 us (2%)
    ppermute x14, starting transfers between devices, swap(): return lax.ppermute(x, ('seq', 'head'), pairs)  18.9 us
    pallas_call x1, Pallas kernels, local(): pl.pallas_call(stage_kernel, out_shape=(jax.ShapeDtypeStruct(slots.shape,...  2.66 us
    pallas_call x1, Pallas kernels, local(): pl.pallas_call(absorb_kernel, out_shape=jax.ShapeDtypeStruct((rows, width...  1.46 us
    ppermute x14, waiting for transfers between devices, swap(): return lax.ppermute(x, ('seq', 'head'), pairs)  1.42 us
    ppermute x1, waiting for transfers between devices, local(): lax.ppermute(bounds, 'head', [(i, i ^ 1) for i in range(head_count)])  1.17 us
    pallas_call x1, Pallas kernels, local(): pl.pallas_call(functools.partial(value_kernel, latent, heads), out_shape=...  1.02 us
    pallas_call x1, Pallas kernels, local(): pl.pallas_call(functools.partial(attend_kernel, scale, heads, offsets, la...  0.94 us
    pallas_call x1, Pallas kernels, local(): pl.pallas_call(largest_kernel, out_shape=jax.ShapeDtypeStruct((requests,...  0.61 us
  transfers between devices with their start and end apart: 15, of which 3 were waited for; matrix products, arithmetic and copies ran while one was open for 0% of the time, Pallas kernels for 14%

profile of v5, /device:TPU:0, one launch (start us, length us, event | category | flops | bytes accessed | tf_op | source)
XLA Modules:
  0.0 29.8 jit_solution(384919160376660825)
XLA Ops:
  0.6 1.5 %absorb.1.refs_0_ = bf16[32,576]{1,0:T(8,128)(2,1)S(1)} custom-call(bf16[4,8,128]{2,1,0:T(8,128)(2,1)} %nope_hbm.1, bf16[4,8,64]{2,1,0:T(8,128)(2,1)} %rope_hbm.1, bf16[8,128,512]{2,1,0:T(8,128)(2,1)} %w_hbm.1), custom_call_target="tpu_custom_call" | custom-call | tf_op jit(solution)/shard_map/absorb/pallas_call | solution.py:287
  2.1 4.6 %collective-permute-start.5 = (bf16[32,576]{1,0:T(8,128)(2,1)S(1)}, bf16[32,576]{1,0:T(8,128)(2,1)S(1)}, u32[]{:S(2)}, u32[]{:S(2)}) collective-permute-start(bf16[32,576]{1,0:T(8,128)(2,1)S(1)} %absorb.1.refs_0_), channel_id=1, source_target_pairs={{0,13},{1,12},{2,15},{3,14},{4,9},{5,8},{6,11},{7,10},{8,5},{9,4},... | collective-permute-start | bytes 110600 | tf_op jit(solution)/shard_map/ppermute | solution.py:285
  6.7 0.0 collective-permute-start.3
  6.7 0.9 %collective-permute-start.1 = (bf16[32,576]{1,0:T(8,128)(2,1)S(1)}, bf16[32,576]{1,0:T(8,128)(2,1)S(1)}, u32[]{:S(2)}, u32[]{:S(2)}) collective-permute-start(bf16[32,576]{1,0:T(8,128)(2,1)S(1)} %absorb.1.refs_0_), channel_id=1, source_target_pairs={{0,5},{1,4},{2,7},{3,6},{4,1},{5,0},{6,3},{7,2},{8,13},{9,12},{10,... | collective-permute-start | bytes 110600 | tf_op jit(solution)/shard_map/ppermute | solution.py:285
  7.6 2.3 %collective-permute-start.2 = (bf16[32,576]{1,0:T(8,128)(2,1)S(1)}, bf16[32,576]{1,0:T(8,128)(2,1)S(1)}, u32[]{:S(2)}, u32[]{:S(2)}) collective-permute-start(bf16[32,576]{1,0:T(8,128)(2,1)S(1)} %absorb.1.refs_0_), channel_id=1, source_target_pairs={{0,6},{1,7},{2,4},{3,5},{4,2},{5,3},{6,0},{7,1},{8,14},{9,15},{10,... | collective-permute-start | bytes 110600 | tf_op jit(solution)/shard_map/ppermute | solution.py:285
  9.9 0.0 collective-permute-start
  9.9 0.0 collective-permute-done.5.refs_6_
  9.9 1.7 %collective-permute-start.6 = (bf16[32,576]{1,0:T(8,128)(2,1)S(1)}, bf16[32,576]{1,0:T(8,128)(2,1)S(1)}, u32[]{:S(2)}, u32[]{:S(2)}) collective-permute-start(bf16[32,576]{1,0:T(8,128)(2,1)S(1)} %collective-permute-done.5.refs_6_), channel_id=1, source_target_pairs={{0,3},{1,2},{2,1},{3,0},{4,7},{5,6},{6,5},{7,4},{8,11},{9,10},{10,... | collective-permute-start | bytes 110600 | tf_op jit(solution)/shard_map/ppermute | solution.py:285
  11.7 0.0 collective-permute-done.3.refs_4_
  11.7 1.1 %collective-permute-start.4 = (bf16[32,576]{1,0:T(8,128)(2,1)S(1)}, bf16[32,576]{1,0:T(8,128)(2,1)S(1)}, u32[]{:S(2)}, u32[]{:S(2)}) collective-permute-start(bf16[32,576]{1,0:T(8,128)(2,1)S(1)} %collective-permute-done.3.refs_4_), channel_id=1, source_target_pairs={{0,3},{1,2},{2,1},{3,0},{4,7},{5,6},{6,5},{7,4},{8,11},{9,10},{10,... | collective-permute-start | bytes 110600 | tf_op jit(solution)/shard_map/ppermute | solution.py:285
  12.8 0.0 collective-permute-done.1.after_ref.refs_2_
  12.8 2.7 %stage_cache.1 = (bf16[4,576,512]{2,1,0:T(8,128)(2,1)S(1)}, bf16[4,512,512]{2,1,0:T(8,128)(2,1)S(1)}, f32[32,512]{1,0:T(8,128)S(1)}, f32[4,8,576]{2,1,0:T(8,128)...) custom-call(bf16[4,576,512]{2,1,0:T(8,128)(2,1)} %bitcast.1, s32[4,8,32]{2,1,0:T(8,128)} %selected_hbm.1, ...), custom_call_target="tpu_custom_call" | custom-call | tf_op jit(solution)/shard_map/stage_cache/pallas_call | solution.py:311
  15.5 0.0 collective-permute-done.2.refs_3_
  15.5 0.0 collective-permute-done.refs_1_
  15.5 0.0 collective-permute-done.6.refs_7_
  15.5 0.2 collective-permute-done.4.refs_5_
  15.7 0.0 copy-start
  15.7 0.9 %attend.1 = (f32[32,640]{1,0:T(8,128)S(1)}, bf16[32,640]{1,0:T(8,128)(2,1)S(1)}, f32[32,640]{1,0:T(8,128)S(1)}, bf16[32,640]{1,0:T(8,128)(2,1)S(1)}, f32[32,640]...) custom-call(bf16[32,576]{1,0:T(8,128)(2,1)S(1)} %absorb.1.refs_0_, ...), custom_call_target="tpu_custom_call" | custom-call | tf_op jit(solution)/shard_map/attend/pallas_call | solution.py:332
  16.6 0.6 %collective-permute-start.8 = (bf16[32,640]{1,0:T(8,128)(2,1)S(1)}, bf16[32,640]{1,0:T(8,128)(2,1)S(1)}, u32[]{:S(2)}, u32[]{:S(2)}) collective-permute-start(bf16[32,640]{1,0:T(8,128)(2,1)S(1)} %get-tuple-element.21), channel_id=1, source_target_pairs={{0,3},{1,2},{2,1},{3,0},{4,7},{5,6},{6,5},{7,4},{8,11},{9,10},{10,... | collective-permute-start | bytes 122888 | tf_op jit(solution)/shard_map/ppermute | solution.py:285
  17.2 1.2 %collective-permute-start.10 = (bf16[32,640]{1,0:T(8,128)(2,1)S(1)}, bf16[32,640]{1,0:T(8,128)(2,1)S(1)}, u32[]{:S(2)}, u32[]{:S(2)}) collective-permute-start(bf16[32,640]{1,0:T(8,128)(2,1)S(1)} %get-tuple-element.23), channel_id=1, source_target_pairs={{0,3},{1,2},{2,1},{3,0},{4,7},{5,6},{6,5},{7,4},{8,11},{9,10},{10,... | collective-permute-start | bytes 122888 | tf_op jit(solution)/shard_map/ppermute | solution.py:285
  18.4 0.5 %collective-permute-start.12 = (bf16[32,640]{1,0:T(8,128)(2,1)S(1)}, bf16[32,640]{1,0:T(8,128)(2,1)S(1)}, u32[]{:S(2)}, u32[]{:S(2)}) collective-permute-start(bf16[32,640]{1,0:T(8,128)(2,1)S(1)} %get-tuple-element.25), channel_id=1, source_target_pairs={{0,3},{1,2},{2,1},{3,0},{4,7},{5,6},{6,5},{7,4},{8,11},{9,10},{10,... | collective-permute-start | bytes 122888 | tf_op jit(solution)/shard_map/ppermute | solution.py:285
  19.0 1.2 %collective-permute-start.7 = (bf16[32,640]{1,0:T(8,128)(2,1)S(1)}, bf16[32,640]{1,0:T(8,128)(2,1)S(1)}, u32[]{:S(2)}, u32[]{:S(2)}) collective-permute-start(bf16[32,640]{1,0:T(8,128)(2,1)S(1)} %get-tuple-element.20), channel_id=1, source_target_pairs={{0,3},{1,2},{2,1},{3,0},{4,7},{5,6},{6,5},{7,4},{8,11},{9,10},{10,... | collective-permute-start | bytes 122888 | tf_op jit(solution)/shard_map/ppermute | solution.py:285
  20.2 0.0 collective-permute-done.8.got_ref
  20.2 0.2 merge_pair.3
  20.4 2.7 %collective-permute-start.9 = (bf16[32,640]{1,0:T(8,128)(2,1)S(1)}, bf16[32,640]{1,0:T(8,128)(2,1)S(1)}, u32[]{:S(2)}, u32[]{:S(2)}) collective-permute-start(bf16[32,640]{1,0:T(8,128)(2,1)S(1)} %merge_pair.3), channel_id=1, source_target_pairs={{0,13},{1,12},{2,15},{3,14},{4,9},{5,8},{6,11},{7,10},{8,5},{9,4},... | collective-permute-start | bytes 122888 | tf_op jit(solution)/shard_map/ppermute | solution.py:285
  23.1 0.0 collective-permute-done.10.got_ref
  23.1 0.2 merge_pair.4
  23.3 0.4 %collective-permute-start.11 = (bf16[32,640]{1,0:T(8,128)(2,1)S(1)}, bf16[32,640]{1,0:T(8,128)(2,1)S(1)}, u32[]{:S(2)}, u32[]{:S(2)}) collective-permute-start(bf16[32,640]{1,0:T(8,128)(2,1)S(1)} %merge_pair.4), channel_id=1, source_target_pairs={{0,9},{1,8},{2,11},{3,10},{4,13},{5,12},{6,15},{7,14},{8,1},{9,0},... | collective-permute-start | bytes 122888 | tf_op jit(solution)/shard_map/ppermute | solution.py:285
  23.7 0.0 collective-permute-done.12.got_ref
  23.7 0.2 merge_pair.5.refs_10_
  23.9 1.5 %collective-permute-start.13 = (bf16[32,640]{1,0:T(8,128)(2,1)S(1)}, bf16[32,640]{1,0:T(8,128)(2,1)S(1)}, u32[]{:S(2)}, u32[]{:S(2)}) collective-permute-start(bf16[32,640]{1,0:T(8,128)(2,1)S(1)} %merge_pair.5.refs_10_), channel_id=1, source_target_pairs={{0,5},{1,4},{2,7},{3,6},{4,1},{5,0},{6,3},{7,2},{8,13},{9,12},{10,... | collective-permute-start | bytes 122888 | tf_op jit(solution)/shard_map/ppermute | solution.py:285
  25.4 0.3 %page_bounds.1.mine_ref = f32[4,8,8]{2,1,0:T(8,128)S(1)} custom-call(bf16[32,576]{1,0:T(8,128)(2,1)S(1)} %absorb.1.refs_0_, bf16[32,576]{1,0:T(8,128)(2,1)S(1)} %collective-permute-done.refs_1_, bf16[32,576]{1,0:T(8,128)(2,1)S(1)} %collective-permute-done.1.after_ref.refs_2_, bf16[32,576]{1,0:T(8,128)(2,1)S(1)} %collective-permute-done.2.refs_3_, ...), custom_call_target="tpu_custom_call" | custom-call | tf_op jit(solution)/shard_map/page_bounds/pallas_call | solution.py:357
  25.7 0.1 collective-permute-start.14
  25.8 1.2 %collective-permute-done.14.other_ref = f32[4,8,8]{2,1,0:T(8,128)S(1)} collective-permute-done((f32[4,8,8]{2,1,0:T(8,128)S(1)}, f32[4,8,8]{2,1,0:T(8,128)S(1)}, u32[]{:S(2)}, u32[]{:S(2)}) %collective-permute-start.14) | collective-permute-done | bytes 1056 | tf_op jit(solution)/shard_map/ppermute | solution.py:365
  27.0 0.6 %group_bounds.1 = f32[4,8,8]{2,1,0:T(8,128)} custom-call(f32[4,8,8]{2,1,0:T(8,128)S(1)} %page_bounds.1.mine_ref, f32[4,8,8]{2,1,0:T(8,128)S(1)} %collective-permute-done.14.other_ref, f32[4,8,8]{2,1,0:T(8,128)S(1)} %get-tuple-element.29.live_ref), custom_call_target="tpu_custom_call" | custom-call | tf_op jit(solution)/shard_map/group_bounds/pallas_call | solution.py:366
  27.6 0.0 collective-permute-done.7.refs_1_
  27.6 0.0 collective-permute-done.9.refs_2_
  27.6 1.2 %collective-permute-done.11.refs_3_ = bf16[32,640]{1,0:T(8,128)(2,1)S(1)} collective-permute-done((bf16[32,640]{1,0:T(8,128)(2,1)S(1)}, bf16[32,640]{1,0:T(8,128)(2,1)S(1)}, u32[]{:S(2)}, u32[]{:S(2)}) %collective-permute-start.11) | collective-permute-done | bytes 40992 | tf_op jit(solution)/shard_map/ppermute | solution.py:285
  28.8 0.0 collective-permute-done.13.refs_4_
  28.8 0.0 copy-done
  28.8 1.0 %merge_and_value.1 = bf16[4,8,128]{2,1,0:T(8,128)(2,1)} custom-call(bf16[8,512,128]{2,1,0:T(8,128)(2,1)S(1)} %copy-done, f32[32,640]{1,0:T(8,128)S(1)} %get-tuple-element.19.refs_0_, bf16[32,640]{1,0:T(8,128)(2,1)S(1)} %collective-permute-done.7.refs_1_, bf16[32,640]{1,0:T(8,128)(2,1)S(1)} %collective-permute-done.9.refs_2_, ...), custom_call_target="tpu_custom_call" | custom-call | tf_op jit(solution)/shard_map/merge_and_value/pallas_call | solution.py:375
Async XLA Ops:
  2.1 7.8 %collective-permute-start.5 = (bf16[32,576]{1,0:T(8,128)(2,1)S(1)}, bf16[32,576]{1,0:T(8,128)(2,1)S(1)}, u32[]{:S(2)}, u32[]{:S(2)}) collective-permute-start(bf16[32,576]{1,0:T(8,128)(2,1)S(1)} %absorb.1.refs_0_), channel_id=1, source_target_pairs={{0,13},{1,12},{2,15},{3,14},{4,9},{5,8},{6,11},{7,10},{8,5},{9,4},... | collective-permute-start | bytes 110600 | tf_op jit(solution)/shard_map/ppermute | solution.py:285
  6.7 5.0 %collective-permute-start.3 = (bf16[32,576]{1,0:T(8,128)(2,1)S(1)}, bf16[32,576]{1,0:T(8,128)(2,1)S(1)}, u32[]{:S(2)}, u32[]{:S(2)}) collective-permute-start(bf16[32,576]{1,0:T(8,128)(2,1)S(1)} %absorb.1.refs_0_), channel_id=1, source_target_pairs={{0,9},{1,8},{2,11},{3,10},{4,13},{5,12},{6,15},{7,14},{8,1},{9,0},... | collective-permute-start | bytes 110600 | tf_op jit(solution)/shard_map/ppermute | solution.py:285
  6.7 6.1 %collective-permute-start.1 = (bf16[32,576]{1,0:T(8,128)(2,1)S(1)}, bf16[32,576]{1,0:T(8,128)(2,1)S(1)}, u32[]{:S(2)}, u32[]{:S(2)}) collective-permute-start(bf16[32,576]{1,0:T(8,128)(2,1)S(1)} %absorb.1.refs_0_), channel_id=1, source_target_pairs={{0,5},{1,4},{2,7},{3,6},{4,1},{5,0},{6,3},{7,2},{8,13},{9,12},{10,... | collective-permute-start | bytes 110600 | tf_op jit(solution)/shard_map/ppermute | solution.py:285
  7.6 7.9 %collective-permute-start.2 = (bf16[32,576]{1,0:T(8,128)(2,1)S(1)}, bf16[32,576]{1,0:T(8,128)(2,1)S(1)}, u32[]{:S(2)}, u32[]{:S(2)}) collective-permute-start(bf16[32,576]{1,0:T(8,128)(2,1)S(1)} %absorb.1.refs_0_), channel_id=1, source_target_pairs={{0,6},{1,7},{2,4},{3,5},{4,2},{5,3},{6,0},{7,1},{8,14},{9,15},{10,... | collective-permute-start | bytes 110600 | tf_op jit(solution)/shard_map/ppermute | solution.py:285
  9.9 5.5 %collective-permute-start = (bf16[32,576]{1,0:T(8,128)(2,1)S(1)}, bf16[32,576]{1,0:T(8,128)(2,1)S(1)}, u32[]{:S(2)}, u32[]{:S(2)}) collective-permute-start(bf16[32,576]{1,0:T(8,128)(2,1)S(1)} %absorb.1.refs_0_), channel_id=1, source_target_pairs={{0,3},{1,2},{2,1},{3,0},{4,7},{5,6},{6,5},{7,4},{8,11},{9,10},{10,... | collective-permute-start | bytes 110600 | tf_op jit(solution)/shard_map/ppermute | solution.py:285
  9.9 5.6 %collective-permute-start.6 = (bf16[32,576]{1,0:T(8,128)(2,1)S(1)}, bf16[32,576]{1,0:T(8,128)(2,1)S(1)}, u32[]{:S(2)}, u32[]{:S(2)}) collective-permute-start(bf16[32,576]{1,0:T(8,128)(2,1)S(1)} %collective-permute-done.5.refs_6_), channel_id=1, source_target_pairs={{0,3},{1,2},{2,1},{3,0},{4,7},{5,6},{6,5},{7,4},{8,11},{9,10},{10,... | collective-permute-start | bytes 110600 | tf_op jit(solution)/shard_map/ppermute | solution.py:285
  11.7 4.0 %collective-permute-start.4 = (bf16[32,576]{1,0:T(8,128)(2,1)S(1)}, bf16[32,576]{1,0:T(8,128)(2,1)S(1)}, u32[]{:S(2)}, u32[]{:S(2)}) collective-permute-start(bf16[32,576]{1,0:T(8,128)(2,1)S(1)} %collective-permute-done.3.refs_4_), channel_id=1, source_target_pairs={{0,3},{1,2},{2,1},{3,0},{4,7},{5,6},{6,5},{7,4},{8,11},{9,10},{10,... | collective-permute-start | bytes 110600 | tf_op jit(solution)/shard_map/ppermute | solution.py:285
  15.7 13.1 %copy-start = (bf16[8,512,128]{2,1,0:T(8,128)(2,1)S(1)}, bf16[8,512,128]{2,1,0:T(8,128)(2,1)}, u32[]{:S(2)}) copy-start(bf16[8,512,128]{2,1,0:T(8,128)(2,1)} %w_ref.1) | copy-start | bytes 3145732
  16.6 3.6 %collective-permute-start.8 = (bf16[32,640]{1,0:T(8,128)(2,1)S(1)}, bf16[32,640]{1,0:T(8,128)(2,1)S(1)}, u32[]{:S(2)}, u32[]{:S(2)}) collective-permute-start(bf16[32,640]{1,0:T(8,128)(2,1)S(1)} %get-tuple-element.21), channel_id=1, source_target_pairs={{0,3},{1,2},{2,1},{3,0},{4,7},{5,6},{6,5},{7,4},{8,11},{9,10},{10,... | collective-permute-start | bytes 122888 | tf_op jit(solution)/shard_map/ppermute | solution.py:285
  17.2 5.8 %collective-permute-start.10 = (bf16[32,640]{1,0:T(8,128)(2,1)S(1)}, bf16[32,640]{1,0:T(8,128)(2,1)S(1)}, u32[]{:S(2)}, u32[]{:S(2)}) collective-permute-start(bf16[32,640]{1,0:T(8,128)(2,1)S(1)} %get-tuple-element.23), channel_id=1, source_target_pairs={{0,3},{1,2},{2,1},{3,0},{4,7},{5,6},{6,5},{7,4},{8,11},{9,10},{10,... | collective-permute-start | bytes 122888 | tf_op jit(solution)/shard_map/ppermute | solution.py:285
  18.4 5.2 %collective-permute-start.12 = (bf16[32,640]{1,0:T(8,128)(2,1)S(1)}, bf16[32,640]{1,0:T(8,128)(2,1)S(1)}, u32[]{:S(2)}, u32[]{:S(2)}) collective-permute-start(bf16[32,640]{1,0:T(8,128)(2,1)S(1)} %get-tuple-element.25), channel_id=1, source_target_pairs={{0,3},{1,2},{2,1},{3,0},{4,7},{5,6},{6,5},{7,4},{8,11},{9,10},{10,... | collective-permute-start | bytes 122888 | tf_op jit(solution)/shard_map/ppermute | solution.py:285
  19.0 8.6 %collective-permute-start.7 = (bf16[32,640]{1,0:T(8,128)(2,1)S(1)}, bf16[32,640]{1,0:T(8,128)(2,1)S(1)}, u32[]{:S(2)}, u32[]{:S(2)}) collective-permute-start(bf16[32,640]{1,0:T(8,128)(2,1)S(1)} %get-tuple-element.20), channel_id=1, source_target_pairs={{0,3},{1,2},{2,1},{3,0},{4,7},{5,6},{6,5},{7,4},{8,11},{9,10},{10,... | collective-permute-start | bytes 122888 | tf_op jit(solution)/shard_map/ppermute | solution.py:285
  20.4 7.2 %collective-permute-start.9 = (bf16[32,640]{1,0:T(8,128)(2,1)S(1)}, bf16[32,640]{1,0:T(8,128)(2,1)S(1)}, u32[]{:S(2)}, u32[]{:S(2)}) collective-permute-start(bf16[32,640]{1,0:T(8,128)(2,1)S(1)} %merge_pair.3), channel_id=1, source_target_pairs={{0,13},{1,12},{2,15},{3,14},{4,9},{5,8},{6,11},{7,10},{8,5},{9,4},... | collective-permute-start | bytes 122888 | tf_op jit(solution)/shard_map/ppermute | solution.py:285
  23.3 5.5 %collective-permute-start.11 = (bf16[32,640]{1,0:T(8,128)(2,1)S(1)}, bf16[32,640]{1,0:T(8,128)(2,1)S(1)}, u32[]{:S(2)}, u32[]{:S(2)}) collective-permute-start(bf16[32,640]{1,0:T(8,128)(2,1)S(1)} %merge_pair.4), channel_id=1, source_target_pairs={{0,9},{1,8},{2,11},{3,10},{4,13},{5,12},{6,15},{7,14},{8,1},{9,0},... | collective-permute-start | bytes 122888 | tf_op jit(solution)/shard_map/ppermute | solution.py:285
  23.9 4.9 %collective-permute-start.13 = (bf16[32,640]{1,0:T(8,128)(2,1)S(1)}, bf16[32,640]{1,0:T(8,128)(2,1)S(1)}, u32[]{:S(2)}, u32[]{:S(2)}) collective-permute-start(bf16[32,640]{1,0:T(8,128)(2,1)S(1)} %merge_pair.5.refs_10_), channel_id=1, source_target_pairs={{0,5},{1,4},{2,7},{3,6},{4,1},{5,0},{6,3},{7,2},{8,13},{9,12},{10,... | collective-permute-start | bytes 122888 | tf_op jit(solution)/shard_map/ppermute | solution.py:285
  25.7 1.2 %collective-permute-start.14 = (f32[4,8,8]{2,1,0:T(8,128)S(1)}, f32[4,8,8]{2,1,0:T(8,128)S(1)}, u32[]{:S(2)}, u32[]{:S(2)}) collective-permute-start(f32[4,8,8]{2,1,0:T(8,128)S(1)} %page_bounds.1.mine_ref), channel_id=1, source_target_pairs={{0,1},{1,0},{2,3},{3,2},{4,5},{5,4},{6,7},{7,6},{8,9},{9,8},{10,11... | collective-permute-start | bytes 3080 | tf_op jit(solution)/shard_map/ppermute | solution.py:365

commit v6 on v5

--- a/solution.py
+++ b/solution.py
@@ -167,23 +167,13 @@
         rows = slice(i * heads, (i + 1) * heads)
         out = jnp.concatenate([o[rows] for o in outs], axis=0)
         lse = jnp.concatenate([s[rows] for s in sums], axis=0)
-        fill(out_refs[i], out, lse)
+        fill(out_refs[i], out, jnp.broadcast_to(lse, (lse.shape[0], LANES)))
 
 
 def fill(ref, out, lse):
     latent = out.shape[1]
-    lse = jnp.broadcast_to(lse, (lse.shape[0], LANES))
     ref[:, :latent] = out.astype(ref.dtype)
     ref[:, latent:] = packed(lse) if ref.dtype == BF16 else lse
-
-
-def read(ref, latent):
-    tail = ref[:, latent:].astype(F32)
-    if ref.dtype == BF16:
-        lse = tail[:, 0:1] + tail[:, 1:2] + tail[:, 2:3]
-    else:
-        lse = tail[:, 0:1]
-    return ref[:, :latent].astype(F32), lse
 
 
 def packed(lse):
@@ -192,12 +182,28 @@
     return jnp.where(lane == 0, high, jnp.where(lane == 1, middle, low)).astype(BF16)
 
 
+def read(ref, latent):
+    lse = ref[:, latent:].astype(F32)
+    if ref.dtype == BF16:
+        high, middle, low = (jnp.broadcast_to(lse[:, i : i + 1], lse.shape) for i in range(3))
+        lse = high + middle + low
+    return ref[:, :latent].astype(F32), lse
+
+
 def merge(parts):
     top = functools.reduce(jnp.maximum, [s for _, s in parts])
     factors = [jnp.exp(s - top) for _, s in parts]
     total = functools.reduce(jnp.add, factors)
-    mixed = functools.reduce(jnp.add, [f * o for f, (o, _) in zip(factors, parts)])
-    return mixed / total, top + jnp.log(total)
+    share = 1.0 / total
+    repeats = parts[0][0].shape[1] // LANES
+    mixed = functools.reduce(
+        jnp.add,
+        [
+            jnp.concatenate([factor * share] * repeats, axis=1) * out
+            for factor, (out, _) in zip(factors, parts)
+        ],
+    )
+    return mixed, top + jnp.log(total)
 
 
 def pair_kernel(latent, got_ref, keep_ref, out_ref):
@@ -209,13 +215,11 @@
     mixed = merge([read(ref, latent) for ref in part_refs])[0].astype(BF16)
     size = w_ref.shape[2]
     head = lax.broadcasted_iota(jnp.int32, (mixed.shape[0], size), 0) % heads
-    out = jnp.zeros((mixed.shape[0], size), F32)
-    step = 2 if heads % 2 == 0 else 1
-    for i in range(0, heads, step):
-        weight = jnp.concatenate([w_ref[i + j] for j in range(step)], axis=1)
-        both = jnp.dot(mixed, weight, preferred_element_type=F32)
-        for j in range(step):
-            out = jnp.where(head == i + j, both[:, j * size : (j + 1) * size], out)
+    weight = jnp.concatenate([w_ref[j] for j in range(heads)], axis=1)
+    every = jnp.dot(mixed, weight, preferred_element_type=F32)
+    out = every[:, :size]
+    for j in range(1, heads):
+        out = jnp.where(head == j, every[:, j * size : (j + 1) * size], out)
     out_ref[...] = out.reshape(out_ref.shape).astype(BF16)
 
 

time: 30.1 us -> 29.9 us (level)
  transfers between devices with their start and end apart: 15 -> 15, of which waited for: 3 -> 3; matrix products, arithmetic and copies ran while one was open for 0% -> 0% of each run, Pallas kernels for 14% -> 13%
where the time goes in v6:
time: 29.9 us; the launch traced here: 29.6 us
  starting transfers between devices  19 us (64%)
  Pallas kernels  7.29 us (24%)
  waiting for transfers between devices  2.66 us (9%)
  between operations  0.72 us (2%)
    ppermute x14, starting transfers between devices, swap(): return lax.ppermute(x, ('seq', 'head'), pairs)  18.9 us
    pallas_call x1, Pallas kernels, local(): pl.pallas_call(stage_kernel, out_shape=(jax.ShapeDtypeStruct(slots.shape,...  2.66 us
    ppermute x14, waiting for transfers between devices, swap(): return lax.ppermute(x, ('seq', 'head'), pairs)  1.49 us
    pallas_call x1, Pallas kernels, local(): pl.pallas_call(absorb_kernel, out_shape=jax.ShapeDtypeStruct((rows, width...  1.46 us
    ppermute x1, waiting for transfers between devices, local(): lax.ppermute(bounds, 'head', [(i, i ^ 1) for i in range(head_count)])  1.17 us
    pallas_call x1, Pallas kernels, local(): pl.pallas_call(functools.partial(value_kernel, latent, heads), out_shape=...  0.96 us
    pallas_call x1, Pallas kernels, local(): pl.pallas_call(functools.partial(attend_kernel, scale, heads, offsets, la...  0.94 us
    pallas_call x1, Pallas kernels, local(): pl.pallas_call(largest_kernel, out_shape=jax.ShapeDtypeStruct((requests,...  0.61 us
  transfers between devices with their start and end apart: 15, of which 3 were waited for; matrix products, arithmetic and copies ran while one was open for 0% of the time, Pallas kernels for 13%

profile of v6, /device:TPU:0, one launch (start us, length us, event | category | flops | bytes accessed | tf_op | source)
XLA Modules:
  0.0 29.6 jit_solution(17541035088573665485)
XLA Ops:
  0.6 1.5 %absorb.1.refs_0_ = bf16[32,576]{1,0:T(8,128)(2,1)S(1)} custom-call(bf16[4,8,128]{2,1,0:T(8,128)(2,1)} %nope_hbm.1, bf16[4,8,64]{2,1,0:T(8,128)(2,1)} %rope_hbm.1, bf16[8,128,512]{2,1,0:T(8,128)(2,1)} %w_hbm.1), custom_call_target="tpu_custom_call" | custom-call | tf_op jit(solution)/shard_map/absorb/pallas_call | solution.py:291
  2.1 4.6 %collective-permute-start.5 = (bf16[32,576]{1,0:T(8,128)(2,1)S(1)}, bf16[32,576]{1,0:T(8,128)(2,1)S(1)}, u32[]{:S(2)}, u32[]{:S(2)}) collective-permute-start(bf16[32,576]{1,0:T(8,128)(2,1)S(1)} %absorb.1.refs_0_), channel_id=1, source_target_pairs={{0,13},{1,12},{2,15},{3,14},{4,9},{5,8},{6,11},{7,10},{8,5},{9,4},... | collective-permute-start | bytes 110600 | tf_op jit(solution)/shard_map/ppermute | solution.py:289
  6.7 0.0 collective-permute-start.3
  6.7 0.9 %collective-permute-start.1 = (bf16[32,576]{1,0:T(8,128)(2,1)S(1)}, bf16[32,576]{1,0:T(8,128)(2,1)S(1)}, u32[]{:S(2)}, u32[]{:S(2)}) collective-permute-start(bf16[32,576]{1,0:T(8,128)(2,1)S(1)} %absorb.1.refs_0_), channel_id=1, source_target_pairs={{0,5},{1,4},{2,7},{3,6},{4,1},{5,0},{6,3},{7,2},{8,13},{9,12},{10,... | collective-permute-start | bytes 110600 | tf_op jit(solution)/shard_map/ppermute | solution.py:289
  7.6 2.3 %collective-permute-start.2 = (bf16[32,576]{1,0:T(8,128)(2,1)S(1)}, bf16[32,576]{1,0:T(8,128)(2,1)S(1)}, u32[]{:S(2)}, u32[]{:S(2)}) collective-permute-start(bf16[32,576]{1,0:T(8,128)(2,1)S(1)} %absorb.1.refs_0_), channel_id=1, source_target_pairs={{0,6},{1,7},{2,4},{3,5},{4,2},{5,3},{6,0},{7,1},{8,14},{9,15},{10,... | collective-permute-start | bytes 110600 | tf_op jit(solution)/shard_map/ppermute | solution.py:289
  9.9 0.0 collective-permute-start
  9.9 0.0 collective-permute-done.5.refs_6_
  9.9 1.7 %collective-permute-start.6 = (bf16[32,576]{1,0:T(8,128)(2,1)S(1)}, bf16[32,576]{1,0:T(8,128)(2,1)S(1)}, u32[]{:S(2)}, u32[]{:S(2)}) collective-permute-start(bf16[32,576]{1,0:T(8,128)(2,1)S(1)} %collective-permute-done.5.refs_6_), channel_id=1, source_target_pairs={{0,3},{1,2},{2,1},{3,0},{4,7},{5,6},{6,5},{7,4},{8,11},{9,10},{10,... | collective-permute-start | bytes 110600 | tf_op jit(solution)/shard_map/ppermute | solution.py:289
  11.7 0.0 collective-permute-done.3.refs_4_
  11.7 1.1 %collective-permute-start.4 = (bf16[32,576]{1,0:T(8,128)(2,1)S(1)}, bf16[32,576]{1,0:T(8,128)(2,1)S(1)}, u32[]{:S(2)}, u32[]{:S(2)}) collective-permute-start(bf16[32,576]{1,0:T(8,128)(2,1)S(1)} %collective-permute-done.3.refs_4_), channel_id=1, source_target_pairs={{0,3},{1,2},{2,1},{3,0},{4,7},{5,6},{6,5},{7,4},{8,11},{9,10},{10,... | collective-permute-start | bytes 110600 | tf_op jit(solution)/shard_map/ppermute | solution.py:289
  12.8 0.0 collective-permute-done.1.after_ref.refs_2_
  12.8 2.7 %stage_cache.1 = (bf16[4,576,512]{2,1,0:T(8,128)(2,1)S(1)}, bf16[4,512,512]{2,1,0:T(8,128)(2,1)S(1)}, f32[32,512]{1,0:T(8,128)S(1)}, f32[4,8,576]{2,1,0:T(8,128)...) custom-call(bf16[4,576,512]{2,1,0:T(8,128)(2,1)} %bitcast.1, s32[4,8,32]{2,1,0:T(8,128)} %selected_hbm.1, ...), custom_call_target="tpu_custom_call" | custom-call | tf_op jit(solution)/shard_map/stage_cache/pallas_call | solution.py:315
  15.5 0.0 collective-permute-done.2.refs_3_
  15.5 0.0 collective-permute-done.refs_1_
  15.5 0.0 collective-permute-done.6.refs_7_
  15.5 0.2 collective-permute-done.4.refs_5_
  15.7 0.0 copy-start
  15.7 0.9 %attend.1 = (f32[32,640]{1,0:T(8,128)S(1)}, bf16[32,640]{1,0:T(8,128)(2,1)S(1)}, f32[32,640]{1,0:T(8,128)S(1)}, bf16[32,640]{1,0:T(8,128)(2,1)S(1)}, f32[32,640]...) custom-call(bf16[32,576]{1,0:T(8,128)(2,1)S(1)} %absorb.1.refs_0_, ...), custom_call_target="tpu_custom_call" | custom-call | tf_op jit(solution)/shard_map/attend/pallas_call | solution.py:336
  16.6 0.6 %collective-permute-start.8 = (bf16[32,640]{1,0:T(8,128)(2,1)S(1)}, bf16[32,640]{1,0:T(8,128)(2,1)S(1)}, u32[]{:S(2)}, u32[]{:S(2)}) collective-permute-start(bf16[32,640]{1,0:T(8,128)(2,1)S(1)} %get-tuple-element.21), channel_id=1, source_target_pairs={{0,3},{1,2},{2,1},{3,0},{4,7},{5,6},{6,5},{7,4},{8,11},{9,10},{10,... | collective-permute-start | bytes 122888 | tf_op jit(solution)/shard_map/ppermute | solution.py:289
  17.2 1.2 %collective-permute-start.10 = (bf16[32,640]{1,0:T(8,128)(2,1)S(1)}, bf16[32,640]{1,0:T(8,128)(2,1)S(1)}, u32[]{:S(2)}, u32[]{:S(2)}) collective-permute-start(bf16[32,640]{1,0:T(8,128)(2,1)S(1)} %get-tuple-element.23), channel_id=1, source_target_pairs={{0,3},{1,2},{2,1},{3,0},{4,7},{5,6},{6,5},{7,4},{8,11},{9,10},{10,... | collective-permute-start | bytes 122888 | tf_op jit(solution)/shard_map/ppermute | solution.py:289
  18.4 0.5 %collective-permute-start.12 = (bf16[32,640]{1,0:T(8,128)(2,1)S(1)}, bf16[32,640]{1,0:T(8,128)(2,1)S(1)}, u32[]{:S(2)}, u32[]{:S(2)}) collective-permute-start(bf16[32,640]{1,0:T(8,128)(2,1)S(1)} %get-tuple-element.25), channel_id=1, source_target_pairs={{0,3},{1,2},{2,1},{3,0},{4,7},{5,6},{6,5},{7,4},{8,11},{9,10},{10,... | collective-permute-start | bytes 122888 | tf_op jit(solution)/shard_map/ppermute | solution.py:289
  19.0 1.2 %collective-permute-start.7 = (bf16[32,640]{1,0:T(8,128)(2,1)S(1)}, bf16[32,640]{1,0:T(8,128)(2,1)S(1)}, u32[]{:S(2)}, u32[]{:S(2)}) collective-permute-start(bf16[32,640]{1,0:T(8,128)(2,1)S(1)} %get-tuple-element.20), channel_id=1, source_target_pairs={{0,3},{1,2},{2,1},{3,0},{4,7},{5,6},{6,5},{7,4},{8,11},{9,10},{10,... | collective-permute-start | bytes 122888 | tf_op jit(solution)/shard_map/ppermute | solution.py:289
  20.2 0.0 collective-permute-done.8.got_ref
  20.2 0.1 merge_pair.3
  20.4 2.7 %collective-permute-start.9 = (bf16[32,640]{1,0:T(8,128)(2,1)S(1)}, bf16[32,640]{1,0:T(8,128)(2,1)S(1)}, u32[]{:S(2)}, u32[]{:S(2)}) collective-permute-start(bf16[32,640]{1,0:T(8,128)(2,1)S(1)} %merge_pair.3), channel_id=1, source_target_pairs={{0,13},{1,12},{2,15},{3,14},{4,9},{5,8},{6,11},{7,10},{8,5},{9,4},... | collective-permute-start | bytes 122888 | tf_op jit(solution)/shard_map/ppermute | solution.py:289
  23.0 0.0 collective-permute-done.10.got_ref
  23.0 0.1 merge_pair.4
  23.1 0.5 %collective-permute-start.11 = (bf16[32,640]{1,0:T(8,128)(2,1)S(1)}, bf16[32,640]{1,0:T(8,128)(2,1)S(1)}, u32[]{:S(2)}, u32[]{:S(2)}) collective-permute-start(bf16[32,640]{1,0:T(8,128)(2,1)S(1)} %merge_pair.4), channel_id=1, source_target_pairs={{0,9},{1,8},{2,11},{3,10},{4,13},{5,12},{6,15},{7,14},{8,1},{9,0},... | collective-permute-start | bytes 122888 | tf_op jit(solution)/shard_map/ppermute | solution.py:289
  23.6 0.0 collective-permute-done.12.got_ref
  23.6 0.1 merge_pair.5.refs_10_
  23.7 1.5 %collective-permute-start.13 = (bf16[32,640]{1,0:T(8,128)(2,1)S(1)}, bf16[32,640]{1,0:T(8,128)(2,1)S(1)}, u32[]{:S(2)}, u32[]{:S(2)}) collective-permute-start(bf16[32,640]{1,0:T(8,128)(2,1)S(1)} %merge_pair.5.refs_10_), channel_id=1, source_target_pairs={{0,5},{1,4},{2,7},{3,6},{4,1},{5,0},{6,3},{7,2},{8,13},{9,12},{10,... | collective-permute-start | bytes 122888 | tf_op jit(solution)/shard_map/ppermute | solution.py:289
  25.2 0.3 %page_bounds.1.mine_ref = f32[4,8,8]{2,1,0:T(8,128)S(1)} custom-call(bf16[32,576]{1,0:T(8,128)(2,1)S(1)} %absorb.1.refs_0_, bf16[32,576]{1,0:T(8,128)(2,1)S(1)} %collective-permute-done.refs_1_, bf16[32,576]{1,0:T(8,128)(2,1)S(1)} %collective-permute-done.1.after_ref.refs_2_, bf16[32,576]{1,0:T(8,128)(2,1)S(1)} %collective-permute-done.2.refs_3_, ...), custom_call_target="tpu_custom_call" | custom-call | tf_op jit(solution)/shard_map/page_bounds/pallas_call | solution.py:361
  25.5 0.1 collective-permute-start.14
  25.6 1.2 %collective-permute-done.14.other_ref = f32[4,8,8]{2,1,0:T(8,128)S(1)} collective-permute-done((f32[4,8,8]{2,1,0:T(8,128)S(1)}, f32[4,8,8]{2,1,0:T(8,128)S(1)}, u32[]{:S(2)}, u32[]{:S(2)}) %collective-permute-start.14) | collective-permute-done | bytes 1056 | tf_op jit(solution)/shard_map/ppermute | solution.py:369
  26.8 0.6 %group_bounds.1 = f32[4,8,8]{2,1,0:T(8,128)} custom-call(f32[4,8,8]{2,1,0:T(8,128)S(1)} %page_bounds.1.mine_ref, f32[4,8,8]{2,1,0:T(8,128)S(1)} %collective-permute-done.14.other_ref, f32[4,8,8]{2,1,0:T(8,128)S(1)} %get-tuple-element.29.live_ref), custom_call_target="tpu_custom_call" | custom-call | tf_op jit(solution)/shard_map/group_bounds/pallas_call | solution.py:370
  27.4 0.0 collective-permute-done.7.refs_1_
  27.4 0.0 collective-permute-done.9.refs_2_
  27.4 1.3 %collective-permute-done.11.refs_3_ = bf16[32,640]{1,0:T(8,128)(2,1)S(1)} collective-permute-done((bf16[32,640]{1,0:T(8,128)(2,1)S(1)}, bf16[32,640]{1,0:T(8,128)(2,1)S(1)}, u32[]{:S(2)}, u32[]{:S(2)}) %collective-permute-start.11) | collective-permute-done | bytes 40992 | tf_op jit(solution)/shard_map/ppermute | solution.py:289
  28.7 0.0 collective-permute-done.13.refs_4_
  28.7 0.0 copy-done
  28.7 1.0 %merge_and_value.1 = bf16[4,8,128]{2,1,0:T(8,128)(2,1)} custom-call(bf16[8,512,128]{2,1,0:T(8,128)(2,1)S(1)} %copy-done, f32[32,640]{1,0:T(8,128)S(1)} %get-tuple-element.19.refs_0_, bf16[32,640]{1,0:T(8,128)(2,1)S(1)} %collective-permute-done.7.refs_1_, bf16[32,640]{1,0:T(8,128)(2,1)S(1)} %collective-permute-done.9.refs_2_, ...), custom_call_target="tpu_custom_call" | custom-call | tf_op jit(solution)/shard_map/merge_and_value/pallas_call | solution.py:379
Async XLA Ops:
  2.1 7.8 %collective-permute-start.5 = (bf16[32,576]{1,0:T(8,128)(2,1)S(1)}, bf16[32,576]{1,0:T(8,128)(2,1)S(1)}, u32[]{:S(2)}, u32[]{:S(2)}) collective-permute-start(bf16[32,576]{1,0:T(8,128)(2,1)S(1)} %absorb.1.refs_0_), channel_id=1, source_target_pairs={{0,13},{1,12},{2,15},{3,14},{4,9},{5,8},{6,11},{7,10},{8,5},{9,4},... | collective-permute-start | bytes 110600 | tf_op jit(solution)/shard_map/ppermute | solution.py:289
  6.7 5.0 %collective-permute-start.3 = (bf16[32,576]{1,0:T(8,128)(2,1)S(1)}, bf16[32,576]{1,0:T(8,128)(2,1)S(1)}, u32[]{:S(2)}, u32[]{:S(2)}) collective-permute-start(bf16[32,576]{1,0:T(8,128)(2,1)S(1)} %absorb.1.refs_0_), channel_id=1, source_target_pairs={{0,9},{1,8},{2,11},{3,10},{4,13},{5,12},{6,15},{7,14},{8,1},{9,0},... | collective-permute-start | bytes 110600 | tf_op jit(solution)/shard_map/ppermute | solution.py:289
  6.7 6.1 %collective-permute-start.1 = (bf16[32,576]{1,0:T(8,128)(2,1)S(1)}, bf16[32,576]{1,0:T(8,128)(2,1)S(1)}, u32[]{:S(2)}, u32[]{:S(2)}) collective-permute-start(bf16[32,576]{1,0:T(8,128)(2,1)S(1)} %absorb.1.refs_0_), channel_id=1, source_target_pairs={{0,5},{1,4},{2,7},{3,6},{4,1},{5,0},{6,3},{7,2},{8,13},{9,12},{10,... | collective-permute-start | bytes 110600 | tf_op jit(solution)/shard_map/ppermute | solution.py:289
  7.6 7.9 %collective-permute-start.2 = (bf16[32,576]{1,0:T(8,128)(2,1)S(1)}, bf16[32,576]{1,0:T(8,128)(2,1)S(1)}, u32[]{:S(2)}, u32[]{:S(2)}) collective-permute-start(bf16[32,576]{1,0:T(8,128)(2,1)S(1)} %absorb.1.refs_0_), channel_id=1, source_target_pairs={{0,6},{1,7},{2,4},{3,5},{4,2},{5,3},{6,0},{7,1},{8,14},{9,15},{10,... | collective-permute-start | bytes 110600 | tf_op jit(solution)/shard_map/ppermute | solution.py:289
  9.9 5.5 %collective-permute-start = (bf16[32,576]{1,0:T(8,128)(2,1)S(1)}, bf16[32,576]{1,0:T(8,128)(2,1)S(1)}, u32[]{:S(2)}, u32[]{:S(2)}) collective-permute-start(bf16[32,576]{1,0:T(8,128)(2,1)S(1)} %absorb.1.refs_0_), channel_id=1, source_target_pairs={{0,3},{1,2},{2,1},{3,0},{4,7},{5,6},{6,5},{7,4},{8,11},{9,10},{10,... | collective-permute-start | bytes 110600 | tf_op jit(solution)/shard_map/ppermute | solution.py:289
  9.9 5.6 %collective-permute-start.6 = (bf16[32,576]{1,0:T(8,128)(2,1)S(1)}, bf16[32,576]{1,0:T(8,128)(2,1)S(1)}, u32[]{:S(2)}, u32[]{:S(2)}) collective-permute-start(bf16[32,576]{1,0:T(8,128)(2,1)S(1)} %collective-permute-done.5.refs_6_), channel_id=1, source_target_pairs={{0,3},{1,2},{2,1},{3,0},{4,7},{5,6},{6,5},{7,4},{8,11},{9,10},{10,... | collective-permute-start | bytes 110600 | tf_op jit(solution)/shard_map/ppermute | solution.py:289
  11.7 4.0 %collective-permute-start.4 = (bf16[32,576]{1,0:T(8,128)(2,1)S(1)}, bf16[32,576]{1,0:T(8,128)(2,1)S(1)}, u32[]{:S(2)}, u32[]{:S(2)}) collective-permute-start(bf16[32,576]{1,0:T(8,128)(2,1)S(1)} %collective-permute-done.3.refs_4_), channel_id=1, source_target_pairs={{0,3},{1,2},{2,1},{3,0},{4,7},{5,6},{6,5},{7,4},{8,11},{9,10},{10,... | collective-permute-start | bytes 110600 | tf_op jit(solution)/shard_map/ppermute | solution.py:289
  15.7 13.0 %copy-start = (bf16[8,512,128]{2,1,0:T(8,128)(2,1)S(1)}, bf16[8,512,128]{2,1,0:T(8,128)(2,1)}, u32[]{:S(2)}) copy-start(bf16[8,512,128]{2,1,0:T(8,128)(2,1)} %w_ref.1) | copy-start | bytes 3145732
  16.6 3.6 %collective-permute-start.8 = (bf16[32,640]{1,0:T(8,128)(2,1)S(1)}, bf16[32,640]{1,0:T(8,128)(2,1)S(1)}, u32[]{:S(2)}, u32[]{:S(2)}) collective-permute-start(bf16[32,640]{1,0:T(8,128)(2,1)S(1)} %get-tuple-element.21), channel_id=1, source_target_pairs={{0,3},{1,2},{2,1},{3,0},{4,7},{5,6},{6,5},{7,4},{8,11},{9,10},{10,... | collective-permute-start | bytes 122888 | tf_op jit(solution)/shard_map/ppermute | solution.py:289
  17.2 5.8 %collective-permute-start.10 = (bf16[32,640]{1,0:T(8,128)(2,1)S(1)}, bf16[32,640]{1,0:T(8,128)(2,1)S(1)}, u32[]{:S(2)}, u32[]{:S(2)}) collective-permute-start(bf16[32,640]{1,0:T(8,128)(2,1)S(1)} %get-tuple-element.23), channel_id=1, source_target_pairs={{0,3},{1,2},{2,1},{3,0},{4,7},{5,6},{6,5},{7,4},{8,11},{9,10},{10,... | collective-permute-start | bytes 122888 | tf_op jit(solution)/shard_map/ppermute | solution.py:289
  18.4 5.2 %collective-permute-start.12 = (bf16[32,640]{1,0:T(8,128)(2,1)S(1)}, bf16[32,640]{1,0:T(8,128)(2,1)S(1)}, u32[]{:S(2)}, u32[]{:S(2)}) collective-permute-start(bf16[32,640]{1,0:T(8,128)(2,1)S(1)} %get-tuple-element.25), channel_id=1, source_target_pairs={{0,3},{1,2},{2,1},{3,0},{4,7},{5,6},{6,5},{7,4},{8,11},{9,10},{10,... | collective-permute-start | bytes 122888 | tf_op jit(solution)/shard_map/ppermute | solution.py:289
  19.0 8.4 %collective-permute-start.7 = (bf16[32,640]{1,0:T(8,128)(2,1)S(1)}, bf16[32,640]{1,0:T(8,128)(2,1)S(1)}, u32[]{:S(2)}, u32[]{:S(2)}) collective-permute-start(bf16[32,640]{1,0:T(8,128)(2,1)S(1)} %get-tuple-element.20), channel_id=1, source_target_pairs={{0,3},{1,2},{2,1},{3,0},{4,7},{5,6},{6,5},{7,4},{8,11},{9,10},{10,... | collective-permute-start | bytes 122888 | tf_op jit(solution)/shard_map/ppermute | solution.py:289
  20.4 7.0 %collective-permute-start.9 = (bf16[32,640]{1,0:T(8,128)(2,1)S(1)}, bf16[32,640]{1,0:T(8,128)(2,1)S(1)}, u32[]{:S(2)}, u32[]{:S(2)}) collective-permute-start(bf16[32,640]{1,0:T(8,128)(2,1)S(1)} %merge_pair.3), channel_id=1, source_target_pairs={{0,13},{1,12},{2,15},{3,14},{4,9},{5,8},{6,11},{7,10},{8,5},{9,4},... | collective-permute-start | bytes 122888 | tf_op jit(solution)/shard_map/ppermute | solution.py:289
  23.1 5.5 %collective-permute-start.11 = (bf16[32,640]{1,0:T(8,128)(2,1)S(1)}, bf16[32,640]{1,0:T(8,128)(2,1)S(1)}, u32[]{:S(2)}, u32[]{:S(2)}) collective-permute-start(bf16[32,640]{1,0:T(8,128)(2,1)S(1)} %merge_pair.4), channel_id=1, source_target_pairs={{0,9},{1,8},{2,11},{3,10},{4,13},{5,12},{6,15},{7,14},{8,1},{9,0},... | collective-permute-start | bytes 122888 | tf_op jit(solution)/shard_map/ppermute | solution.py:289
  23.7 4.9 %collective-permute-start.13 = (bf16[32,640]{1,0:T(8,128)(2,1)S(1)}, bf16[32,640]{1,0:T(8,128)(2,1)S(1)}, u32[]{:S(2)}, u32[]{:S(2)}) collective-permute-start(bf16[32,640]{1,0:T(8,128)(2,1)S(1)} %merge_pair.5.refs_10_), channel_id=1, source_target_pairs={{0,5},{1,4},{2,7},{3,6},{4,1},{5,0},{6,3},{7,2},{8,13},{9,12},{10,... | collective-permute-start | bytes 122888 | tf_op jit(solution)/shard_map/ppermute | solution.py:289
  25.5 1.2 %collective-permute-start.14 = (f32[4,8,8]{2,1,0:T(8,128)S(1)}, f32[4,8,8]{2,1,0:T(8,128)S(1)}, u32[]{:S(2)}, u32[]{:S(2)}) collective-permute-start(f32[4,8,8]{2,1,0:T(8,128)S(1)} %page_bounds.1.mine_ref), channel_id=1, source_target_pairs={{0,1},{1,0},{2,3},{3,2},{4,5},{5,4},{6,7},{7,6},{8,9},{9,8},{10,11... | collective-permute-start | bytes 3080 | tf_op jit(solution)/shard_map/ppermute | solution.py:369

commit v7 on v6

--- a/solution.py
+++ b/solution.py
@@ -356,7 +356,8 @@
         )(got[k], parts[k])
         for k in far
     }
-    arrived = [swap(send[k], k) for k in far]
+    turns = far[:1] + far[:0:-1]
+    arrived = [swap(send[k], k) for k in turns]
 
     bounds = pl.pallas_call(
         functools.partial(bounds_kernel, scale, heads, offsets),

time: 29.9 us -> 29.1 us (0.973)
  waiting for transfers between devices: 2.66 us -> 1.83 us
    ppermute x14, waiting for transfers between devices: 1.49 us -> 0.66 us  [swap(): return lax.ppermute(x, ('seq', 'head'), pairs)]
  transfers between devices with their start and end apart: 15 -> 15, of which waited for: 3 -> 3; matrix products, arithmetic and copies ran while one was open for 0% -> 0% of each run, Pallas kernels for 13% -> 14%
where the time goes in v7:
time: 29.1 us; the launch traced here: 28.8 us
  starting transfers between devices  18.9 us (65%)
  Pallas kernels  7.29 us (25%)
  waiting for transfers between devices  1.83 us (6%)
  between operations  0.73 us (3%)
    ppermute x14, starting transfers between devices, swap(): return lax.ppermute(x, ('seq', 'head'), pairs)  18.9 us
    pallas_call x1, Pallas kernels, local(): pl.pallas_call(stage_kernel, out_shape=(jax.ShapeDtypeStruct(slots.shape,...  2.66 us
    pallas_call x1, Pallas kernels, local(): pl.pallas_call(absorb_kernel, out_shape=jax.ShapeDtypeStruct((rows, width...  1.46 us
    ppermute x1, waiting for transfers between devices, local(): lax.ppermute(bounds, 'head', [(i, i ^ 1) for i in range(head_count)])  1.17 us
    pallas_call x1, Pallas kernels, local(): pl.pallas_call(functools.partial(value_kernel, latent, heads), out_shape=...  0.96 us
    pallas_call x1, Pallas kernels, local(): pl.pallas_call(functools.partial(attend_kernel, scale, heads, offsets, la...  0.94 us
    ppermute x14, waiting for transfers between devices, swap(): return lax.ppermute(x, ('seq', 'head'), pairs)  0.66 us
    pallas_call x1, Pallas kernels, local(): pl.pallas_call(largest_kernel, out_shape=jax.ShapeDtypeStruct((requests,...  0.61 us
  transfers between devices with their start and end apart: 15, of which 3 were waited for; matrix products, arithmetic and copies ran while one was open for 0% of the time, Pallas kernels for 14%

profile of v7, /device:TPU:0, one launch (start us, length us, event | category | flops | bytes accessed | tf_op | source)
XLA Modules:
  0.0 28.8 jit_solution(4921075986085001511)
XLA Ops:
  0.6 1.5 %absorb.1.refs_0_ = bf16[32,576]{1,0:T(8,128)(2,1)S(1)} custom-call(bf16[4,8,128]{2,1,0:T(8,128)(2,1)} %nope_hbm.1, bf16[4,8,64]{2,1,0:T(8,128)(2,1)} %rope_hbm.1, bf16[8,128,512]{2,1,0:T(8,128)(2,1)} %w_hbm.1), custom_call_target="tpu_custom_call" | custom-call | tf_op jit(solution)/shard_map/absorb/pallas_call | solution.py:291
  2.1 4.6 %collective-permute-start.5 = (bf16[32,576]{1,0:T(8,128)(2,1)S(1)}, bf16[32,576]{1,0:T(8,128)(2,1)S(1)}, u32[]{:S(2)}, u32[]{:S(2)}) collective-permute-start(bf16[32,576]{1,0:T(8,128)(2,1)S(1)} %absorb.1.refs_0_), channel_id=1, source_target_pairs={{0,13},{1,12},{2,15},{3,14},{4,9},{5,8},{6,11},{7,10},{8,5},{9,4},... | collective-permute-start | bytes 110600 | tf_op jit(solution)/shard_map/ppermute | solution.py:289
  6.7 0.0 collective-permute-start.3
  6.7 0.9 %collective-permute-start.1 = (bf16[32,576]{1,0:T(8,128)(2,1)S(1)}, bf16[32,576]{1,0:T(8,128)(2,1)S(1)}, u32[]{:S(2)}, u32[]{:S(2)}) collective-permute-start(bf16[32,576]{1,0:T(8,128)(2,1)S(1)} %absorb.1.refs_0_), channel_id=1, source_target_pairs={{0,5},{1,4},{2,7},{3,6},{4,1},{5,0},{6,3},{7,2},{8,13},{9,12},{10,... | collective-permute-start | bytes 110600 | tf_op jit(solution)/shard_map/ppermute | solution.py:289
  7.6 2.3 %collective-permute-start.2 = (bf16[32,576]{1,0:T(8,128)(2,1)S(1)}, bf16[32,576]{1,0:T(8,128)(2,1)S(1)}, u32[]{:S(2)}, u32[]{:S(2)}) collective-permute-start(bf16[32,576]{1,0:T(8,128)(2,1)S(1)} %absorb.1.refs_0_), channel_id=1, source_target_pairs={{0,6},{1,7},{2,4},{3,5},{4,2},{5,3},{6,0},{7,1},{8,14},{9,15},{10,... | collective-permute-start | bytes 110600 | tf_op jit(solution)/shard_map/ppermute | solution.py:289
  9.9 0.0 collective-permute-start
  9.9 0.0 collective-permute-done.5.refs_6_
  9.9 1.7 %collective-permute-start.6 = (bf16[32,576]{1,0:T(8,128)(2,1)S(1)}, bf16[32,576]{1,0:T(8,128)(2,1)S(1)}, u32[]{:S(2)}, u32[]{:S(2)}) collective-permute-start(bf16[32,576]{1,0:T(8,128)(2,1)S(1)} %collective-permute-done.5.refs_6_), channel_id=1, source_target_pairs={{0,3},{1,2},{2,1},{3,0},{4,7},{5,6},{6,5},{7,4},{8,11},{9,10},{10,... | collective-permute-start | bytes 110600 | tf_op jit(solution)/shard_map/ppermute | solution.py:289
  11.7 0.0 collective-permute-done.3.refs_4_
  11.7 1.1 %collective-permute-start.4 = (bf16[32,576]{1,0:T(8,128)(2,1)S(1)}, bf16[32,576]{1,0:T(8,128)(2,1)S(1)}, u32[]{:S(2)}, u32[]{:S(2)}) collective-permute-start(bf16[32,576]{1,0:T(8,128)(2,1)S(1)} %collective-permute-done.3.refs_4_), channel_id=1, source_target_pairs={{0,3},{1,2},{2,1},{3,0},{4,7},{5,6},{6,5},{7,4},{8,11},{9,10},{10,... | collective-permute-start | bytes 110600 | tf_op jit(solution)/shard_map/ppermute | solution.py:289
  12.8 0.0 collective-permute-done.1.after_ref.refs_2_
  12.8 2.7 %stage_cache.1 = (bf16[4,576,512]{2,1,0:T(8,128)(2,1)S(1)}, bf16[4,512,512]{2,1,0:T(8,128)(2,1)S(1)}, f32[32,512]{1,0:T(8,128)S(1)}, f32[4,8,576]{2,1,0:T(8,128)...) custom-call(bf16[4,576,512]{2,1,0:T(8,128)(2,1)} %bitcast.1, s32[4,8,32]{2,1,0:T(8,128)} %selected_hbm.1, ...), custom_call_target="tpu_custom_call" | custom-call | tf_op jit(solution)/shard_map/stage_cache/pallas_call | solution.py:315
  15.5 0.0 collective-permute-done.2.refs_3_
  15.5 0.0 collective-permute-done.refs_1_
  15.5 0.0 collective-permute-done.6.refs_7_
  15.5 0.2 collective-permute-done.4.refs_5_
  15.7 0.0 copy-start
  15.7 0.9 %attend.1 = (f32[32,640]{1,0:T(8,128)S(1)}, bf16[32,640]{1,0:T(8,128)(2,1)S(1)}, f32[32,640]{1,0:T(8,128)S(1)}, bf16[32,640]{1,0:T(8,128)(2,1)S(1)}, f32[32,640]...) custom-call(bf16[32,576]{1,0:T(8,128)(2,1)S(1)} %absorb.1.refs_0_, ...), custom_call_target="tpu_custom_call" | custom-call | tf_op jit(solution)/shard_map/attend/pallas_call | solution.py:336
  16.6 0.6 %collective-permute-start.8 = (bf16[32,640]{1,0:T(8,128)(2,1)S(1)}, bf16[32,640]{1,0:T(8,128)(2,1)S(1)}, u32[]{:S(2)}, u32[]{:S(2)}) collective-permute-start(bf16[32,640]{1,0:T(8,128)(2,1)S(1)} %get-tuple-element.21), channel_id=1, source_target_pairs={{0,3},{1,2},{2,1},{3,0},{4,7},{5,6},{6,5},{7,4},{8,11},{9,10},{10,... | collective-permute-start | bytes 122888 | tf_op jit(solution)/shard_map/ppermute | solution.py:289
  17.2 1.2 %collective-permute-start.10 = (bf16[32,640]{1,0:T(8,128)(2,1)S(1)}, bf16[32,640]{1,0:T(8,128)(2,1)S(1)}, u32[]{:S(2)}, u32[]{:S(2)}) collective-permute-start(bf16[32,640]{1,0:T(8,128)(2,1)S(1)} %get-tuple-element.23), channel_id=1, source_target_pairs={{0,3},{1,2},{2,1},{3,0},{4,7},{5,6},{6,5},{7,4},{8,11},{9,10},{10,... | collective-permute-start | bytes 122888 | tf_op jit(solution)/shard_map/ppermute | solution.py:289
  18.4 0.5 %collective-permute-start.12 = (bf16[32,640]{1,0:T(8,128)(2,1)S(1)}, bf16[32,640]{1,0:T(8,128)(2,1)S(1)}, u32[]{:S(2)}, u32[]{:S(2)}) collective-permute-start(bf16[32,640]{1,0:T(8,128)(2,1)S(1)} %get-tuple-element.25), channel_id=1, source_target_pairs={{0,3},{1,2},{2,1},{3,0},{4,7},{5,6},{6,5},{7,4},{8,11},{9,10},{10,... | collective-permute-start | bytes 122888 | tf_op jit(solution)/shard_map/ppermute | solution.py:289
  19.0 1.2 %collective-permute-start.7 = (bf16[32,640]{1,0:T(8,128)(2,1)S(1)}, bf16[32,640]{1,0:T(8,128)(2,1)S(1)}, u32[]{:S(2)}, u32[]{:S(2)}) collective-permute-start(bf16[32,640]{1,0:T(8,128)(2,1)S(1)} %get-tuple-element.20), channel_id=1, source_target_pairs={{0,3},{1,2},{2,1},{3,0},{4,7},{5,6},{6,5},{7,4},{8,11},{9,10},{10,... | collective-permute-start | bytes 122888 | tf_op jit(solution)/shard_map/ppermute | solution.py:289
  20.2 0.0 collective-permute-done.8.got_ref
  20.2 0.1 merge_pair.3
  20.4 2.7 %collective-permute-start.9 = (bf16[32,640]{1,0:T(8,128)(2,1)S(1)}, bf16[32,640]{1,0:T(8,128)(2,1)S(1)}, u32[]{:S(2)}, u32[]{:S(2)}) collective-permute-start(bf16[32,640]{1,0:T(8,128)(2,1)S(1)} %merge_pair.3), channel_id=1, source_target_pairs={{0,13},{1,12},{2,15},{3,14},{4,9},{5,8},{6,11},{7,10},{8,5},{9,4},... | collective-permute-start | bytes 122888 | tf_op jit(solution)/shard_map/ppermute | solution.py:289
  23.0 0.0 collective-permute-done.10.got_ref
  23.0 0.1 merge_pair.4.refs_10_
  23.1 0.1 collective-permute-start.11
  23.2 0.0 collective-permute-done.12.got_ref
  23.2 0.1 merge_pair.5
  23.3 1.9 %collective-permute-start.13 = (bf16[32,640]{1,0:T(8,128)(2,1)S(1)}, bf16[32,640]{1,0:T(8,128)(2,1)S(1)}, u32[]{:S(2)}, u32[]{:S(2)}) collective-permute-start(bf16[32,640]{1,0:T(8,128)(2,1)S(1)} %merge_pair.5), channel_id=1, source_target_pairs={{0,9},{1,8},{2,11},{3,10},{4,13},{5,12},{6,15},{7,14},{8,1},{9,0},... | collective-permute-start | bytes 122888 | tf_op jit(solution)/shard_map/ppermute | solution.py:289
  25.2 0.3 %page_bounds.1.mine_ref = f32[4,8,8]{2,1,0:T(8,128)S(1)} custom-call(bf16[32,576]{1,0:T(8,128)(2,1)S(1)} %absorb.1.refs_0_, bf16[32,576]{1,0:T(8,128)(2,1)S(1)} %collective-permute-done.refs_1_, bf16[32,576]{1,0:T(8,128)(2,1)S(1)} %collective-permute-done.1.after_ref.refs_2_, bf16[32,576]{1,0:T(8,128)(2,1)S(1)} %collective-permute-done.2.refs_3_, ...), custom_call_target="tpu_custom_call" | custom-call | tf_op jit(solution)/shard_map/page_bounds/pallas_call | solution.py:362
  25.5 0.1 collective-permute-start.14
  25.6 1.2 %collective-permute-done.14.other_ref = f32[4,8,8]{2,1,0:T(8,128)S(1)} collective-permute-done((f32[4,8,8]{2,1,0:T(8,128)S(1)}, f32[4,8,8]{2,1,0:T(8,128)S(1)}, u32[]{:S(2)}, u32[]{:S(2)}) %collective-permute-start.14) | collective-permute-done | bytes 1056 | tf_op jit(solution)/shard_map/ppermute | solution.py:370
  26.8 0.6 %group_bounds.1 = f32[4,8,8]{2,1,0:T(8,128)} custom-call(f32[4,8,8]{2,1,0:T(8,128)S(1)} %page_bounds.1.mine_ref, f32[4,8,8]{2,1,0:T(8,128)S(1)} %collective-permute-done.14.other_ref, f32[4,8,8]{2,1,0:T(8,128)S(1)} %get-tuple-element.29.live_ref), custom_call_target="tpu_custom_call" | custom-call | tf_op jit(solution)/shard_map/group_bounds/pallas_call | solution.py:371
  27.4 0.0 collective-permute-done.7.refs_1_
  27.4 0.0 collective-permute-done.9.refs_2_
  27.4 0.4 %collective-permute-done.11.refs_3_ = bf16[32,640]{1,0:T(8,128)(2,1)S(1)} collective-permute-done((bf16[32,640]{1,0:T(8,128)(2,1)S(1)}, bf16[32,640]{1,0:T(8,128)(2,1)S(1)}, u32[]{:S(2)}, u32[]{:S(2)}) %collective-permute-start.11) | collective-permute-done | bytes 40992 | tf_op jit(solution)/shard_map/ppermute | solution.py:289
  27.8 0.0 collective-permute-done.13.refs_4_
  27.8 0.0 copy-done
  27.8 1.0 %merge_and_value.1 = bf16[4,8,128]{2,1,0:T(8,128)(2,1)} custom-call(bf16[8,512,128]{2,1,0:T(8,128)(2,1)S(1)} %copy-done, f32[32,640]{1,0:T(8,128)S(1)} %get-tuple-element.19.refs_0_, bf16[32,640]{1,0:T(8,128)(2,1)S(1)} %collective-permute-done.7.refs_1_, bf16[32,640]{1,0:T(8,128)(2,1)S(1)} %collective-permute-done.9.refs_2_, ...), custom_call_target="tpu_custom_call" | custom-call | tf_op jit(solution)/shard_map/merge_and_value/pallas_call | solution.py:380
Async XLA Ops:
  2.1 7.8 %collective-permute-start.5 = (bf16[32,576]{1,0:T(8,128)(2,1)S(1)}, bf16[32,576]{1,0:T(8,128)(2,1)S(1)}, u32[]{:S(2)}, u32[]{:S(2)}) collective-permute-start(bf16[32,576]{1,0:T(8,128)(2,1)S(1)} %absorb.1.refs_0_), channel_id=1, source_target_pairs={{0,13},{1,12},{2,15},{3,14},{4,9},{5,8},{6,11},{7,10},{8,5},{9,4},... | collective-permute-start | bytes 110600 | tf_op jit(solution)/shard_map/ppermute | solution.py:289
  6.7 5.0 %collective-permute-start.3 = (bf16[32,576]{1,0:T(8,128)(2,1)S(1)}, bf16[32,576]{1,0:T(8,128)(2,1)S(1)}, u32[]{:S(2)}, u32[]{:S(2)}) collective-permute-start(bf16[32,576]{1,0:T(8,128)(2,1)S(1)} %absorb.1.refs_0_), channel_id=1, source_target_pairs={{0,9},{1,8},{2,11},{3,10},{4,13},{5,12},{6,15},{7,14},{8,1},{9,0},... | collective-permute-start | bytes 110600 | tf_op jit(solution)/shard_map/ppermute | solution.py:289
  6.7 6.1 %collective-permute-start.1 = (bf16[32,576]{1,0:T(8,128)(2,1)S(1)}, bf16[32,576]{1,0:T(8,128)(2,1)S(1)}, u32[]{:S(2)}, u32[]{:S(2)}) collective-permute-start(bf16[32,576]{1,0:T(8,128)(2,1)S(1)} %absorb.1.refs_0_), channel_id=1, source_target_pairs={{0,5},{1,4},{2,7},{3,6},{4,1},{5,0},{6,3},{7,2},{8,13},{9,12},{10,... | collective-permute-start | bytes 110600 | tf_op jit(solution)/shard_map/ppermute | solution.py:289
  7.6 7.9 %collective-permute-start.2 = (bf16[32,576]{1,0:T(8,128)(2,1)S(1)}, bf16[32,576]{1,0:T(8,128)(2,1)S(1)}, u32[]{:S(2)}, u32[]{:S(2)}) collective-permute-start(bf16[32,576]{1,0:T(8,128)(2,1)S(1)} %absorb.1.refs_0_), channel_id=1, source_target_pairs={{0,6},{1,7},{2,4},{3,5},{4,2},{5,3},{6,0},{7,1},{8,14},{9,15},{10,... | collective-permute-start | bytes 110600 | tf_op jit(solution)/shard_map/ppermute | solution.py:289
  9.9 5.5 %collective-permute-start = (bf16[32,576]{1,0:T(8,128)(2,1)S(1)}, bf16[32,576]{1,0:T(8,128)(2,1)S(1)}, u32[]{:S(2)}, u32[]{:S(2)}) collective-permute-start(bf16[32,576]{1,0:T(8,128)(2,1)S(1)} %absorb.1.refs_0_), channel_id=1, source_target_pairs={{0,3},{1,2},{2,1},{3,0},{4,7},{5,6},{6,5},{7,4},{8,11},{9,10},{10,... | collective-permute-start | bytes 110600 | tf_op jit(solution)/shard_map/ppermute | solution.py:289
  9.9 5.6 %collective-permute-start.6 = (bf16[32,576]{1,0:T(8,128)(2,1)S(1)}, bf16[32,576]{1,0:T(8,128)(2,1)S(1)}, u32[]{:S(2)}, u32[]{:S(2)}) collective-permute-start(bf16[32,576]{1,0:T(8,128)(2,1)S(1)} %collective-permute-done.5.refs_6_), channel_id=1, source_target_pairs={{0,3},{1,2},{2,1},{3,0},{4,7},{5,6},{6,5},{7,4},{8,11},{9,10},{10,... | collective-permute-start | bytes 110600 | tf_op jit(solution)/shard_map/ppermute | solution.py:289
  11.7 4.0 %collective-permute-start.4 = (bf16[32,576]{1,0:T(8,128)(2,1)S(1)}, bf16[32,576]{1,0:T(8,128)(2,1)S(1)}, u32[]{:S(2)}, u32[]{:S(2)}) collective-permute-start(bf16[32,576]{1,0:T(8,128)(2,1)S(1)} %collective-permute-done.3.refs_4_), channel_id=1, source_target_pairs={{0,3},{1,2},{2,1},{3,0},{4,7},{5,6},{6,5},{7,4},{8,11},{9,10},{10,... | collective-permute-start | bytes 110600 | tf_op jit(solution)/shard_map/ppermute | solution.py:289
  15.7 12.2 %copy-start = (bf16[8,512,128]{2,1,0:T(8,128)(2,1)S(1)}, bf16[8,512,128]{2,1,0:T(8,128)(2,1)}, u32[]{:S(2)}) copy-start(bf16[8,512,128]{2,1,0:T(8,128)(2,1)} %w_ref.1) | copy-start | bytes 3145732
  16.6 3.6 %collective-permute-start.8 = (bf16[32,640]{1,0:T(8,128)(2,1)S(1)}, bf16[32,640]{1,0:T(8,128)(2,1)S(1)}, u32[]{:S(2)}, u32[]{:S(2)}) collective-permute-start(bf16[32,640]{1,0:T(8,128)(2,1)S(1)} %get-tuple-element.21), channel_id=1, source_target_pairs={{0,3},{1,2},{2,1},{3,0},{4,7},{5,6},{6,5},{7,4},{8,11},{9,10},{10,... | collective-permute-start | bytes 122888 | tf_op jit(solution)/shard_map/ppermute | solution.py:289
  17.2 5.8 %collective-permute-start.10 = (bf16[32,640]{1,0:T(8,128)(2,1)S(1)}, bf16[32,640]{1,0:T(8,128)(2,1)S(1)}, u32[]{:S(2)}, u32[]{:S(2)}) collective-permute-start(bf16[32,640]{1,0:T(8,128)(2,1)S(1)} %get-tuple-element.23), channel_id=1, source_target_pairs={{0,3},{1,2},{2,1},{3,0},{4,7},{5,6},{6,5},{7,4},{8,11},{9,10},{10,... | collective-permute-start | bytes 122888 | tf_op jit(solution)/shard_map/ppermute | solution.py:289
  18.4 4.8 %collective-permute-start.12 = (bf16[32,640]{1,0:T(8,128)(2,1)S(1)}, bf16[32,640]{1,0:T(8,128)(2,1)S(1)}, u32[]{:S(2)}, u32[]{:S(2)}) collective-permute-start(bf16[32,640]{1,0:T(8,128)(2,1)S(1)} %get-tuple-element.25), channel_id=1, source_target_pairs={{0,3},{1,2},{2,1},{3,0},{4,7},{5,6},{6,5},{7,4},{8,11},{9,10},{10,... | collective-permute-start | bytes 122888 | tf_op jit(solution)/shard_map/ppermute | solution.py:289
  19.0 8.4 %collective-permute-start.7 = (bf16[32,640]{1,0:T(8,128)(2,1)S(1)}, bf16[32,640]{1,0:T(8,128)(2,1)S(1)}, u32[]{:S(2)}, u32[]{:S(2)}) collective-permute-start(bf16[32,640]{1,0:T(8,128)(2,1)S(1)} %get-tuple-element.20), channel_id=1, source_target_pairs={{0,3},{1,2},{2,1},{3,0},{4,7},{5,6},{6,5},{7,4},{8,11},{9,10},{10,... | collective-permute-start | bytes 122888 | tf_op jit(solution)/shard_map/ppermute | solution.py:289
  20.4 7.0 %collective-permute-start.9 = (bf16[32,640]{1,0:T(8,128)(2,1)S(1)}, bf16[32,640]{1,0:T(8,128)(2,1)S(1)}, u32[]{:S(2)}, u32[]{:S(2)}) collective-permute-start(bf16[32,640]{1,0:T(8,128)(2,1)S(1)} %merge_pair.3), channel_id=1, source_target_pairs={{0,13},{1,12},{2,15},{3,14},{4,9},{5,8},{6,11},{7,10},{8,5},{9,4},... | collective-permute-start | bytes 122888 | tf_op jit(solution)/shard_map/ppermute | solution.py:289
  23.1 4.7 %collective-permute-start.11 = (bf16[32,640]{1,0:T(8,128)(2,1)S(1)}, bf16[32,640]{1,0:T(8,128)(2,1)S(1)}, u32[]{:S(2)}, u32[]{:S(2)}) collective-permute-start(bf16[32,640]{1,0:T(8,128)(2,1)S(1)} %merge_pair.4.refs_10_), channel_id=1, source_target_pairs={{0,5},{1,4},{2,7},{3,6},{4,1},{5,0},{6,3},{7,2},{8,13},{9,12},{10,... | collective-permute-start | bytes 122888 | tf_op jit(solution)/shard_map/ppermute | solution.py:289
  23.3 4.5 %collective-permute-start.13 = (bf16[32,640]{1,0:T(8,128)(2,1)S(1)}, bf16[32,640]{1,0:T(8,128)(2,1)S(1)}, u32[]{:S(2)}, u32[]{:S(2)}) collective-permute-start(bf16[32,640]{1,0:T(8,128)(2,1)S(1)} %merge_pair.5), channel_id=1, source_target_pairs={{0,9},{1,8},{2,11},{3,10},{4,13},{5,12},{6,15},{7,14},{8,1},{9,0},... | collective-permute-start | bytes 122888 | tf_op jit(solution)/shard_map/ppermute | solution.py:289
  25.5 1.2 %collective-permute-start.14 = (f32[4,8,8]{2,1,0:T(8,128)S(1)}, f32[4,8,8]{2,1,0:T(8,128)S(1)}, u32[]{:S(2)}, u32[]{:S(2)}) collective-permute-start(f32[4,8,8]{2,1,0:T(8,128)S(1)} %page_bounds.1.mine_ref), channel_id=1, source_target_pairs={{0,1},{1,0},{2,3},{3,2},{4,5},{5,4},{6,7},{7,6},{8,9},{9,8},{10,11... | collective-permute-start | bytes 3080 | tf_op jit(solution)/shard_map/ppermute | solution.py:370

commit v8 on v7

--- a/solution.py
+++ b/solution.py
@@ -18,6 +18,29 @@
 SMEM = pl.BlockSpec(memory_space=pltpu.SMEM)
 HBM = pl.BlockSpec(memory_space=pltpu.HBM)
 ANY = pl.BlockSpec(memory_space=pl.ANY)
+
+
+def height(rows):
+    return -(-rows // 16) * 16
+
+
+def block_shape(rows, latent):
+    return (latent // LANES * height(rows) + 16, LANES)
+
+
+def put(ref, x, last):
+    rows, width = x.shape
+    for c in range(width // LANES):
+        start = c * height(rows)
+        ref[start : start + rows, :] = x[:, c * LANES : (c + 1) * LANES].astype(BF16)
+    last = jnp.concatenate([last] * (16 // last.shape[0]), axis=0)
+    ref[width // LANES * height(rows) :, :] = last.astype(BF16)
+
+
+def take(ref, rows, width):
+    x = ref[...].astype(F32)
+    starts = [c * height(rows) for c in range(width // LANES)]
+    return jnp.concatenate([x[a : a + rows] for a in starts], axis=1), x[-16:]
 
 
 def params(mib=24):
@@ -46,7 +69,10 @@
         copy.wait()
     nope = nope_ref[...].astype(F32).reshape(rows, size)
     head = lax.broadcasted_iota(jnp.int32, (rows, size), 0) % heads
-    out_ref[:, latent:] = rope_ref[...].astype(F32).reshape(rows, rope_ref.shape[2]).astype(BF16)
+    rope = rope_ref[...].astype(F32).reshape(rows, rope_ref.shape[2])
+    fold = LANES // rope.shape[1]
+    part = rows // fold
+    rope = jnp.concatenate([rope[i * part : (i + 1) * part] for i in range(fold)], axis=1)
     total = jnp.zeros((rows, latent), F32)
     for i, copy in enumerate(large):
         wide = jnp.concatenate(
@@ -55,7 +81,7 @@
         copy.wait()
         weight = w_ref[i * step : (i + 1) * step].reshape(step * size, latent)
         total += jnp.dot(wide, weight, preferred_element_type=F32)
-    out_ref[:, :latent] = total.astype(BF16)
+    put(out_ref, total, rope)
 
 
 def stage_kernel(
@@ -113,9 +139,22 @@
     return high, middle, (rest - middle.astype(F32)).astype(BF16)
 
 
-def queries_of(blocks, request, heads):
-    rows = slice(request * heads, (request + 1) * heads)
-    return jnp.concatenate([b[rows] for b in blocks], axis=0)
+def queries_of(blocks, request, heads, width):
+    found = []
+    for latent, rope in blocks:
+        size = width - latent.shape[1]
+        part = latent.shape[0] * size // LANES
+        column, row = divmod(request * heads, part)
+        found.append(
+            jnp.concatenate(
+                [
+                    latent[request * heads : (request + 1) * heads],
+                    rope[row : row + heads, column * size : (column + 1) * size],
+                ],
+                axis=1,
+            )
+        )
+    return jnp.concatenate(found, axis=0)
 
 
 def crossings(offset):
@@ -132,12 +171,14 @@
     count = len(offsets)
     block_refs = refs[:count]
     cache_ref, slots_ref, mask_ref, *out_refs = refs[count:]
-    requests, _, tokens = cache_ref.shape
+    requests, width, tokens = cache_ref.shape
     groups = mask_ref.shape[0] // requests
-    blocks = [b[...].astype(F32) for b in block_refs]
+    blocks = [take(b, requests * heads, latent) for b in block_refs]
     scores = [
         jnp.dot(
-            queries_of(blocks, r, heads).astype(BF16), cache_ref[r], preferred_element_type=F32
+            queries_of(blocks, r, heads, width).astype(BF16),
+            cache_ref[r],
+            preferred_element_type=F32,
         )
         for r in range(requests)
     ]
@@ -171,23 +212,43 @@
 
 
 def fill(ref, out, lse):
-    latent = out.shape[1]
-    ref[:, :latent] = out.astype(ref.dtype)
-    ref[:, latent:] = packed(lse) if ref.dtype == BF16 else lse
+    if ref.dtype == BF16:
+        put(ref, out, packed(lse))
+    else:
+        ref[:, : out.shape[1]] = out
+        ref[:, out.shape[1] :] = lse
 
 
 def packed(lse):
-    lane = lax.broadcasted_iota(jnp.int32, lse.shape, 1)
-    high, middle, low = (p.astype(F32) for p in split3(lse))
-    return jnp.where(lane == 0, high, jnp.where(lane == 1, middle, low)).astype(BF16)
-
-
-def read(ref, latent):
-    lse = ref[:, latent:].astype(F32)
+    count = lse.shape[0] // 8
+    span = LANES // count
+    lane = lax.broadcasted_iota(jnp.int32, (8, LANES), 1)
+    value = lse[:8]
+    for i in range(1, count):
+        value = jnp.where(lane // span == i, lse[i * 8 : (i + 1) * 8], value)
+    high, middle, low = (p.astype(F32) for p in split3(value))
+    place = lane % span
+    return jnp.where(place == 0, high, jnp.where(place == 1, middle, low))
+
+
+def unpacked(last, rows):
+    count = rows // 8
+    span = LANES // count
+    found = []
+    for i in range(count):
+        high, middle, low = (
+            jnp.broadcast_to(last[:8, i * span + j : i * span + j + 1], (8, LANES))
+            for j in range(3)
+        )
+        found.append(high + middle + low)
+    return jnp.concatenate(found, axis=0)
+
+
+def read(ref, rows, latent):
     if ref.dtype == BF16:
-        high, middle, low = (jnp.broadcast_to(lse[:, i : i + 1], lse.shape) for i in range(3))
-        lse = high + middle + low
-    return ref[:, :latent].astype(F32), lse
+        out, last = take(ref, rows, latent)
+        return out, unpacked(last, rows)
+    return ref[:, :latent], ref[:, latent:]
 
 
 def merge(parts):
@@ -206,13 +267,13 @@
     return mixed, top + jnp.log(total)
 
 
-def pair_kernel(latent, got_ref, keep_ref, out_ref):
-    fill(out_ref, *merge([read(got_ref, latent), read(keep_ref, latent)]))
-
-
-def value_kernel(latent, heads, w_ref, *refs):
+def pair_kernel(rows, latent, got_ref, keep_ref, out_ref):
+    fill(out_ref, *merge([read(got_ref, rows, latent), read(keep_ref, rows, latent)]))
+
+
+def value_kernel(rows, latent, heads, w_ref, *refs):
     part_refs, out_ref = refs[:-1], refs[-1]
-    mixed = merge([read(ref, latent) for ref in part_refs])[0].astype(BF16)
+    mixed = merge([read(ref, rows, latent) for ref in part_refs])[0].astype(BF16)
     size = w_ref.shape[2]
     head = lax.broadcasted_iota(jnp.int32, (mixed.shape[0], size), 0) % heads
     weight = jnp.concatenate([w_ref[j] for j in range(heads)], axis=1)
@@ -229,16 +290,17 @@
     )
 
 
-def bounds_kernel(scale, heads, offsets, *refs):
+def bounds_kernel(scale, heads, offsets, latent, *refs):
     count = len(offsets)
     block_refs = refs[:count]
     low_ref, high_ref, after_ref, out_ref = refs[count:]
     requests, groups, pages = out_ref.shape
-    blocks = [b[...].astype(F32) for b in block_refs]
+    width = low_ref.shape[2]
+    blocks = [take(b, requests * heads, latent) for b in block_refs]
     group = lax.broadcasted_iota(jnp.int32, (groups, pages), 0)
     dims = (((1,), (1,)), ((), ()))
     for r in range(requests):
-        query = queries_of(blocks, r, heads)
+        query = queries_of(blocks, r, heads, width)
         bound = lax.dot_general(
             jnp.maximum(query, 0.0).astype(BF16),
             high_ref[r].astype(BF16),
@@ -263,7 +325,6 @@
     head_count = lax.axis_size("head")
     requests, heads, _ = q_nope.shape
     latent = w_uk.shape[2]
-    width = cache.shape[2]
     tokens = cache.shape[1]
     pages = tokens // PAGE
     groups = selected.shape[1]
@@ -290,7 +351,7 @@
 
     mine = pl.pallas_call(
         absorb_kernel,
-        out_shape=jax.ShapeDtypeStruct((rows, width), BF16),
+        out_shape=jax.ShapeDtypeStruct(block_shape(rows, latent), BF16),
         in_specs=[HBM] * 3,
         out_specs=VMEM,
         scratch_shapes=[
@@ -318,8 +379,8 @@
             jax.ShapeDtypeStruct(slots.shape, BF16),
             jax.ShapeDtypeStruct((requests, tokens, latent), BF16),
             jax.ShapeDtypeStruct((requests * groups, tokens), F32),
-            jax.ShapeDtypeStruct((requests, pages, width), F32),
-            jax.ShapeDtypeStruct((requests, pages, width), F32),
+            jax.ShapeDtypeStruct((requests, pages, cache.shape[2]), F32),
+            jax.ShapeDtypeStruct((requests, pages, cache.shape[2]), F32),
             jax.ShapeDtypeStruct((requests, groups, pages), F32),
         ),
         in_specs=[HBM] * 3 + [ANY],
@@ -336,7 +397,10 @@
     parts = pl.pallas_call(
         functools.partial(attend_kernel, scale, heads, offsets, latent),
         out_shape=tuple(
-            jax.ShapeDtypeStruct((rows, latent + LANES), BF16 if k % 2 else F32) for k in offsets
+            jax.ShapeDtypeStruct(block_shape(rows, latent), BF16)
+            if k % 2
+            else jax.ShapeDtypeStruct((rows, latent + LANES), F32)
+            for k in offsets
         ),
         in_specs=[VMEM] * (seq_count + 3),
         out_specs=(VMEM,) * seq_count,
@@ -347,8 +411,8 @@
     got = {k: swap(parts[k + 1], 1) for k in far + (0,)}
     send = {
         k: pl.pallas_call(
-            functools.partial(pair_kernel, latent),
-            out_shape=jax.ShapeDtypeStruct((rows, latent + LANES), BF16),
+            functools.partial(pair_kernel, rows, latent),
+            out_shape=jax.ShapeDtypeStruct(block_shape(rows, latent), BF16),
             in_specs=[VMEM] * 2,
             out_specs=VMEM,
             compiler_params=params(),
@@ -360,7 +424,7 @@
     arrived = [swap(send[k], k) for k in turns]
 
     bounds = pl.pallas_call(
-        functools.partial(bounds_kernel, scale, heads, offsets),
+        functools.partial(bounds_kernel, scale, heads, offsets, latent),
         out_shape=jax.ShapeDtypeStruct((requests, groups, pages), F32),
         in_specs=[VMEM] * (seq_count + 2) + [ANY],
         out_specs=VMEM,
@@ -378,7 +442,7 @@
     )(bounds, others, live)
 
     attended = pl.pallas_call(
-        functools.partial(value_kernel, latent, heads),
+        functools.partial(value_kernel, rows, latent, heads),
         out_shape=jax.ShapeDtypeStruct((requests, heads, w_uv.shape[2]), BF16),
         in_specs=[VMEM] * (half + 2),
         out_specs=VMEM,

time: 29.1 us -> 28.3 us (0.973)
  waiting for transfers between devices: 1.83 us -> 1.29 us
    ppermute x14, waiting for transfers between devices: 0.66 us -> 0.13 us  [swap(): return lax.ppermute(x, ('seq', 'head'), pairs)]
  transfers between devices with their start and end apart: 15 -> 15, of which waited for: 3 -> 2; matrix products, arithmetic and copies ran while one was open for 0% -> 0% of each run, Pallas kernels for 14% -> 14%
where the time goes in v8:
time: 28.3 us; the launch traced here: 28 us
  starting transfers between devices  18.7 us (66%)
  Pallas kernels  7.33 us (26%)
  waiting for transfers between devices  1.29 us (5%)
  between operations  0.73 us (3%)
    ppermute x14, starting transfers between devices, swap(): return lax.ppermute(x, ('seq', 'head'), pairs)  18.6 us
    pallas_call x1, Pallas kernels, local(): pl.pallas_call(stage_kernel, out_shape=(jax.ShapeDtypeStruct(slots.shape,...  2.66 us
    pallas_call x1, Pallas kernels, local(): pl.pallas_call(absorb_kernel, out_shape=jax.ShapeDtypeStruct(block_shape(...  1.46 us
    ppermute x1, waiting for transfers between devices, local(): lax.ppermute(bounds, 'head', [(i, i ^ 1) for i in range(head_count)])  1.16 us
    pallas_call x1, Pallas kernels, local(): pl.pallas_call(functools.partial(attend_kernel, scale, heads, offsets, la...  0.97 us
    pallas_call x1, Pallas kernels, local(): pl.pallas_call(functools.partial(value_kernel, rows, latent, heads), out_...  0.96 us
    pallas_call x1, Pallas kernels, local(): pl.pallas_call(largest_kernel, out_shape=jax.ShapeDtypeStruct((requests,...  0.61 us
  transfers between devices with their start and end apart: 15, of which 2 were waited for; matrix products, arithmetic and copies ran while one was open for 0% of the time, Pallas kernels for 14%

profile of v8, /device:TPU:0, one launch (start us, length us, event | category | flops | bytes accessed | tf_op | source)
XLA Modules:
  0.0 28.0 jit_solution(14146425026243144755)
XLA Ops:
  0.6 1.5 %absorb.1.refs_0_ = bf16[144,128]{1,0:T(8,128)(2,1)S(1)} custom-call(bf16[4,8,128]{2,1,0:T(8,128)(2,1)} %nope_hbm.1, bf16[4,8,64]{2,1,0:T(8,128)(2,1)} %rope_hbm.1, bf16[8,128,512]{2,1,0:T(8,128)(2,1)} %w_hbm.1), custom_call_target="tpu_custom_call" | custom-call | tf_op jit(solution)/shard_map/absorb/pallas_call | solution.py:352
  2.1 4.6 %collective-permute-start.5 = (bf16[144,128]{1,0:T(8,128)(2,1)S(1)}, bf16[144,128]{1,0:T(8,128)(2,1)S(1)}, u32[]{:S(2)}, u32[]{:S(2)}) collective-permute-start(bf16[144,128]{1,0:T(8,128)(2,1)S(1)} %absorb.1.refs_0_), channel_id=1, source_target_pairs={{0,13},{1,12},{2,15},{3,14},{4,9},{5,8},{6,11},{7,10},{8,5},{9,4},... | collective-permute-start | bytes 110600 | tf_op jit(solution)/shard_map/ppermute | solution.py:350
  6.7 0.0 collective-permute-start.3
  6.7 0.9 %collective-permute-start.1 = (bf16[144,128]{1,0:T(8,128)(2,1)S(1)}, bf16[144,128]{1,0:T(8,128)(2,1)S(1)}, u32[]{:S(2)}, u32[]{:S(2)}) collective-permute-start(bf16[144,128]{1,0:T(8,128)(2,1)S(1)} %absorb.1.refs_0_), channel_id=1, source_target_pairs={{0,5},{1,4},{2,7},{3,6},{4,1},{5,0},{6,3},{7,2},{8,13},{9,12},{10,... | collective-permute-start | bytes 110600 | tf_op jit(solution)/shard_map/ppermute | solution.py:350
  7.6 2.3 %collective-permute-start.2 = (bf16[144,128]{1,0:T(8,128)(2,1)S(1)}, bf16[144,128]{1,0:T(8,128)(2,1)S(1)}, u32[]{:S(2)}, u32[]{:S(2)}) collective-permute-start(bf16[144,128]{1,0:T(8,128)(2,1)S(1)} %absorb.1.refs_0_), channel_id=1, source_target_pairs={{0,6},{1,7},{2,4},{3,5},{4,2},{5,3},{6,0},{7,1},{8,14},{9,15},{10,... | collective-permute-start | bytes 110600 | tf_op jit(solution)/shard_map/ppermute | solution.py:350
  9.9 0.0 collective-permute-start
  9.9 0.0 collective-permute-done.5.refs_6_
  9.9 1.7 %collective-permute-start.6 = (bf16[144,128]{1,0:T(8,128)(2,1)S(1)}, bf16[144,128]{1,0:T(8,128)(2,1)S(1)}, u32[]{:S(2)}, u32[]{:S(2)}) collective-permute-start(bf16[144,128]{1,0:T(8,128)(2,1)S(1)} %collective-permute-done.5.refs_6_), channel_id=1, source_target_pairs={{0,3},{1,2},{2,1},{3,0},{4,7},{5,6},{6,5},{7,4},{8,11},{9,10},{10,... | collective-permute-start | bytes 110600 | tf_op jit(solution)/shard_map/ppermute | solution.py:350
  11.7 0.0 collective-permute-done.3.refs_4_
  11.7 1.1 %collective-permute-start.4 = (bf16[144,128]{1,0:T(8,128)(2,1)S(1)}, bf16[144,128]{1,0:T(8,128)(2,1)S(1)}, u32[]{:S(2)}, u32[]{:S(2)}) collective-permute-start(bf16[144,128]{1,0:T(8,128)(2,1)S(1)} %collective-permute-done.3.refs_4_), channel_id=1, source_target_pairs={{0,3},{1,2},{2,1},{3,0},{4,7},{5,6},{6,5},{7,4},{8,11},{9,10},{10,... | collective-permute-start | bytes 110600 | tf_op jit(solution)/shard_map/ppermute | solution.py:350
  12.7 0.0 collective-permute-done.1.after_ref.refs_2_
  12.7 2.7 %stage_cache.1 = (bf16[4,576,512]{2,1,0:T(8,128)(2,1)S(1)}, bf16[4,512,512]{2,1,0:T(8,128)(2,1)S(1)}, f32[32,512]{1,0:T(8,128)S(1)}, f32[4,8,576]{2,1,0:T(8,128)...) custom-call(bf16[4,576,512]{2,1,0:T(8,128)(2,1)} %bitcast.1, s32[4,8,32]{2,1,0:T(8,128)} %selected_hbm.1, ...), custom_call_target="tpu_custom_call" | custom-call | tf_op jit(solution)/shard_map/stage_cache/pallas_call | solution.py:376
  15.4 0.0 collective-permute-done.2.refs_3_
  15.4 0.0 collective-permute-done.refs_1_
  15.4 0.0 collective-permute-done.6.refs_7_
  15.4 0.0 collective-permute-done.4.refs_5_
  15.5 0.0 copy-start
  15.5 1.0 %attend.1 = (f32[32,640]{1,0:T(8,128)S(1)}, bf16[144,128]{1,0:T(8,128)(2,1)S(1)}, f32[32,640]{1,0:T(8,128)S(1)}, bf16[144,128]{1,0:T(8,128)(2,1)S(1)}, f32[32,64...) custom-call(bf16[144,128]{1,0:T(8,128)(2,1)S(1)} %absorb.1.refs_0_, ...), custom_call_target="tpu_custom_call" | custom-call | tf_op jit(solution)/shard_map/attend/pallas_call | solution.py:397
  16.4 0.7 %collective-permute-start.8 = (bf16[144,128]{1,0:T(8,128)(2,1)S(1)}, bf16[144,128]{1,0:T(8,128)(2,1)S(1)}, u32[]{:S(2)}, u32[]{:S(2)}) collective-permute-start(bf16[144,128]{1,0:T(8,128)(2,1)S(1)} %get-tuple-element.21), channel_id=1, source_target_pairs={{0,3},{1,2},{2,1},{3,0},{4,7},{5,6},{6,5},{7,4},{8,11},{9,10},{10,... | collective-permute-start | bytes 110600 | tf_op jit(solution)/shard_map/ppermute | solution.py:350
  17.2 1.1 %collective-permute-start.10 = (bf16[144,128]{1,0:T(8,128)(2,1)S(1)}, bf16[144,128]{1,0:T(8,128)(2,1)S(1)}, u32[]{:S(2)}, u32[]{:S(2)}) collective-permute-start(bf16[144,128]{1,0:T(8,128)(2,1)S(1)} %get-tuple-element.23), channel_id=1, source_target_pairs={{0,3},{1,2},{2,1},{3,0},{4,7},{5,6},{6,5},{7,4},{8,11},{9,10},{10,... | collective-permute-start | bytes 110600 | tf_op jit(solution)/shard_map/ppermute | solution.py:350
  18.3 0.7 %collective-permute-start.12 = (bf16[144,128]{1,0:T(8,128)(2,1)S(1)}, bf16[144,128]{1,0:T(8,128)(2,1)S(1)}, u32[]{:S(2)}, u32[]{:S(2)}) collective-permute-start(bf16[144,128]{1,0:T(8,128)(2,1)S(1)} %get-tuple-element.25), channel_id=1, source_target_pairs={{0,3},{1,2},{2,1},{3,0},{4,7},{5,6},{6,5},{7,4},{8,11},{9,10},{10,... | collective-permute-start | bytes 110600 | tf_op jit(solution)/shard_map/ppermute | solution.py:350
  18.9 1.1 %collective-permute-start.7 = (bf16[144,128]{1,0:T(8,128)(2,1)S(1)}, bf16[144,128]{1,0:T(8,128)(2,1)S(1)}, u32[]{:S(2)}, u32[]{:S(2)}) collective-permute-start(bf16[144,128]{1,0:T(8,128)(2,1)S(1)} %get-tuple-element.20), channel_id=1, source_target_pairs={{0,3},{1,2},{2,1},{3,0},{4,7},{5,6},{6,5},{7,4},{8,11},{9,10},{10,... | collective-permute-start | bytes 110600 | tf_op jit(solution)/shard_map/ppermute | solution.py:350
  20.0 0.0 collective-permute-done.8.got_ref
  20.0 0.1 merge_pair.3
  20.1 2.1 %collective-permute-start.9 = (bf16[144,128]{1,0:T(8,128)(2,1)S(1)}, bf16[144,128]{1,0:T(8,128)(2,1)S(1)}, u32[]{:S(2)}, u32[]{:S(2)}) collective-permute-start(bf16[144,128]{1,0:T(8,128)(2,1)S(1)} %merge_pair.3), channel_id=1, source_target_pairs={{0,13},{1,12},{2,15},{3,14},{4,9},{5,8},{6,11},{7,10},{8,5},{9,4},... | collective-permute-start | bytes 110600 | tf_op jit(solution)/shard_map/ppermute | solution.py:350
  22.2 0.0 collective-permute-done.10.got_ref
  22.2 0.1 merge_pair.4.refs_10_
  22.3 0.2 collective-permute-start.11
  22.6 0.0 collective-permute-done.12.got_ref
  22.6 0.1 merge_pair.5
  22.7 2.1 %collective-permute-start.13 = (bf16[144,128]{1,0:T(8,128)(2,1)S(1)}, bf16[144,128]{1,0:T(8,128)(2,1)S(1)}, u32[]{:S(2)}, u32[]{:S(2)}) collective-permute-start(bf16[144,128]{1,0:T(8,128)(2,1)S(1)} %merge_pair.5), channel_id=1, source_target_pairs={{0,9},{1,8},{2,11},{3,10},{4,13},{5,12},{6,15},{7,14},{8,1},{9,0},... | collective-permute-start | bytes 110600 | tf_op jit(solution)/shard_map/ppermute | solution.py:350
  24.8 0.3 %page_bounds.1.mine_ref = f32[4,8,8]{2,1,0:T(8,128)S(1)} custom-call(bf16[144,128]{1,0:T(8,128)(2,1)S(1)} %absorb.1.refs_0_, bf16[144,128]{1,0:T(8,128)(2,1)S(1)} %collective-permute-done.refs_1_, bf16[144,128]{1,0:T(8,128)(2,1)S(1)} %collective-permute-done.1.after_ref.refs_2_, bf16[144,128]{1,0:T(8,128)(2,1)S(1)} %collective-permute-done.2.refs_3_, ...), custom_call_target="tpu_custom_call" | custom-call | tf_op jit(solution)/shard_map/page_bounds/pallas_call | solution.py:426
  25.1 0.1 collective-permute-start.14
  25.2 1.2 %collective-permute-done.14.other_ref = f32[4,8,8]{2,1,0:T(8,128)S(1)} collective-permute-done((f32[4,8,8]{2,1,0:T(8,128)S(1)}, f32[4,8,8]{2,1,0:T(8,128)S(1)}, u32[]{:S(2)}, u32[]{:S(2)}) %collective-permute-start.14) | collective-permute-done | bytes 1056 | tf_op jit(solution)/shard_map/ppermute | solution.py:434
  26.4 0.6 %group_bounds.1 = f32[4,8,8]{2,1,0:T(8,128)} custom-call(f32[4,8,8]{2,1,0:T(8,128)S(1)} %page_bounds.1.mine_ref, f32[4,8,8]{2,1,0:T(8,128)S(1)} %collective-permute-done.14.other_ref, f32[4,8,8]{2,1,0:T(8,128)S(1)} %get-tuple-element.29.live_ref), custom_call_target="tpu_custom_call" | custom-call | tf_op jit(solution)/shard_map/group_bounds/pallas_call | solution.py:435
  27.0 0.0 collective-permute-done.7.refs_1_
  27.0 0.0 collective-permute-done.9.refs_2_
  27.0 0.0 collective-permute-done.11.refs_3_
  27.0 0.1 collective-permute-done.13.refs_4_
  27.1 0.0 copy-done
  27.1 1.0 %merge_and_value.1 = bf16[4,8,128]{2,1,0:T(8,128)(2,1)} custom-call(bf16[8,512,128]{2,1,0:T(8,128)(2,1)S(1)} %copy-done, f32[32,640]{1,0:T(8,128)S(1)} %get-tuple-element.19.refs_0_, bf16[144,128]{1,0:T(8,128)(2,1)S(1)} %collective-permute-done.7.refs_1_, bf16[144,128]{1,0:T(8,128)(2,1)S(1)} %collective-permute-done.9.refs_2_, ...), custom_call_target="tpu_custom_call" | custom-call | tf_op jit(solution)/shard_map/merge_and_value/pallas_call | solution.py:444
Async XLA Ops:
  2.1 7.8 %collective-permute-start.5 = (bf16[144,128]{1,0:T(8,128)(2,1)S(1)}, bf16[144,128]{1,0:T(8,128)(2,1)S(1)}, u32[]{:S(2)}, u32[]{:S(2)}) collective-permute-start(bf16[144,128]{1,0:T(8,128)(2,1)S(1)} %absorb.1.refs_0_), channel_id=1, source_target_pairs={{0,13},{1,12},{2,15},{3,14},{4,9},{5,8},{6,11},{7,10},{8,5},{9,4},... | collective-permute-start | bytes 110600 | tf_op jit(solution)/shard_map/ppermute | solution.py:350
  6.7 5.0 %collective-permute-start.3 = (bf16[144,128]{1,0:T(8,128)(2,1)S(1)}, bf16[144,128]{1,0:T(8,128)(2,1)S(1)}, u32[]{:S(2)}, u32[]{:S(2)}) collective-permute-start(bf16[144,128]{1,0:T(8,128)(2,1)S(1)} %absorb.1.refs_0_), channel_id=1, source_target_pairs={{0,9},{1,8},{2,11},{3,10},{4,13},{5,12},{6,15},{7,14},{8,1},{9,0},... | collective-permute-start | bytes 110600 | tf_op jit(solution)/shard_map/ppermute | solution.py:350
  6.7 6.1 %collective-permute-start.1 = (bf16[144,128]{1,0:T(8,128)(2,1)S(1)}, bf16[144,128]{1,0:T(8,128)(2,1)S(1)}, u32[]{:S(2)}, u32[]{:S(2)}) collective-permute-start(bf16[144,128]{1,0:T(8,128)(2,1)S(1)} %absorb.1.refs_0_), channel_id=1, source_target_pairs={{0,5},{1,4},{2,7},{3,6},{4,1},{5,0},{6,3},{7,2},{8,13},{9,12},{10,... | collective-permute-start | bytes 110600 | tf_op jit(solution)/shard_map/ppermute | solution.py:350
  7.6 7.8 %collective-permute-start.2 = (bf16[144,128]{1,0:T(8,128)(2,1)S(1)}, bf16[144,128]{1,0:T(8,128)(2,1)S(1)}, u32[]{:S(2)}, u32[]{:S(2)}) collective-permute-start(bf16[144,128]{1,0:T(8,128)(2,1)S(1)} %absorb.1.refs_0_), channel_id=1, source_target_pairs={{0,6},{1,7},{2,4},{3,5},{4,2},{5,3},{6,0},{7,1},{8,14},{9,15},{10,... | collective-permute-start | bytes 110600 | tf_op jit(solution)/shard_map/ppermute | solution.py:350
  9.9 5.5 %collective-permute-start = (bf16[144,128]{1,0:T(8,128)(2,1)S(1)}, bf16[144,128]{1,0:T(8,128)(2,1)S(1)}, u32[]{:S(2)}, u32[]{:S(2)}) collective-permute-start(bf16[144,128]{1,0:T(8,128)(2,1)S(1)} %absorb.1.refs_0_), channel_id=1, source_target_pairs={{0,3},{1,2},{2,1},{3,0},{4,7},{5,6},{6,5},{7,4},{8,11},{9,10},{10,... | collective-permute-start | bytes 110600 | tf_op jit(solution)/shard_map/ppermute | solution.py:350
  9.9 5.5 %collective-permute-start.6 = (bf16[144,128]{1,0:T(8,128)(2,1)S(1)}, bf16[144,128]{1,0:T(8,128)(2,1)S(1)}, u32[]{:S(2)}, u32[]{:S(2)}) collective-permute-start(bf16[144,128]{1,0:T(8,128)(2,1)S(1)} %collective-permute-done.5.refs_6_), channel_id=1, source_target_pairs={{0,3},{1,2},{2,1},{3,0},{4,7},{5,6},{6,5},{7,4},{8,11},{9,10},{10,... | collective-permute-start | bytes 110600 | tf_op jit(solution)/shard_map/ppermute | solution.py:350
  11.7 3.8 %collective-permute-start.4 = (bf16[144,128]{1,0:T(8,128)(2,1)S(1)}, bf16[144,128]{1,0:T(8,128)(2,1)S(1)}, u32[]{:S(2)}, u32[]{:S(2)}) collective-permute-start(bf16[144,128]{1,0:T(8,128)(2,1)S(1)} %collective-permute-done.3.refs_4_), channel_id=1, source_target_pairs={{0,3},{1,2},{2,1},{3,0},{4,7},{5,6},{6,5},{7,4},{8,11},{9,10},{10,... | collective-permute-start | bytes 110600 | tf_op jit(solution)/shard_map/ppermute | solution.py:350
  15.5 11.6 %copy-start = (bf16[8,512,128]{2,1,0:T(8,128)(2,1)S(1)}, bf16[8,512,128]{2,1,0:T(8,128)(2,1)}, u32[]{:S(2)}) copy-start(bf16[8,512,128]{2,1,0:T(8,128)(2,1)} %w_ref.1) | copy-start | bytes 3145732
  16.4 3.6 %collective-permute-start.8 = (bf16[144,128]{1,0:T(8,128)(2,1)S(1)}, bf16[144,128]{1,0:T(8,128)(2,1)S(1)}, u32[]{:S(2)}, u32[]{:S(2)}) collective-permute-start(bf16[144,128]{1,0:T(8,128)(2,1)S(1)} %get-tuple-element.21), channel_id=1, source_target_pairs={{0,3},{1,2},{2,1},{3,0},{4,7},{5,6},{6,5},{7,4},{8,11},{9,10},{10,... | collective-permute-start | bytes 110600 | tf_op jit(solution)/shard_map/ppermute | solution.py:350
  17.2 5.0 %collective-permute-start.10 = (bf16[144,128]{1,0:T(8,128)(2,1)S(1)}, bf16[144,128]{1,0:T(8,128)(2,1)S(1)}, u32[]{:S(2)}, u32[]{:S(2)}) collective-permute-start(bf16[144,128]{1,0:T(8,128)(2,1)S(1)} %get-tuple-element.23), channel_id=1, source_target_pairs={{0,3},{1,2},{2,1},{3,0},{4,7},{5,6},{6,5},{7,4},{8,11},{9,10},{10,... | collective-permute-start | bytes 110600 | tf_op jit(solution)/shard_map/ppermute | solution.py:350
  18.3 4.3 %collective-permute-start.12 = (bf16[144,128]{1,0:T(8,128)(2,1)S(1)}, bf16[144,128]{1,0:T(8,128)(2,1)S(1)}, u32[]{:S(2)}, u32[]{:S(2)}) collective-permute-start(bf16[144,128]{1,0:T(8,128)(2,1)S(1)} %get-tuple-element.25), channel_id=1, source_target_pairs={{0,3},{1,2},{2,1},{3,0},{4,7},{5,6},{6,5},{7,4},{8,11},{9,10},{10,... | collective-permute-start | bytes 110600 | tf_op jit(solution)/shard_map/ppermute | solution.py:350
  18.9 8.1 %collective-permute-start.7 = (bf16[144,128]{1,0:T(8,128)(2,1)S(1)}, bf16[144,128]{1,0:T(8,128)(2,1)S(1)}, u32[]{:S(2)}, u32[]{:S(2)}) collective-permute-start(bf16[144,128]{1,0:T(8,128)(2,1)S(1)} %get-tuple-element.20), channel_id=1, source_target_pairs={{0,3},{1,2},{2,1},{3,0},{4,7},{5,6},{6,5},{7,4},{8,11},{9,10},{10,... | collective-permute-start | bytes 110600 | tf_op jit(solution)/shard_map/ppermute | solution.py:350
  20.1 6.8 %collective-permute-start.9 = (bf16[144,128]{1,0:T(8,128)(2,1)S(1)}, bf16[144,128]{1,0:T(8,128)(2,1)S(1)}, u32[]{:S(2)}, u32[]{:S(2)}) collective-permute-start(bf16[144,128]{1,0:T(8,128)(2,1)S(1)} %merge_pair.3), channel_id=1, source_target_pairs={{0,13},{1,12},{2,15},{3,14},{4,9},{5,8},{6,11},{7,10},{8,5},{9,4},... | collective-permute-start | bytes 110600 | tf_op jit(solution)/shard_map/ppermute | solution.py:350
  22.3 4.6 %collective-permute-start.11 = (bf16[144,128]{1,0:T(8,128)(2,1)S(1)}, bf16[144,128]{1,0:T(8,128)(2,1)S(1)}, u32[]{:S(2)}, u32[]{:S(2)}) collective-permute-start(bf16[144,128]{1,0:T(8,128)(2,1)S(1)} %merge_pair.4.refs_10_), channel_id=1, source_target_pairs={{0,5},{1,4},{2,7},{3,6},{4,1},{5,0},{6,3},{7,2},{8,13},{9,12},{10,... | collective-permute-start | bytes 110600 | tf_op jit(solution)/shard_map/ppermute | solution.py:350
  22.7 4.3 %collective-permute-start.13 = (bf16[144,128]{1,0:T(8,128)(2,1)S(1)}, bf16[144,128]{1,0:T(8,128)(2,1)S(1)}, u32[]{:S(2)}, u32[]{:S(2)}) collective-permute-start(bf16[144,128]{1,0:T(8,128)(2,1)S(1)} %merge_pair.5), channel_id=1, source_target_pairs={{0,9},{1,8},{2,11},{3,10},{4,13},{5,12},{6,15},{7,14},{8,1},{9,0},... | collective-permute-start | bytes 110600 | tf_op jit(solution)/shard_map/ppermute | solution.py:350
  25.1 1.2 %collective-permute-start.14 = (f32[4,8,8]{2,1,0:T(8,128)S(1)}, f32[4,8,8]{2,1,0:T(8,128)S(1)}, u32[]{:S(2)}, u32[]{:S(2)}) collective-permute-start(f32[4,8,8]{2,1,0:T(8,128)S(1)} %page_bounds.1.mine_ref), channel_id=1, source_target_pairs={{0,1},{1,0},{2,3},{3,2},{4,5},{5,4},{6,7},{7,6},{8,9},{9,8},{10,11... | collective-permute-start | bytes 3080 | tf_op jit(solution)/shard_map/ppermute | solution.py:434

commit v9 on v8

--- a/solution.py
+++ b/solution.py
@@ -63,7 +63,7 @@
         )
         for i in range(pieces)
     ]
-    for copy in small + large:
+    for copy in large + small:
         copy.start()
     for copy in small:
         copy.wait()
@@ -73,14 +73,17 @@
     fold = LANES // rope.shape[1]
     part = rows // fold
     rope = jnp.concatenate([rope[i * part : (i + 1) * part] for i in range(fold)], axis=1)
+    wides = [
+        jnp.concatenate(
+            [jnp.where(head == i * step + j, nope, 0.0) for j in range(step)], axis=1
+        ).astype(BF16)
+        for i in range(pieces)
+    ]
     total = jnp.zeros((rows, latent), F32)
     for i, copy in enumerate(large):
-        wide = jnp.concatenate(
-            [jnp.where(head == i * step + j, nope, 0.0) for j in range(step)], axis=1
-        ).astype(BF16)
         copy.wait()
         weight = w_ref[i * step : (i + 1) * step].reshape(step * size, latent)
-        total += jnp.dot(wide, weight, preferred_element_type=F32)
+        total += jnp.dot(wides[i], weight, preferred_element_type=F32)
     put(out_ref, total, rope)
 
 

time: 28.3 us -> 28.4 us (level)
  no operation moved by 1% of the time
where the time goes in v9:
time: 28.4 us; the launch traced here: 28.1 us
  starting transfers between devices  18.7 us (66%)
  Pallas kernels  7.37 us (26%)
  waiting for transfers between devices  1.3 us (5%)
  between operations  0.73 us (3%)
    ppermute x14, starting transfers between devices, swap(): return lax.ppermute(x, ('seq', 'head'), pairs)  18.6 us
    pallas_call x1, Pallas kernels, local(): pl.pallas_call(stage_kernel, out_shape=(jax.ShapeDtypeStruct(slots.shape,...  2.66 us
    pallas_call x1, Pallas kernels, local(): pl.pallas_call(absorb_kernel, out_shape=jax.ShapeDtypeStruct(block_shape(...  1.51 us
    ppermute x1, waiting for transfers between devices, local(): lax.ppermute(bounds, 'head', [(i, i ^ 1) for i in range(head_count)])  1.16 us
    pallas_call x1, Pallas kernels, local(): pl.pallas_call(functools.partial(value_kernel, rows, latent, heads), out_...  0.96 us
    pallas_call x1, Pallas kernels, local(): pl.pallas_call(functools.partial(attend_kernel, scale, heads, offsets, la...  0.96 us
    pallas_call x1, Pallas kernels, local(): pl.pallas_call(largest_kernel, out_shape=jax.ShapeDtypeStruct((requests,...  0.61 us
  transfers between devices with their start and end apart: 15, of which 2 were waited for; matrix products, arithmetic and copies ran while one was open for 0% of the time, Pallas kernels for 14%

profile of v9, /device:TPU:0, one launch (start us, length us, event | category | flops | bytes accessed | tf_op | source)
XLA Modules:
  0.0 28.1 jit_solution(14098300653051932368)
XLA Ops:
  0.6 1.5 %absorb.1.refs_0_ = bf16[144,128]{1,0:T(8,128)(2,1)S(1)} custom-call(bf16[4,8,128]{2,1,0:T(8,128)(2,1)} %nope_hbm.1, bf16[4,8,64]{2,1,0:T(8,128)(2,1)} %rope_hbm.1, bf16[8,128,512]{2,1,0:T(8,128)(2,1)} %w_hbm.1), custom_call_target="tpu_custom_call" | custom-call | tf_op jit(solution)/shard_map/absorb/pallas_call | solution.py:355
  2.1 4.6 %collective-permute-start.5 = (bf16[144,128]{1,0:T(8,128)(2,1)S(1)}, bf16[144,128]{1,0:T(8,128)(2,1)S(1)}, u32[]{:S(2)}, u32[]{:S(2)}) collective-permute-start(bf16[144,128]{1,0:T(8,128)(2,1)S(1)} %absorb.1.refs_0_), channel_id=1, source_target_pairs={{0,13},{1,12},{2,15},{3,14},{4,9},{5,8},{6,11},{7,10},{8,5},{9,4},... | collective-permute-start | bytes 110600 | tf_op jit(solution)/shard_map/ppermute | solution.py:353
  6.7 0.0 collective-permute-start.3
  6.7 0.9 %collective-permute-start.1 = (bf16[144,128]{1,0:T(8,128)(2,1)S(1)}, bf16[144,128]{1,0:T(8,128)(2,1)S(1)}, u32[]{:S(2)}, u32[]{:S(2)}) collective-permute-start(bf16[144,128]{1,0:T(8,128)(2,1)S(1)} %absorb.1.refs_0_), channel_id=1, source_target_pairs={{0,5},{1,4},{2,7},{3,6},{4,1},{5,0},{6,3},{7,2},{8,13},{9,12},{10,... | collective-permute-start | bytes 110600 | tf_op jit(solution)/shard_map/ppermute | solution.py:353
  7.6 2.3 %collective-permute-start.2 = (bf16[144,128]{1,0:T(8,128)(2,1)S(1)}, bf16[144,128]{1,0:T(8,128)(2,1)S(1)}, u32[]{:S(2)}, u32[]{:S(2)}) collective-permute-start(bf16[144,128]{1,0:T(8,128)(2,1)S(1)} %absorb.1.refs_0_), channel_id=1, source_target_pairs={{0,6},{1,7},{2,4},{3,5},{4,2},{5,3},{6,0},{7,1},{8,14},{9,15},{10,... | collective-permute-start | bytes 110600 | tf_op jit(solution)/shard_map/ppermute | solution.py:353
  10.0 0.0 collective-permute-start
  10.0 0.0 collective-permute-done.5.refs_6_
  10.0 1.7 %collective-permute-start.6 = (bf16[144,128]{1,0:T(8,128)(2,1)S(1)}, bf16[144,128]{1,0:T(8,128)(2,1)S(1)}, u32[]{:S(2)}, u32[]{:S(2)}) collective-permute-start(bf16[144,128]{1,0:T(8,128)(2,1)S(1)} %collective-permute-done.5.refs_6_), channel_id=1, source_target_pairs={{0,3},{1,2},{2,1},{3,0},{4,7},{5,6},{6,5},{7,4},{8,11},{9,10},{10,... | collective-permute-start | bytes 110600 | tf_op jit(solution)/shard_map/ppermute | solution.py:353
  11.7 0.0 collective-permute-done.3.refs_4_
  11.7 1.1 %collective-permute-start.4 = (bf16[144,128]{1,0:T(8,128)(2,1)S(1)}, bf16[144,128]{1,0:T(8,128)(2,1)S(1)}, u32[]{:S(2)}, u32[]{:S(2)}) collective-permute-start(bf16[144,128]{1,0:T(8,128)(2,1)S(1)} %collective-permute-done.3.refs_4_), channel_id=1, source_target_pairs={{0,3},{1,2},{2,1},{3,0},{4,7},{5,6},{6,5},{7,4},{8,11},{9,10},{10,... | collective-permute-start | bytes 110600 | tf_op jit(solution)/shard_map/ppermute | solution.py:353
  12.8 0.0 collective-permute-done.1.after_ref.refs_2_
  12.8 2.7 %stage_cache.1 = (bf16[4,576,512]{2,1,0:T(8,128)(2,1)S(1)}, bf16[4,512,512]{2,1,0:T(8,128)(2,1)S(1)}, f32[32,512]{1,0:T(8,128)S(1)}, f32[4,8,576]{2,1,0:T(8,128)...) custom-call(bf16[4,576,512]{2,1,0:T(8,128)(2,1)} %bitcast.1, s32[4,8,32]{2,1,0:T(8,128)} %selected_hbm.1, ...), custom_call_target="tpu_custom_call" | custom-call | tf_op jit(solution)/shard_map/stage_cache/pallas_call | solution.py:379
  15.5 0.0 collective-permute-done.2.refs_3_
  15.5 0.0 collective-permute-done.refs_1_
  15.5 0.0 collective-permute-done.6.refs_7_
  15.5 0.0 collective-permute-done.4.refs_5_
  15.5 0.0 copy-start
  15.5 1.0 %attend.1 = (f32[32,640]{1,0:T(8,128)S(1)}, bf16[144,128]{1,0:T(8,128)(2,1)S(1)}, f32[32,640]{1,0:T(8,128)S(1)}, bf16[144,128]{1,0:T(8,128)(2,1)S(1)}, f32[32,64...) custom-call(bf16[144,128]{1,0:T(8,128)(2,1)S(1)} %absorb.1.refs_0_, ...), custom_call_target="tpu_custom_call" | custom-call | tf_op jit(solution)/shard_map/attend/pallas_call | solution.py:400
  16.5 0.7 %collective-permute-start.8 = (bf16[144,128]{1,0:T(8,128)(2,1)S(1)}, bf16[144,128]{1,0:T(8,128)(2,1)S(1)}, u32[]{:S(2)}, u32[]{:S(2)}) collective-permute-start(bf16[144,128]{1,0:T(8,128)(2,1)S(1)} %get-tuple-element.21), channel_id=1, source_target_pairs={{0,3},{1,2},{2,1},{3,0},{4,7},{5,6},{6,5},{7,4},{8,11},{9,10},{10,... | collective-permute-start | bytes 110600 | tf_op jit(solution)/shard_map/ppermute | solution.py:353
  17.2 1.1 %collective-permute-start.10 = (bf16[144,128]{1,0:T(8,128)(2,1)S(1)}, bf16[144,128]{1,0:T(8,128)(2,1)S(1)}, u32[]{:S(2)}, u32[]{:S(2)}) collective-permute-start(bf16[144,128]{1,0:T(8,128)(2,1)S(1)} %get-tuple-element.23), channel_id=1, source_target_pairs={{0,3},{1,2},{2,1},{3,0},{4,7},{5,6},{6,5},{7,4},{8,11},{9,10},{10,... | collective-permute-start | bytes 110600 | tf_op jit(solution)/shard_map/ppermute | solution.py:353
  18.3 0.7 %collective-permute-start.12 = (bf16[144,128]{1,0:T(8,128)(2,1)S(1)}, bf16[144,128]{1,0:T(8,128)(2,1)S(1)}, u32[]{:S(2)}, u32[]{:S(2)}) collective-permute-start(bf16[144,128]{1,0:T(8,128)(2,1)S(1)} %get-tuple-element.25), channel_id=1, source_target_pairs={{0,3},{1,2},{2,1},{3,0},{4,7},{5,6},{6,5},{7,4},{8,11},{9,10},{10,... | collective-permute-start | bytes 110600 | tf_op jit(solution)/shard_map/ppermute | solution.py:353
  19.0 1.1 %collective-permute-start.7 = (bf16[144,128]{1,0:T(8,128)(2,1)S(1)}, bf16[144,128]{1,0:T(8,128)(2,1)S(1)}, u32[]{:S(2)}, u32[]{:S(2)}) collective-permute-start(bf16[144,128]{1,0:T(8,128)(2,1)S(1)} %get-tuple-element.20), channel_id=1, source_target_pairs={{0,3},{1,2},{2,1},{3,0},{4,7},{5,6},{6,5},{7,4},{8,11},{9,10},{10,... | collective-permute-start | bytes 110600 | tf_op jit(solution)/shard_map/ppermute | solution.py:353
  20.0 0.0 collective-permute-done.8.got_ref
  20.1 0.1 merge_pair.3
  20.2 2.1 %collective-permute-start.9 = (bf16[144,128]{1,0:T(8,128)(2,1)S(1)}, bf16[144,128]{1,0:T(8,128)(2,1)S(1)}, u32[]{:S(2)}, u32[]{:S(2)}) collective-permute-start(bf16[144,128]{1,0:T(8,128)(2,1)S(1)} %merge_pair.3), channel_id=1, source_target_pairs={{0,13},{1,12},{2,15},{3,14},{4,9},{5,8},{6,11},{7,10},{8,5},{9,4},... | collective-permute-start | bytes 110600 | tf_op jit(solution)/shard_map/ppermute | solution.py:353
  22.3 0.0 collective-permute-done.10.got_ref
  22.3 0.1 merge_pair.4.refs_10_
  22.4 0.2 collective-permute-start.11
  22.6 0.0 collective-permute-done.12.got_ref
  22.6 0.1 merge_pair.5
  22.8 2.1 %collective-permute-start.13 = (bf16[144,128]{1,0:T(8,128)(2,1)S(1)}, bf16[144,128]{1,0:T(8,128)(2,1)S(1)}, u32[]{:S(2)}, u32[]{:S(2)}) collective-permute-start(bf16[144,128]{1,0:T(8,128)(2,1)S(1)} %merge_pair.5), channel_id=1, source_target_pairs={{0,9},{1,8},{2,11},{3,10},{4,13},{5,12},{6,15},{7,14},{8,1},{9,0},... | collective-permute-start | bytes 110600 | tf_op jit(solution)/shard_map/ppermute | solution.py:353
  24.8 0.3 %page_bounds.1.mine_ref = f32[4,8,8]{2,1,0:T(8,128)S(1)} custom-call(bf16[144,128]{1,0:T(8,128)(2,1)S(1)} %absorb.1.refs_0_, bf16[144,128]{1,0:T(8,128)(2,1)S(1)} %collective-permute-done.refs_1_, bf16[144,128]{1,0:T(8,128)(2,1)S(1)} %collective-permute-done.1.after_ref.refs_2_, bf16[144,128]{1,0:T(8,128)(2,1)S(1)} %collective-permute-done.2.refs_3_, ...), custom_call_target="tpu_custom_call" | custom-call | tf_op jit(solution)/shard_map/page_bounds/pallas_call | solution.py:429
  25.2 0.1 collective-permute-start.14
  25.2 1.2 %collective-permute-done.14.other_ref = f32[4,8,8]{2,1,0:T(8,128)S(1)} collective-permute-done((f32[4,8,8]{2,1,0:T(8,128)S(1)}, f32[4,8,8]{2,1,0:T(8,128)S(1)}, u32[]{:S(2)}, u32[]{:S(2)}) %collective-permute-start.14) | collective-permute-done | bytes 1056 | tf_op jit(solution)/shard_map/ppermute | solution.py:437
  26.4 0.6 %group_bounds.1 = f32[4,8,8]{2,1,0:T(8,128)} custom-call(f32[4,8,8]{2,1,0:T(8,128)S(1)} %page_bounds.1.mine_ref, f32[4,8,8]{2,1,0:T(8,128)S(1)} %collective-permute-done.14.other_ref, f32[4,8,8]{2,1,0:T(8,128)S(1)} %get-tuple-element.29.live_ref), custom_call_target="tpu_custom_call" | custom-call | tf_op jit(solution)/shard_map/group_bounds/pallas_call | solution.py:438
  27.0 0.0 collective-permute-done.7.refs_1_
  27.0 0.0 collective-permute-done.9.refs_2_
  27.0 0.0 collective-permute-done.11.refs_3_
  27.0 0.1 collective-permute-done.13.refs_4_
  27.1 0.0 copy-done
  27.1 1.0 %merge_and_value.1 = bf16[4,8,128]{2,1,0:T(8,128)(2,1)} custom-call(bf16[8,512,128]{2,1,0:T(8,128)(2,1)S(1)} %copy-done, f32[32,640]{1,0:T(8,128)S(1)} %get-tuple-element.19.refs_0_, bf16[144,128]{1,0:T(8,128)(2,1)S(1)} %collective-permute-done.7.refs_1_, bf16[144,128]{1,0:T(8,128)(2,1)S(1)} %collective-permute-done.9.refs_2_, ...), custom_call_target="tpu_custom_call" | custom-call | tf_op jit(solution)/shard_map/merge_and_value/pallas_call | solution.py:447
Async XLA Ops:
  2.1 7.8 %collective-permute-start.5 = (bf16[144,128]{1,0:T(8,128)(2,1)S(1)}, bf16[144,128]{1,0:T(8,128)(2,1)S(1)}, u32[]{:S(2)}, u32[]{:S(2)}) collective-permute-start(bf16[144,128]{1,0:T(8,128)(2,1)S(1)} %absorb.1.refs_0_), channel_id=1, source_target_pairs={{0,13},{1,12},{2,15},{3,14},{4,9},{5,8},{6,11},{7,10},{8,5},{9,4},... | collective-permute-start | bytes 110600 | tf_op jit(solution)/shard_map/ppermute | solution.py:353
  6.7 5.0 %collective-permute-start.3 = (bf16[144,128]{1,0:T(8,128)(2,1)S(1)}, bf16[144,128]{1,0:T(8,128)(2,1)S(1)}, u32[]{:S(2)}, u32[]{:S(2)}) collective-permute-start(bf16[144,128]{1,0:T(8,128)(2,1)S(1)} %absorb.1.refs_0_), channel_id=1, source_target_pairs={{0,9},{1,8},{2,11},{3,10},{4,13},{5,12},{6,15},{7,14},{8,1},{9,0},... | collective-permute-start | bytes 110600 | tf_op jit(solution)/shard_map/ppermute | solution.py:353
  6.7 6.1 %collective-permute-start.1 = (bf16[144,128]{1,0:T(8,128)(2,1)S(1)}, bf16[144,128]{1,0:T(8,128)(2,1)S(1)}, u32[]{:S(2)}, u32[]{:S(2)}) collective-permute-start(bf16[144,128]{1,0:T(8,128)(2,1)S(1)} %absorb.1.refs_0_), channel_id=1, source_target_pairs={{0,5},{1,4},{2,7},{3,6},{4,1},{5,0},{6,3},{7,2},{8,13},{9,12},{10,... | collective-permute-start | bytes 110600 | tf_op jit(solution)/shard_map/ppermute | solution.py:353
  7.6 7.8 %collective-permute-start.2 = (bf16[144,128]{1,0:T(8,128)(2,1)S(1)}, bf16[144,128]{1,0:T(8,128)(2,1)S(1)}, u32[]{:S(2)}, u32[]{:S(2)}) collective-permute-start(bf16[144,128]{1,0:T(8,128)(2,1)S(1)} %absorb.1.refs_0_), channel_id=1, source_target_pairs={{0,6},{1,7},{2,4},{3,5},{4,2},{5,3},{6,0},{7,1},{8,14},{9,15},{10,... | collective-permute-start | bytes 110600 | tf_op jit(solution)/shard_map/ppermute | solution.py:353
  10.0 5.5 %collective-permute-start = (bf16[144,128]{1,0:T(8,128)(2,1)S(1)}, bf16[144,128]{1,0:T(8,128)(2,1)S(1)}, u32[]{:S(2)}, u32[]{:S(2)}) collective-permute-start(bf16[144,128]{1,0:T(8,128)(2,1)S(1)} %absorb.1.refs_0_), channel_id=1, source_target_pairs={{0,3},{1,2},{2,1},{3,0},{4,7},{5,6},{6,5},{7,4},{8,11},{9,10},{10,... | collective-permute-start | bytes 110600 | tf_op jit(solution)/shard_map/ppermute | solution.py:353
  10.0 5.5 %collective-permute-start.6 = (bf16[144,128]{1,0:T(8,128)(2,1)S(1)}, bf16[144,128]{1,0:T(8,128)(2,1)S(1)}, u32[]{:S(2)}, u32[]{:S(2)}) collective-permute-start(bf16[144,128]{1,0:T(8,128)(2,1)S(1)} %collective-permute-done.5.refs_6_), channel_id=1, source_target_pairs={{0,3},{1,2},{2,1},{3,0},{4,7},{5,6},{6,5},{7,4},{8,11},{9,10},{10,... | collective-permute-start | bytes 110600 | tf_op jit(solution)/shard_map/ppermute | solution.py:353
  11.7 3.8 %collective-permute-start.4 = (bf16[144,128]{1,0:T(8,128)(2,1)S(1)}, bf16[144,128]{1,0:T(8,128)(2,1)S(1)}, u32[]{:S(2)}, u32[]{:S(2)}) collective-permute-start(bf16[144,128]{1,0:T(8,128)(2,1)S(1)} %collective-permute-done.3.refs_4_), channel_id=1, source_target_pairs={{0,3},{1,2},{2,1},{3,0},{4,7},{5,6},{6,5},{7,4},{8,11},{9,10},{10,... | collective-permute-start | bytes 110600 | tf_op jit(solution)/shard_map/ppermute | solution.py:353
  15.5 11.6 %copy-start = (bf16[8,512,128]{2,1,0:T(8,128)(2,1)S(1)}, bf16[8,512,128]{2,1,0:T(8,128)(2,1)}, u32[]{:S(2)}) copy-start(bf16[8,512,128]{2,1,0:T(8,128)(2,1)} %w_ref.1) | copy-start | bytes 3145732
  16.5 3.6 %collective-permute-start.8 = (bf16[144,128]{1,0:T(8,128)(2,1)S(1)}, bf16[144,128]{1,0:T(8,128)(2,1)S(1)}, u32[]{:S(2)}, u32[]{:S(2)}) collective-permute-start(bf16[144,128]{1,0:T(8,128)(2,1)S(1)} %get-tuple-element.21), channel_id=1, source_target_pairs={{0,3},{1,2},{2,1},{3,0},{4,7},{5,6},{6,5},{7,4},{8,11},{9,10},{10,... | collective-permute-start | bytes 110600 | tf_op jit(solution)/shard_map/ppermute | solution.py:353
  17.2 5.0 %collective-permute-start.10 = (bf16[144,128]{1,0:T(8,128)(2,1)S(1)}, bf16[144,128]{1,0:T(8,128)(2,1)S(1)}, u32[]{:S(2)}, u32[]{:S(2)}) collective-permute-start(bf16[144,128]{1,0:T(8,128)(2,1)S(1)} %get-tuple-element.23), channel_id=1, source_target_pairs={{0,3},{1,2},{2,1},{3,0},{4,7},{5,6},{6,5},{7,4},{8,11},{9,10},{10,... | collective-permute-start | bytes 110600 | tf_op jit(solution)/shard_map/ppermute | solution.py:353
  18.3 4.3 %collective-permute-start.12 = (bf16[144,128]{1,0:T(8,128)(2,1)S(1)}, bf16[144,128]{1,0:T(8,128)(2,1)S(1)}, u32[]{:S(2)}, u32[]{:S(2)}) collective-permute-start(bf16[144,128]{1,0:T(8,128)(2,1)S(1)} %get-tuple-element.25), channel_id=1, source_target_pairs={{0,3},{1,2},{2,1},{3,0},{4,7},{5,6},{6,5},{7,4},{8,11},{9,10},{10,... | collective-permute-start | bytes 110600 | tf_op jit(solution)/shard_map/ppermute | solution.py:353
  19.0 8.0 %collective-permute-start.7 = (bf16[144,128]{1,0:T(8,128)(2,1)S(1)}, bf16[144,128]{1,0:T(8,128)(2,1)S(1)}, u32[]{:S(2)}, u32[]{:S(2)}) collective-permute-start(bf16[144,128]{1,0:T(8,128)(2,1)S(1)} %get-tuple-element.20), channel_id=1, source_target_pairs={{0,3},{1,2},{2,1},{3,0},{4,7},{5,6},{6,5},{7,4},{8,11},{9,10},{10,... | collective-permute-start | bytes 110600 | tf_op jit(solution)/shard_map/ppermute | solution.py:353
  20.2 6.8 %collective-permute-start.9 = (bf16[144,128]{1,0:T(8,128)(2,1)S(1)}, bf16[144,128]{1,0:T(8,128)(2,1)S(1)}, u32[]{:S(2)}, u32[]{:S(2)}) collective-permute-start(bf16[144,128]{1,0:T(8,128)(2,1)S(1)} %merge_pair.3), channel_id=1, source_target_pairs={{0,13},{1,12},{2,15},{3,14},{4,9},{5,8},{6,11},{7,10},{8,5},{9,4},... | collective-permute-start | bytes 110600 | tf_op jit(solution)/shard_map/ppermute | solution.py:353
  22.4 4.6 %collective-permute-start.11 = (bf16[144,128]{1,0:T(8,128)(2,1)S(1)}, bf16[144,128]{1,0:T(8,128)(2,1)S(1)}, u32[]{:S(2)}, u32[]{:S(2)}) collective-permute-start(bf16[144,128]{1,0:T(8,128)(2,1)S(1)} %merge_pair.4.refs_10_), channel_id=1, source_target_pairs={{0,5},{1,4},{2,7},{3,6},{4,1},{5,0},{6,3},{7,2},{8,13},{9,12},{10,... | collective-permute-start | bytes 110600 | tf_op jit(solution)/shard_map/ppermute | solution.py:353
  22.8 4.3 %collective-permute-start.13 = (bf16[144,128]{1,0:T(8,128)(2,1)S(1)}, bf16[144,128]{1,0:T(8,128)(2,1)S(1)}, u32[]{:S(2)}, u32[]{:S(2)}) collective-permute-start(bf16[144,128]{1,0:T(8,128)(2,1)S(1)} %merge_pair.5), channel_id=1, source_target_pairs={{0,9},{1,8},{2,11},{3,10},{4,13},{5,12},{6,15},{7,14},{8,1},{9,0},... | collective-permute-start | bytes 110600 | tf_op jit(solution)/shard_map/ppermute | solution.py:353
  25.2 1.2 %collective-permute-start.14 = (f32[4,8,8]{2,1,0:T(8,128)S(1)}, f32[4,8,8]{2,1,0:T(8,128)S(1)}, u32[]{:S(2)}, u32[]{:S(2)}) collective-permute-start(f32[4,8,8]{2,1,0:T(8,128)S(1)} %page_bounds.1.mine_ref), channel_id=1, source_target_pairs={{0,1},{1,0},{2,3},{3,2},{4,5},{5,4},{6,7},{7,6},{8,9},{9,8},{10,11... | collective-permute-start | bytes 3080 | tf_op jit(solution)/shard_map/ppermute | solution.py:437
